TPU v7x, 32 devices: a whole 2x2x4 slice. The times are simulated.
32 devices in a mesh: dp: 4 (over z), tensor: 8 (over y, x, core).
Axes of the slice: x: 2, y: 2, z: 4, core: 2. Of those that a mesh axis runs over, the one named last changes fastest.
Arguments:
- tokens: bfloat16 [1024, 4096], P('dp', 'tensor'), may hold values from -0.25 to 0.25
- small_weights: bfloat16 [2, 3328, 8960], P(None, ('dp', 'tensor')), may hold values from -6 to 6
- ffn_growth: bfloat16 [11008, 8960], P('tensor'), may hold values from -0.0625 to 0.0625
- width_growth: bfloat16 [4096, 3328], P('dp'), may hold values from -0.109375 to 0.109375
Outputs:
- grown_weights: bfloat16 [2, 4096, 11008], P(None, 'dp', 'tensor')
- hidden: bfloat16 [1024, 11008], P('dp', 'tensor')
All inputs are finite; a program needn't handle non-finite values.
Results may differ from a plain program's by a relative error of at most 0.0071.
Values may be sent and summed in bfloat16 or wider, within the bound.
No kernel may reach another device: no remote copies, remote signals or barrier semaphores. Data moves between devices by JAX's collectives and lax.ppermute only.
A program may use at most 128 MiB of HBM per device.

v0:
```python
import functools

import jax
import jax.numpy as jnp
from jax import lax
from jax.experimental import pallas as pl
from jax.experimental.pallas import tpu as pltpu
from jax.sharding import PartitionSpec as P

BF16, F32 = jnp.bfloat16, jnp.float32
WIDTH = 512
VMEM_LIMIT = 56 * 1024 * 1024
ANY = pl.BlockSpec(memory_space=pl.ANY)


def pieces(extent, width):
    starts = list(range(0, extent, width))
    return [(start, min(width, extent - start)) for start in starts]


def after(array, *made):
    return lax.optimization_barrier((array,) + made)[0]


def token_rows(tokens, width_growth, *fetched):
    nd = lax.axis_size("dp")
    by_rows = lax.all_to_all(tokens, "tensor", 0, 1, tiled=True)
    by_features = lax.all_to_all(by_rows, "dp", 1, 0, tiled=True)
    by_features = after(by_features, *fetched[:1])
    part = jnp.dot(by_features, width_growth, preferred_element_type=F32).astype(BF16)
    parts = lax.all_to_all(part, "dp", 0, 0, tiled=True)
    return jnp.sum(parts.reshape(nd, -1, parts.shape[1]).astype(F32), axis=0).astype(BF16)


def swap(rows, bit):
    return lax.ppermute(rows, "tensor", [(j, j ^ bit) for j in range(lax.axis_size("tensor"))])


def joined(rows, got, bit):
    low = (lax.axis_index("tensor") // bit) % 2 == 0
    return jnp.concatenate([jnp.where(low, rows, got), jnp.where(low, got, rows)], axis=0)


def gathered_form(tokens, small_weights, ffn_growth, width_growth):
    columns = ffn_growth.shape[0]
    small = [lax.all_gather(small_weights[m], "tensor", axis=0, tiled=True) for m in range(2)]
    token_growth = lax.all_gather(token_rows(tokens, width_growth), "tensor", axis=0, tiled=True)
    grown, pre = [], []
    for m in range(2):
        grown_parts, pre_parts = [], []
        for start, width in pieces(columns, WIDTH):
            panel = jnp.einsum(
                "sf,cf->sc", small[m], ffn_growth[start:start + width], preferred_element_type=F32
            ).astype(BF16)
            panels = lax.all_gather(panel, "dp", axis=0, tiled=True)
            grown_parts.append(jnp.dot(width_growth, panels, preferred_element_type=F32).astype(BF16))
            pre_parts.append(jnp.dot(token_growth, panels, preferred_element_type=F32))
        grown.append(jnp.concatenate(grown_parts, axis=1))
        pre.append(jnp.concatenate(pre_parts, axis=1))
    hidden = (jax.nn.silu(pre[0]) * pre[1]).astype(BF16)
    return (jnp.stack(grown), hidden)


SWAP_INNER = [(1, 2), (2, 1)]
TO_INNER = [(0, 1), (3, 2)]
TO_OUTER = [(1, 0), (2, 3)]
SLOTS = [[0, 1, 2, 3], [1, 0, 2, 3], [2, 3, 1, 0], [3, 0, 1, 2]]


def panel_kernel(steps, splits, small_ref, growth_ref, *refs):
    out_refs, acc_ref = refs[:-1], refs[-1]
    step = pl.program_id(0)
    part = lax.dot_general(
        small_ref[...], growth_ref[...], (((1,), (1,)), ((), ())), preferred_element_type=F32
    )

    @pl.when(step == 0)
    def _():
        acc_ref[...] = part

    @pl.when((step > 0) & (step < steps - 1))
    def _():
        acc_ref[...] += part

    @pl.when(step == steps - 1)
    def _():
        total = acc_ref[...] + part
        for (start, width), out_ref in zip(splits, out_refs):
            wide = out_ref.shape[1]
            piece = total[:, start - splits[0][0]:start - splits[0][0] + wide]
            if width < wide:
                column = lax.broadcasted_iota(jnp.int32, piece.shape, 1)
                piece = jnp.where(column < width, piece, 0.0)
            out_ref[...] = piece.astype(BF16)


def tiled(width):
    return -(-width // 128) * 128


def panel_of(small, growth, splits):
    rows, depth = small.shape
    first = splits[0][0]
    wide = tiled(splits[-1][0] + splits[-1][1] - first)
    steps = 7
    deep = depth // steps
    return pl.pallas_call(
        functools.partial(panel_kernel, steps, splits),
        out_shape=[jax.ShapeDtypeStruct((rows, tiled(width)), BF16) for _, width in splits],
        grid=(steps,),
        in_specs=[
            pl.BlockSpec((rows, deep), lambda k: (0, k)),
            pl.BlockSpec((pl.Element(wide, (0, max(0, first + wide - growth.shape[0]))), pl.Element(deep)), lambda k: (first, k * deep)),
        ],
        out_specs=[pl.BlockSpec((rows, tiled(width)), lambda k: (0, 0)) for _, width in splits],
        scratch_shapes=[pltpu.VMEM((rows, wide), F32)],
        compiler_params=pltpu.CompilerParams(vmem_limit_bytes=VMEM_LIMIT),
        cost_estimate=pl.CostEstimate(flops=3 * rows * depth * wide, bytes_accessed=0, transcendentals=0),
        name="panel",
    )(small, growth)


def gated(gate, up):
    return (gate / (1.0 + jnp.exp(-gate)) * up).astype(BF16)


def products_kernel(m, start, width, sending, keeping, slots_ref, *refs):
    refs = list(refs)
    theirs, their_tokens = (refs.pop(0), refs.pop(0)), (refs.pop(0), refs.pop(0))
    rows_ref, tokens_ref = refs.pop(0), refs.pop(0)
    sources = [refs.pop(0) for _ in range(4)]
    if keeping:
        if m:
            gate_ref = refs.pop(0)
        if m or start:
            refs.pop(0)
        if start:
            refs.pop(0)
    if sending:
        out_ref = refs.pop(0)
    if keeping:
        grown_ref, last_ref = refs.pop(0), refs.pop(0)
    panels_ref, factors_ref, stage_ref, slab_ref, extra_ref, gate_buf, sems, factor_sems, end_sems = refs
    block = sources[0].shape[0]
    count = rows_ref.shape[0]
    extra = tokens_ref.shape[0]
    half, few = count // 2, extra // 2
    depth, used = panels_ref.shape[0], their_tokens[0].shape[1]

    def placed(s):
        row = pl.multiple_of(slots_ref[s] * block, 16)
        return pltpu.make_async_copy(sources[s], panels_ref.at[pl.ds(row, block), :], sems.at[s])

    def from_either(pair, i, buffer, offset, sem):
        size = pair[0].shape[0]
        copies = [
            pltpu.make_async_copy(ref, factors_ref.at[buffer, pl.ds(offset, size), pl.ds(0, used)], sem) for ref in pair
        ]
        mine = slots_ref[6] == i

        @pl.when(mine)
        def _():
            copies[0].start()

        @pl.when(jnp.logical_not(mine))
        def _():
            copies[1].start()

        return copies[0]

    def plain(ref, first, size, buffer, offset, sem):
        copy = pltpu.make_async_copy(
            ref.at[pl.ds(first, size), :], factors_ref.at[buffer, pl.ds(offset, size), :], sem
        )
        copy.start()
        return copy

    work = ["sent", "sent", "tokens", "kept", "kept"][0 if sending else 2:5 if keeping else 3]
    place = {"sent": 0, "kept": 0}

    def fetch(i):
        buffer = i % 3
        sem = [factor_sems.at[buffer, j] for j in range(3)]
        if work[i] == "sent":
            place["sent"] += 1
            return [from_either(theirs, place["sent"] - 1, buffer, 0, sem[0])]
        if work[i] == "kept":
            place["kept"] += 1
            return [plain(rows_ref, (place["kept"] - 1) * half, half, buffer, 0, sem[0])]
        copies = []
        if sending:
            copies.append(from_either(their_tokens, 0, buffer, 0, sem[0]))
            copies.append(from_either(their_tokens, 1, buffer, few, sem[1]))
        if keeping:
            copies.append(plain(tokens_ref, 0, extra, buffer, extra, sem[2]))
        return copies

    def product(buffer, first, size):
        return jnp.dot(factors_ref[buffer, first:first + size, :], panels_ref[...], preferred_element_type=F32)

    def product_out(buffer, size):
        row = pl.multiple_of(jnp.where(slots_ref[0] == 1, depth - used, 0), 128)
        return jnp.dot(
            factors_ref[buffer, :size, :used], panels_ref[pl.ds(row, used), :], preferred_element_type=F32
        )

    @pl.when(slots_ref[4] == 1)
    def _():
        first = [placed(s) for s in ((0, 2, 3) if sending else (0, 1, 2, 3))]
        for copy in first:
            copy.start()
        coming = [fetch(0), fetch(1)]
        if sending:
            outer_row = pl.multiple_of(slots_ref[1] * block, 16)
            panels_ref[pl.ds(outer_row, block), :] = jnp.zeros((block, panels_ref.shape[1]), BF16)
        if m and keeping:
            gate_copy = pltpu.make_async_copy(
                gate_ref.at[:, pl.ds(start, tiled(width))], gate_buf, end_sems.at[4])
            gate_copy.start()
        for copy in first:
            copy.wait()
        ends = []

        def finished(source, target):
            copy = pltpu.make_async_copy(source, target, end_sems.at[len(ends)])
            copy.start()
            ends.append(copy)

        done = {"sent": 0, "kept": 0}
        for i, kind in enumerate(work):
            if i + 2 < len(work):
                coming.append(fetch(i + 2))
            for copy in coming[i]:
                copy.wait()
            if kind == "sent":
                stage_ref[done[kind] * half:(done[kind] + 1) * half, :] = product_out(i % 3, half).astype(BF16)
                done[kind] += 1
            elif kind == "kept":
                part = slice(done[kind] * half, (done[kind] + 1) * half)
                slab_ref[:, part] = product(i % 3, 0, half).astype(BF16).T
                done[kind] += 1
            else:
                if sending:
                    stage_ref[count:, :] = product_out(i % 3, extra).astype(BF16)
                    finished(stage_ref, out_ref)
                if sending and keeping:
                    outer = placed(1)
                    outer.start()
                    outer.wait()
                if keeping:
                    pre = product(i % 3, extra, extra)
                    if m:
                        gate_copy.wait()
                        extra_ref[...] = gated(gate_buf[...], pre).T
                        finished(extra_ref.at[:width, :], last_ref.at[pl.ds(start, width), :])
                    else:
                        extra_ref[...] = pre
                        finished(extra_ref, last_ref.at[:, pl.ds(start, tiled(width))])
        if keeping:
            finished(slab_ref.at[:width, :], grown_ref.at[m, pl.ds(start, width), :])
        for copy in ends:
            copy.wait()


def products(m, start, width, slots, mine, theirs, panels, gate, grown, last, columns, sending, keeping):
    rows, token_growth = mine
    count, depth = rows.shape
    extra = token_growth.shape[0]
    block, wide = panels[0].shape
    args = [*theirs, rows, token_growth, *panels]
    aliases = {}
    if keeping and m:
        args.append(gate)
    if keeping and grown is not None:
        aliases[len(args) + 1] = int(sending)
        args.append(grown)
    if keeping and last is not None:
        aliases[len(args) + 1] = int(sending) + 1
        args.append(last)
    out_shape = []
    if sending:
        out_shape.append(jax.ShapeDtypeStruct((count + extra, wide), BF16))
    if keeping:
        out_shape.append(jax.ShapeDtypeStruct((2, columns, count), BF16))
        out_shape.append(
            jax.ShapeDtypeStruct((columns, extra), BF16) if m else jax.ShapeDtypeStruct((extra, tiled(columns)), F32)
        )
    return pl.pallas_call(
        functools.partial(products_kernel, m, start, width, sending, keeping),
        out_shape=out_shape,
        grid_spec=pltpu.PrefetchScalarGridSpec(
            num_scalar_prefetch=1,
            grid=(1,),
            in_specs=[ANY] * len(args),
            out_specs=[ANY] * len(out_shape),
            scratch_shapes=[
                pltpu.VMEM((depth, wide), BF16),
                pltpu.VMEM((3, count // 2, depth), BF16),
                pltpu.VMEM((count + extra, wide), BF16),
                pltpu.VMEM((wide, count), BF16),
                pltpu.VMEM((wide, extra), BF16) if m else pltpu.VMEM((extra, wide), F32),
                pltpu.VMEM((extra, wide), F32),
                pltpu.SemaphoreType.DMA((4,)),
                pltpu.SemaphoreType.DMA((3, 3)),
                pltpu.SemaphoreType.DMA((5,)),
            ],
        ),
        input_output_aliases=aliases,
        compiler_params=pltpu.CompilerParams(vmem_limit_bytes=VMEM_LIMIT),
        cost_estimate=pl.CostEstimate(flops=3 * (sending + keeping) * (count + extra) * depth * wide, bytes_accessed=0, transcendentals=0),
        name="products",
    )(slots, *args)


def finish_kernel(m, start, width, slots_ref, rows_ref, tokens_ref, own_ref, got_ref, gate_ref, *refs):
    grown_ref, last_ref = refs[2 if m else 1:][:2]
    factors_ref, panels_ref, got_buf, gate_buf, slab_ref, extra_ref, sems = refs[2 if m else 1:][2:]
    block = own_ref.shape[0]
    count = rows_ref.shape[0]
    wide = panels_ref.shape[1]
    half = count // 2
    depth = factors_ref.shape[1]

    @pl.when(slots_ref[4] == 0)
    def _():
        side = pl.multiple_of(slots_ref[5] * depth, 128)
        place = pl.multiple_of(slots_ref[5] * block, 16)
        other = pl.multiple_of((1 - slots_ref[5]) * block, 16)
        copies = [
            pltpu.make_async_copy(own_ref, panels_ref.at[pl.ds(place, block), :], sems.at[0]),
            pltpu.make_async_copy(
                tokens_ref.at[:, pl.ds(side, depth)], factors_ref.at[pl.ds(count, tokens_ref.shape[0]), :], sems.at[1]),
            pltpu.make_async_copy(rows_ref.at[:, pl.ds(side, depth)], factors_ref.at[pl.ds(0, count), :], sems.at[2]),
            pltpu.make_async_copy(got_ref, got_buf, sems.at[3]),
        ]
        if m:
            copies.append(pltpu.make_async_copy(gate_ref.at[:, pl.ds(start, tiled(width))], gate_buf, sems.at[4]))
        for copy in copies:
            copy.start()
        panels_ref[pl.ds(other, block), :] = jnp.zeros((block, wide), BF16)
        for copy in copies:
            copy.wait()

        def product(first, size):
            sums = jnp.dot(factors_ref[first:first + size, :], panels_ref[...], preferred_element_type=F32)
            return sums + got_buf[first:first + size, :].astype(F32)

        pre = product(count, tokens_ref.shape[0])
        if m:
            extra_ref[...] = gated(gate_buf[...], pre).T
            end = pltpu.make_async_copy(
                extra_ref.at[:width, :], last_ref.at[pl.ds(start, width), :], sems.at[0])
        else:
            extra_ref[...] = pre
            end = pltpu.make_async_copy(extra_ref, last_ref.at[:, pl.ds(start, tiled(width))], sems.at[0])
        end.start()
        for i in range(2):
            slab_ref[:, i * half:(i + 1) * half] = product(i * half, half).astype(BF16).T
        slab = pltpu.make_async_copy(
            slab_ref.at[:width, :], grown_ref.at[m, pl.ds(start, width), :], sems.at[1])
        slab.start()
        end.wait()
        slab.wait()


def finish(m, start, width, slots, mine, own, got, gate, grown, hidden, columns):
    rows, token_growth = mine
    count, depth = rows.shape
    extra = token_growth.shape[0]
    block, wide = own.shape
    args = [rows, token_growth, own, got, gate, grown] + ([hidden] if m else [])
    return pl.pallas_call(
        functools.partial(finish_kernel, m, start, width),
        out_shape=(
            jax.ShapeDtypeStruct((2, columns, count), BF16),
            jax.ShapeDtypeStruct((columns, extra), BF16) if m else jax.ShapeDtypeStruct((extra, tiled(columns)), F32),
        ),
        grid_spec=pltpu.PrefetchScalarGridSpec(
            num_scalar_prefetch=1,
            grid=(1,),
            in_specs=[ANY] * len(args),
            out_specs=(ANY, ANY),
            scratch_shapes=[
                pltpu.VMEM((count + extra, 2 * block), BF16),
                pltpu.VMEM((2 * block, wide), BF16),
                pltpu.VMEM((count + extra, wide), BF16),
                pltpu.VMEM((extra, wide), F32),
                pltpu.VMEM((wide, count), BF16),
                pltpu.VMEM((wide, extra), BF16) if m else pltpu.VMEM((extra, wide), F32),
                pltpu.SemaphoreType.DMA((5,)),
            ],
        ),
        input_output_aliases={6: 0, 7: 1} if m else {6: 0, 5: 1},
        compiler_params=pltpu.CompilerParams(vmem_limit_bytes=VMEM_LIMIT),
        cost_estimate=pl.CostEstimate(flops=0, bytes_accessed=0, transcendentals=0),
        name="finish",
    )(slots, *args)


def used_depth(depth):
    return tiled(3 * depth // 4)


def fetch_half(rows, parts):
    half, depth = rows.shape[0] // 2, rows.shape[1]
    core = lax.rem(lax.axis_index("tensor"), 2)
    first = jnp.where(lax.axis_index("dp") == 0, depth - used_depth(depth), 0)
    size = -(-half // parts // 16) * 16
    fetched = []
    for start in range(0, half, size):
        part = lax.dynamic_slice(rows, (core * half + start, first), (min(size, half - start), used_depth(depth)))
        fetched.append(lax.ppermute(after(part, *fetched[-1:]), "dp", TO_INNER))
    return fetched


def line_form(tokens, small_weights, ffn_growth, width_growth):
    columns = ffn_growth.shape[0]
    index = lax.axis_index("dp")
    is_inner = ((index == 1) | (index == 2)).astype(jnp.int32)
    core = lax.rem(lax.axis_index("tensor"), 2)
    slots = jnp.concatenate(
        [jnp.array(SLOTS, jnp.int32)[index], jnp.stack([is_inner, (index == 3).astype(jnp.int32), core])]
    )
    small = [lax.all_gather(small_weights[m], "tensor", axis=0, tiled=True) for m in range(2)]
    fetched = fetch_half(width_growth, 3)
    token_share = token_rows(tokens, width_growth, fetched[0])
    token_share = joined(token_share, swap(token_share, 1), 1)
    token_share = joined(token_share, swap(token_share, 2), 2)
    token_rest = swap(token_share, 4)

    work = [(0, start, width) for start, width in pieces(columns, 768)]
    work += [(1, start, width) for start, width in pieces(columns, WIDTH)]
    own, outer, mate, far, out, received = ({} for _ in range(6))
    grown = gate = hidden = theirs = None

    def panel(chosen, *made):
        m = work[chosen[0]][0]
        source = after(small[m], *made) if made else small[m]
        for k, part in zip(chosen, panel_of(source, ffn_growth, [work[k][1:] for k in chosen])):
            own[k] = part

    def send(k, *made):
        sent = after(own[k], *made) if made else own[k]
        with jax.named_scope(f"outer{k}"):
            outer[k] = lax.ppermute(sent, "dp", TO_INNER)
        with jax.named_scope(f"mate{k}"):
            mate[k] = lax.ppermute(sent, "dp", SWAP_INNER)

    def forward(k, *made):
        outer[k] = after(outer[k], *made)
        with jax.named_scope(f"far{k}"):
            far[k] = lax.ppermute(outer[k], "dp", SWAP_INNER)

    def multiply(k, *made, sending=True, keeping=True):
        nonlocal grown, gate, hidden
        m, start, width = work[k]
        panels = [after(own[k], *made), outer[k], mate[k], far[k]]
        last = hidden if m else gate
        made = products(
            m, start, width, slots, mine, theirs, panels, gate, grown, last, columns, sending, keeping
        )
        if sending:
            out[k] = made[0]
            with jax.named_scope(f"sums{k}"):
                received[k] = lax.ppermute(out[k], "dp", TO_OUTER)
        if keeping:
            grown = made[-2]
            if m:
                hidden = made[-1]
            else:
                gate = made[-1]

    def conclude(k, *made):
        nonlocal grown, gate, hidden
        m, start, width = work[k]
        got = after(received[k], *made) if made else received[k]
        grown, last = finish(m, start, width, slots, mine, own[k], got, gate, grown, hidden, columns)
        if m:
            hidden = last
        else:
            gate = last

    panel([0], fetched[1], token_share)
    token_growth = joined(token_share, after(token_rest, own[0]), 4)
    token_half, = fetch_half(token_growth, 1)
    mine = (width_growth, token_growth)
    rows_half = jnp.concatenate(fetched[:2] + [after(fetched[2], own[0])], axis=0)
    send(0)
    panel([1], own[0], token_growth, rows_half)
    forward(0, mate[0], own[1])
    token_half = after(token_half, own[1])
    theirs = (rows_half, swap(rows_half, 1), token_half, swap(token_half, 1))
    send(1, outer[0])
    multiply(0, far[0])
    forward(1, out[0])
    panel([2], outer[1], out[0], mate[1])
    send(2)
    panel([3, 4], own[2], received[0])
    forward(2, own[3], mate[1])
    send(3, outer[2])
    conclude(0)
    multiply(1, outer[2])
    multiply(2, out[1], mate[3])
    forward(3, out[2])
    send(4, outer[3])
    conclude(1)
    multiply(3, outer[3])
    forward(4, out[3])
    conclude(2)
    multiply(4, out[3], received[2], keeping=False)
    multiply(4, out[4], sending=False)
    conclude(3)
    conclude(4)
    return jnp.swapaxes(grown, 1, 2), hidden.T


def solution(mesh):
    placed = (P("dp", "tensor"), P(None, ("dp", "tensor"), None), P("tensor", None), P("dp", None))
    return jax.shard_map(
        line_form if mesh.shape["dp"] == 4 else gathered_form,
        mesh=mesh,
        in_specs=placed,
        out_specs=(P(None, "dp", "tensor"), P("dp", "tensor")),
        check_vma=False,
    )
```

profile of v0, /device:TPU:0, one launch (start us, length us, event | category | flops | bytes accessed | tf_op | source)
XLA Modules:
  0.0 437.3 jit_solution(3817398281306656533)
XLA Ops:
  7.2 4.2 fusion.2
  13.8 5.0 %collective-permute-start = (bf16[176,2560]{1,0:T(8,128)(2,1)S(1)}, bf16[176,2560]{1,0:T(8,128)(2,1)S(1)}, u32[]{:S(2)}, u32[]{:S(2)}) collective-permute-start(bf16[176,2560]{1,0:T(8,128)(2,1)S(1)} %get-tuple-element.103), channel_id=1, source_target_pairs={{0,8},{24,16},{1,9},{25,17},{2,10},{26,18},{3,11},{27,19},{4,12},{... | collective-permute-start | bytes 2703368 | tf_op jit(solution)/shard_map/ppermute | solution.py:412
  18.8 13.3 %all_to_all.44 = bf16[8,32,512]{2,1,0:T(8,128)(2,1)S(1)} all-to-all(bf16[8,32,512]{2,1,0:T(8,128)(2,1)S(1)} %bitcast.22), channel_id=1, replica_groups=mesh['dp'=4,'tensor'=8] {'tensor'}, dimensions={0} | all-to-all | bytes 524288 | tf_op jit(solution)/shard_map/all_to_all | solution.py:27
  32.5 11.9 %all_to_all.45 = bf16[32,4,1024]{2,0,1:T(8,128)(2,1)S(1)} all-to-all(bf16[32,4,1024]{2,0,1:T(8,128)(2,1)S(1)} %copy.27), channel_id=1, replica_groups=mesh['dp'=4,'tensor'=8] {'dp'}, dimensions={1} | all-to-all | bytes 524288 | tf_op jit(solution)/shard_map/all_to_all | solution.py:28
  44.4 4.3 convolution_convert_fusion
  48.8 23.1 %all_to_all.46 = bf16[4,32,3328]{2,1,0:T(8,128)(2,1)S(1)} all-to-all(bf16[4,32,3328]{2,1,0:T(8,128)(2,1)S(1)} %bitcast.19), channel_id=1, replica_groups=mesh['dp'=4,'tensor'=8] {'dp'}, dimensions={0} | all-to-all | bytes 1703936 | tf_op jit(solution)/shard_map/all_to_all | solution.py:31
  72.1 2.1 dynamic_slice.18
  74.2 2.4 collective-permute-start.4
  79.5 16.9 %collective-permute-done.4 = bf16[176,2560]{1,0:T(8,128)(2,1)S(1)} collective-permute-done((bf16[176,2560]{1,0:T(8,128)(2,1)S(1)}, bf16[176,2560]{1,0:T(8,128)(2,1)S(1)}, u32[]{:S(2)}, u32[]{:S(2)}) %collective-permute-start.4) | collective-permute-done | bytes 901152 | tf_op jit(solution)/shard_map/ppermute | solution.py:412
  96.4 5.3 %collective-permute-start.5 = (bf16[160,2560]{1,0:T(8,128)(2,1)}, bf16[160,2560]{1,0:T(8,128)(2,1)}, u32[]{:S(2)}, u32[]{:S(2)}) collective-permute-start(bf16[160,2560]{1,0:T(8,128)(2,1)} %dynamic_slice.18), channel_id=1, source_target_pairs={{0,8},{24,16},{1,9},{25,17},{2,10},{26,18},{3,11},{27,19},{4,12},{... | collective-permute-start | bytes 2457608 | tf_op jit(solution)/shard_map/ppermute | solution.py:412
  106.0 18.8 %panel.4.refs_6_.own_ref = bf16[832,768]{1,0:T(8,128)(2,1)} custom-call(bf16[832,8960]{1,0:T(8,128)(2,1)} %bitcast.25, bf16[1376,8960]{1,0:T(8,128)(2,1)} %growth_ref.7), custom_call_target="tpu_custom_call" | custom-call | flops 17175674880 | tf_op jit(solution)/shard_map/panel/pallas_call | solution.py:107
  124.8 4.5 %collective-permute-start.6 = (bf16[832,768]{1,0:T(8,128)(2,1)}, bf16[832,768]{1,0:T(8,128)(2,1)}, u32[]{:S(2)}, u32[]{:S(2)}) collective-permute-start(bf16[832,768]{1,0:T(8,128)(2,1)} %panel.4.refs_6_.own_ref), channel_id=1, source_target_pairs={{0,8},{24,16},{1,9},{25,17},{2,10},{26,18},{3,11},{27,19},{4,12},{... | collective-permute-start | bytes 3833864 | tf_op jit(solution)/shard_map/outer0/ppermute | solution.py:445
  135.1 2.9 collective-permute-start.10
  138.0 18.6 %panel.5.refs_6_.own_ref = bf16[832,640]{1,0:T(8,128)(2,1)} custom-call(bf16[832,8960]{1,0:T(8,128)(2,1)} %bitcast.26, bf16[1376,8960]{1,0:T(8,128)(2,1)} %growth_ref.7), custom_call_target="tpu_custom_call" | custom-call | flops 14313062400 | tf_op jit(solution)/shard_map/panel/pallas_call | solution.py:107
  158.7 11.5 %collective-permute-done.10.refs_2_ = bf16[128,2560]{1,0:T(8,128)(2,1)S(1)} collective-permute-done((bf16[128,2560]{1,0:T(8,128)(2,1)S(1)}, bf16[128,2560]{1,0:T(8,128)(2,1)S(1)}, u32[]{:S(2)}, u32[]{:S(2)}) %collective-permute-start.10) | collective-permute-done | bytes 655392 | tf_op jit(solution)/shard_map/ppermute | solution.py:412
  171.5 5.5 %collective-permute-start.8 = (bf16[832,640]{1,0:T(8,128)(2,1)}, bf16[832,640]{1,0:T(8,128)(2,1)}, u32[]{:S(2)}, u32[]{:S(2)}) collective-permute-start(bf16[832,640]{1,0:T(8,128)(2,1)} %panel.5.refs_6_.own_ref), channel_id=1, source_target_pairs={{0,8},{24,16},{1,9},{25,17},{2,10},{26,18},{3,11},{27,19},{4,12},{... | collective-permute-start | bytes 3194888 | tf_op jit(solution)/shard_map/outer1/ppermute | solution.py:445
  181.0 18.7 %collective-permute-done.8.refs_7_ = bf16[832,640]{1,0:T(8,128)(2,1)} collective-permute-done((bf16[832,640]{1,0:T(8,128)(2,1)}, bf16[832,640]{1,0:T(8,128)(2,1)}, u32[]{:S(2)}, u32[]{:S(2)}) %collective-permute-start.8) | collective-permute-done | bytes 1064992 | tf_op jit(solution)/shard_map/outer1/ppermute | solution.py:445
  200.4 14.6 %panel.6.refs_6_.own_ref = bf16[832,512]{1,0:T(8,128)(2,1)} custom-call(bf16[832,8960]{1,0:T(8,128)(2,1)} %bitcast.23, bf16[1376,8960]{1,0:T(8,128)(2,1)} %growth_ref.7), custom_call_target="tpu_custom_call" | custom-call | flops 11450449920 | tf_op jit(solution)/shard_map/panel/pallas_call | solution.py:107
  215.0 22.7 %collective-permute-start.15 = (bf16[832,512]{1,0:T(8,128)(2,1)}, bf16[832,512]{1,0:T(8,128)(2,1)S(1)}, u32[]{:S(2)}, u32[]{:S(2)}) collective-permute-start(bf16[832,512]{1,0:T(8,128)(2,1)} %panel.6.refs_6_.own_ref), channel_id=1, source_target_pairs={{0,8},{24,16},{1,9},{25,17},{2,10},{26,18},{3,11},{27,19},{4,12},{... | collective-permute-start | bytes 2555912 | tf_op jit(solution)/shard_map/outer2/ppermute | solution.py:445
  238.6 19.5 %collective-permute-done.14.got_ref = bf16[1280,768]{1,0:T(8,128)(2,1)S(1)} collective-permute-done((bf16[1280,768]{1,0:T(8,128)(2,1)}, bf16[1280,768]{1,0:T(8,128)(2,1)S(1)}, u32[]{:S(2)}, u32[]{:S(2)}) %collective-permute-start.14) | collective-permute-done | bytes 1966112 | tf_op jit(solution)/shard_map/sums0/ppermute | solution.py:465
  258.1 22.9 %panel.7 = (bf16[832,512]{1,0:T(8,128)(2,1)}, bf16[832,384]{1,0:T(8,128)(2,1)}) custom-call(bf16[832,8960]{1,0:T(8,128)(2,1)} %bitcast.24, bf16[1376,8960]{1,0:T(8,128)(2,1)} %growth_ref.7), custom_call_target="tpu_custom_call" | custom-call | flops 20038287360 | tf_op jit(solution)/shard_map/panel/pallas_call | solution.py:107
  283.5 5.1 %collective-permute-start.16 = (bf16[832,512]{1,0:T(8,128)(2,1)}, bf16[832,512]{1,0:T(8,128)(2,1)S(1)}, u32[]{:S(2)}, u32[]{:S(2)}) collective-permute-start(bf16[832,512]{1,0:T(8,128)(2,1)} %get-tuple-element.82.refs_6_.own_ref), channel_id=1, source_target_pairs={{0,8},{24,16},{1,9},{25,17},{2,10},{26,18},{3,11},{27,19},{4,12},{... | collective-permute-start | bytes 2555912 | tf_op jit(solution)/shard_map/outer3/ppermute | solution.py:445
  288.6 8.9 %finish.5 = (bf16[2,1376,1024]{2,1,0:T(8,128)(2,1)}, f32[256,1408]{1,0:T(8,128)}) custom-call(s32[7]{0:T(128)} %pad_add_fusion.slots_ref, bf16[1024,3328]{1,0:T(8,128)(2,1)} %rows_ref.9, bf16[256,3328]{1,0:T(8,128)(2,1)} %pad_maximum_fusion.refs_5_.tokens_ref, bf16[832,768]{1,0:T(8,128)(2,1)} %panel.4.refs_6_.own_ref, ...), custom_call_target="tpu_custom_call", output_to_operand_aliasing={{0}: (6, {}), {1}: (5, {})} | custom-call | tf_op jit(solution)/shard_map/finish/pallas_call | solution.py:372
  305.4 36.4 %collective-permute-start.24 = (bf16[832,384]{1,0:T(8,128)(2,1)S(1)}, bf16[832,384]{1,0:T(8,128)(2,1)S(1)}, u32[]{:S(2)}, u32[]{:S(2)}) collective-permute-start(bf16[832,384]{1,0:T(8,128)(2,1)S(1)} %copy-done.1), channel_id=1, source_target_pairs={{0,8},{24,16},{1,9},{25,17},{2,10},{26,18},{3,11},{27,19},{4,12},{... | collective-permute-start | bytes 1916936 | tf_op jit(solution)/shard_map/outer4/ppermute | solution.py:445
  342.5 7.1 %collective-permute-done.22.got_ref = bf16[1280,640]{1,0:T(8,128)(2,1)S(1)} collective-permute-done((bf16[1280,640]{1,0:T(8,128)(2,1)}, bf16[1280,640]{1,0:T(8,128)(2,1)S(1)}, u32[]{:S(2)}, u32[]{:S(2)}) %collective-permute-start.22) | collective-permute-done | bytes 1638432 | tf_op jit(solution)/shard_map/sums1/ppermute | solution.py:465
  350.8 8.5 %finish.6 = (bf16[2,1376,1024]{2,1,0:T(8,128)(2,1)}, f32[256,1408]{1,0:T(8,128)}) custom-call(s32[7]{0:T(128)} %pad_add_fusion.slots_ref, bf16[1024,3328]{1,0:T(8,128)(2,1)} %rows_ref.9, bf16[256,3328]{1,0:T(8,128)(2,1)} %pad_maximum_fusion.refs_5_.tokens_ref, bf16[832,640]{1,0:T(8,128)(2,1)} %panel.5.refs_6_.own_ref, ...), custom_call_target="tpu_custom_call", output_to_operand_aliasing={{0}: (6, {}), {1}: (5, {})} | custom-call | tf_op jit(solution)/shard_map/finish/pallas_call | solution.py:372
  363.4 12.8 %collective-permute-done.23.got_ref = bf16[1280,512]{1,0:T(8,128)(2,1)S(1)} collective-permute-done((bf16[1280,512]{1,0:T(8,128)(2,1)}, bf16[1280,512]{1,0:T(8,128)(2,1)S(1)}, u32[]{:S(2)}, u32[]{:S(2)}) %collective-permute-start.23) | collective-permute-done | bytes 1310752 | tf_op jit(solution)/shard_map/sums2/ppermute | solution.py:465
  380.0 7.3 %finish.7 = (bf16[2,1376,1024]{2,1,0:T(8,128)(2,1)}, bf16[1376,256]{1,0:T(8,128)(2,1)}) custom-call(s32[7]{0:T(128)} %pad_add_fusion.slots_ref, bf16[1024,3328]{1,0:T(8,128)(2,1)} %rows_ref.9, bf16[256,3328]{1,0:T(8,128)(2,1)} %pad_maximum_fusion.refs_5_.tokens_ref, ...), custom_call_target="tpu_custom_call", output_to_operand_aliasing={{0}: (6, {}), {1}: (7, {})} | custom-call | tf_op jit(solution)/shard_map/finish/pallas_call | solution.py:372
  388.4 21.3 %collective-permute-done.28.got_ref = bf16[1280,512]{1,0:T(8,128)(2,1)S(1)} collective-permute-done((bf16[1280,512]{1,0:T(8,128)(2,1)}, bf16[1280,512]{1,0:T(8,128)(2,1)S(1)}, u32[]{:S(2)}, u32[]{:S(2)}) %collective-permute-start.28) | collective-permute-done | bytes 1310752 | tf_op jit(solution)/shard_map/sums3/ppermute | solution.py:465
  410.8 7.3 %finish.8 = (bf16[2,1376,1024]{2,1,0:T(8,128)(2,1)}, bf16[1376,256]{1,0:T(8,128)(2,1)}) custom-call(s32[7]{0:T(128)} %pad_add_fusion.slots_ref, bf16[1024,3328]{1,0:T(8,128)(2,1)} %rows_ref.9, bf16[256,3328]{1,0:T(8,128)(2,1)} %pad_maximum_fusion.refs_5_.tokens_ref, ...), custom_call_target="tpu_custom_call", output_to_operand_aliasing={{0}: (6, {}), {1}: (7, {})} | custom-call | tf_op jit(solution)/shard_map/finish/pallas_call | solution.py:372
  418.1 4.2 collective-permute-done.27.got_ref
  423.3 6.9 %finish.9 = (bf16[2,1376,1024]{2,1,0:T(8,128)(2,1)}, bf16[1376,256]{1,0:T(8,128)(2,1)}) custom-call(s32[7]{0:T(128)} %pad_add_fusion.slots_ref, bf16[1024,3328]{1,0:T(8,128)(2,1)} %rows_ref.9, bf16[256,3328]{1,0:T(8,128)(2,1)} %pad_maximum_fusion.refs_5_.tokens_ref, ...), custom_call_target="tpu_custom_call", output_to_operand_aliasing={{0}: (6, {}), {1}: (7, {})} | custom-call | tf_op jit(solution)/shard_map/finish/pallas_call | solution.py:372
  (110 shorter events, 48.0 us)
Async XLA Ops:
  7.2 98.8 %all-gather.5.cloned.1.call-start = ((), (), s32[]{:S(2)}) async-start(), calls=%async_computation.3 | async-start | bytes 16773120 | tf_op jit(solution)/shard_map/all_gather | solution.py:424
  11.4 189.0 %all-gather.7.cloned.1.call-start = ((), (), s32[]{:S(2)}) async-start(), calls=%async_computation.4 | async-start | bytes 16773120 | tf_op jit(solution)/shard_map/all_gather | solution.py:424
  13.8 30.6 %collective-permute-start = (bf16[176,2560]{1,0:T(8,128)(2,1)S(1)}, bf16[176,2560]{1,0:T(8,128)(2,1)S(1)}, u32[]{:S(2)}, u32[]{:S(2)}) collective-permute-start(bf16[176,2560]{1,0:T(8,128)(2,1)S(1)} %get-tuple-element.103), channel_id=1, source_target_pairs={{0,8},{24,16},{1,9},{25,17},{2,10},{26,18},{3,11},{27,19},{4,12},{... | collective-permute-start | bytes 2703368 | tf_op jit(solution)/shard_map/ppermute | solution.py:412
  72.0 4.6 %collective-permute-start.1 = (bf16[32,3328]{1,0:T(8,128)(2,1)S(1)}, bf16[32,3328]{1,0:T(8,128)(2,1)S(1)}, u32[]{:S(2)}, u32[]{:S(2)}) collective-permute-start(bf16[32,3328]{1,0:T(8,128)(2,1)S(1)} %reduce_sum.12), channel_id=1, source_target_pairs={{0,1},{1,0},{2,3},{3,2},{4,5},{5,4},{6,7},{7,6},{8,9},{9,8},{10,11... | collective-permute-start | bytes 638984 | tf_op jit(solution)/shard_map/ppermute | solution.py:36
  74.2 22.1 %collective-permute-start.4 = (bf16[176,2560]{1,0:T(8,128)(2,1)S(1)}, bf16[176,2560]{1,0:T(8,128)(2,1)S(1)}, u32[]{:S(2)}, u32[]{:S(2)}) collective-permute-start(bf16[176,2560]{1,0:T(8,128)(2,1)S(1)} %get-tuple-element.53), channel_id=1, source_target_pairs={{0,8},{24,16},{1,9},{25,17},{2,10},{26,18},{3,11},{27,19},{4,12},{... | collective-permute-start | bytes 2703368 | tf_op jit(solution)/shard_map/ppermute | solution.py:412
  76.7 25.0 %collective-permute-start.2 = (bf16[64,3328]{1,0:T(8,128)(2,1)S(1)}, bf16[64,3328]{1,0:T(8,128)(2,1)S(1)}, u32[]{:S(2)}, u32[]{:S(2)}) collective-permute-start(bf16[64,3328]{1,0:T(8,128)(2,1)S(1)} %pad_maximum_fusion.2), channel_id=1, source_target_pairs={{0,2},{1,3},{2,0},{3,1},{4,6},{5,7},{6,4},{7,5},{8,10},{9,11},{10,... | collective-permute-start | bytes 1277960 | tf_op jit(solution)/shard_map/ppermute | solution.py:36
  96.4 33.7 %collective-permute-start.5 = (bf16[160,2560]{1,0:T(8,128)(2,1)}, bf16[160,2560]{1,0:T(8,128)(2,1)}, u32[]{:S(2)}, u32[]{:S(2)}) collective-permute-start(bf16[160,2560]{1,0:T(8,128)(2,1)} %dynamic_slice.18), channel_id=1, source_target_pairs={{0,8},{24,16},{1,9},{25,17},{2,10},{26,18},{3,11},{27,19},{4,12},{... | collective-permute-start | bytes 2457608 | tf_op jit(solution)/shard_map/ppermute | solution.py:412
  102.8 27.2 %collective-permute-start.3 = (bf16[128,3328]{1,0:T(8,128)(2,1)}, bf16[128,3328]{1,0:T(8,128)(2,1)}, u32[]{:S(2)}, u32[]{:S(2)}) collective-permute-start(bf16[128,3328]{1,0:T(8,128)(2,1)} %pad_maximum_fusion.1), channel_id=1, source_target_pairs={{0,4},{1,5},{2,6},{3,7},{4,0},{5,1},{6,2},{7,3},{8,12},{9,13},{10,... | collective-permute-start | bytes 2555912 | tf_op jit(solution)/shard_map/ppermute | solution.py:36
  124.8 32.1 %collective-permute-start.6 = (bf16[832,768]{1,0:T(8,128)(2,1)}, bf16[832,768]{1,0:T(8,128)(2,1)}, u32[]{:S(2)}, u32[]{:S(2)}) collective-permute-start(bf16[832,768]{1,0:T(8,128)(2,1)} %panel.4.refs_6_.own_ref), channel_id=1, source_target_pairs={{0,8},{24,16},{1,9},{25,17},{2,10},{26,18},{3,11},{27,19},{4,12},{... | collective-permute-start | bytes 3833864 | tf_op jit(solution)/shard_map/outer0/ppermute | solution.py:445
  129.3 27.6 %collective-permute-start.7 = (bf16[832,768]{1,0:T(8,128)(2,1)}, bf16[832,768]{1,0:T(8,128)(2,1)S(1)}, u32[]{:S(2)}, u32[]{:S(2)}) collective-permute-start(bf16[832,768]{1,0:T(8,128)(2,1)} %panel.4.refs_6_.own_ref), channel_id=1, source_target_pairs={{8,16},{16,8},{9,17},{17,9},{10,18},{18,10},{11,19},{19,11},{12,20... | collective-permute-start | bytes 3833864 | tf_op jit(solution)/shard_map/mate0/ppermute | solution.py:447
  131.3 47.4 %collective-permute-start.9 = (bf16[512,2560]{1,0:T(8,128)(2,1)S(1)}, bf16[512,2560]{1,0:T(8,128)(2,1)}, u32[]{:S(2)}, u32[]{:S(2)}) collective-permute-start(bf16[512,2560]{1,0:T(8,128)(2,1)S(1)} %constant_dynamic-update-slice_fusion.refs_0_), channel_id=1, source_target_pairs={{0,1},{1,0},{2,3},{3,2},{4,5},{5,4},{6,7},{7,6},{8,9},{9,8},{10,11... | collective-permute-start | bytes 7864328 | tf_op jit(solution)/shard_map/ppermute | solution.py:36
  135.1 35.1 %collective-permute-start.10 = (bf16[128,2560]{1,0:T(8,128)(2,1)S(1)}, bf16[128,2560]{1,0:T(8,128)(2,1)S(1)}, u32[]{:S(2)}, u32[]{:S(2)}) collective-permute-start(bf16[128,2560]{1,0:T(8,128)(2,1)S(1)} %fusion), channel_id=1, source_target_pairs={{0,8},{24,16},{1,9},{25,17},{2,10},{26,18},{3,11},{27,19},{4,12},{... | collective-permute-start | bytes 1966088 | tf_op jit(solution)/shard_map/ppermute | solution.py:412
  156.9 21.7 %collective-permute-start.12 = (bf16[832,768]{1,0:T(8,128)(2,1)}, bf16[832,768]{1,0:T(8,128)(2,1)}, u32[]{:S(2)}, u32[]{:S(2)}) collective-permute-start(bf16[832,768]{1,0:T(8,128)(2,1)} %collective-permute-done.6.refs_7_), channel_id=1, source_target_pairs={{8,16},{16,8},{9,17},{17,9},{10,18},{18,10},{11,19},{19,11},{12,20... | collective-permute-start | bytes 3833864 | tf_op jit(solution)/shard_map/far0/ppermute | solution.py:452
  170.2 8.4 %collective-permute-start.11 = (bf16[128,2560]{1,0:T(8,128)(2,1)S(1)}, bf16[128,2560]{1,0:T(8,128)(2,1)}, u32[]{:S(2)}, u32[]{:S(2)}) collective-permute-start(bf16[128,2560]{1,0:T(8,128)(2,1)S(1)} %collective-permute-done.10.refs_2_), channel_id=1, source_target_pairs={{0,1},{1,0},{2,3},{3,2},{4,5},{5,4},{6,7},{7,6},{8,9},{9,8},{10,11... | collective-permute-start | bytes 1966088 | tf_op jit(solution)/shard_map/ppermute | solution.py:36
  171.5 28.1 %collective-permute-start.8 = (bf16[832,640]{1,0:T(8,128)(2,1)}, bf16[832,640]{1,0:T(8,128)(2,1)}, u32[]{:S(2)}, u32[]{:S(2)}) collective-permute-start(bf16[832,640]{1,0:T(8,128)(2,1)} %panel.5.refs_6_.own_ref), channel_id=1, source_target_pairs={{0,8},{24,16},{1,9},{25,17},{2,10},{26,18},{3,11},{27,19},{4,12},{... | collective-permute-start | bytes 3194888 | tf_op jit(solution)/shard_map/outer1/ppermute | solution.py:445
  177.0 23.4 %collective-permute-start.13 = (bf16[832,640]{1,0:T(8,128)(2,1)}, bf16[832,640]{1,0:T(8,128)(2,1)}, u32[]{:S(2)}, u32[]{:S(2)}) collective-permute-start(bf16[832,640]{1,0:T(8,128)(2,1)} %panel.5.refs_6_.own_ref), channel_id=1, source_target_pairs={{8,16},{16,8},{9,17},{17,9},{10,18},{18,10},{11,19},{19,11},{12,20... | collective-permute-start | bytes 3194888 | tf_op jit(solution)/shard_map/mate1/ppermute | solution.py:447
  179.7 78.5 %collective-permute-start.14 = (bf16[1280,768]{1,0:T(8,128)(2,1)}, bf16[1280,768]{1,0:T(8,128)(2,1)S(1)}, u32[]{:S(2)}, u32[]{:S(2)}) collective-permute-start(bf16[1280,768]{1,0:T(8,128)(2,1)} %get-tuple-element.63), channel_id=1, source_target_pairs={{8,0},{16,24},{9,1},{17,25},{10,2},{18,26},{11,3},{19,27},{12,4},{... | collective-permute-start | bytes 5898248 | tf_op jit(solution)/shard_map/sums0/ppermute | solution.py:465
  199.6 97.9 %collective-permute-start.17 = (bf16[832,640]{1,0:T(8,128)(2,1)}, bf16[832,640]{1,0:T(8,128)(2,1)S(1)}, u32[]{:S(2)}, u32[]{:S(2)}) collective-permute-start(bf16[832,640]{1,0:T(8,128)(2,1)} %collective-permute-done.8.refs_7_), channel_id=1, source_target_pairs={{8,16},{16,8},{9,17},{17,9},{10,18},{18,10},{11,19},{19,11},{12,20... | collective-permute-start | bytes 3194888 | tf_op jit(solution)/shard_map/far1/ppermute | solution.py:452
  215.0 66.1 %collective-permute-start.15 = (bf16[832,512]{1,0:T(8,128)(2,1)}, bf16[832,512]{1,0:T(8,128)(2,1)S(1)}, u32[]{:S(2)}, u32[]{:S(2)}) collective-permute-start(bf16[832,512]{1,0:T(8,128)(2,1)} %panel.6.refs_6_.own_ref), channel_id=1, source_target_pairs={{0,8},{24,16},{1,9},{25,17},{2,10},{26,18},{3,11},{27,19},{4,12},{... | collective-permute-start | bytes 2555912 | tf_op jit(solution)/shard_map/outer2/ppermute | solution.py:445
  237.7 63.0 %collective-permute-start.19 = (bf16[832,512]{1,0:T(8,128)(2,1)}, bf16[832,512]{1,0:T(8,128)(2,1)S(1)}, u32[]{:S(2)}, u32[]{:S(2)}) collective-permute-start(bf16[832,512]{1,0:T(8,128)(2,1)} %panel.6.refs_6_.own_ref), channel_id=1, source_target_pairs={{8,16},{16,8},{9,17},{17,9},{10,18},{18,10},{11,19},{19,11},{12,20... | collective-permute-start | bytes 2555912 | tf_op jit(solution)/shard_map/mate2/ppermute | solution.py:447
  281.1 19.6 %collective-permute-start.20 = (bf16[832,512]{1,0:T(8,128)(2,1)S(1)}, bf16[832,512]{1,0:T(8,128)(2,1)}, u32[]{:S(2)}, u32[]{:S(2)}) collective-permute-start(bf16[832,512]{1,0:T(8,128)(2,1)S(1)} %collective-permute-done.15.refs_7_), channel_id=1, source_target_pairs={{8,16},{16,8},{9,17},{17,9},{10,18},{18,10},{11,19},{19,11},{12,20... | collective-permute-start | bytes 2555912 | tf_op jit(solution)/shard_map/far2/ppermute | solution.py:452
  282.7 17.9 %collective-permute-start.18 = (bf16[832,512]{1,0:T(8,128)(2,1)}, bf16[832,512]{1,0:T(8,128)(2,1)S(1)}, u32[]{:S(2)}, u32[]{:S(2)}) collective-permute-start(bf16[832,512]{1,0:T(8,128)(2,1)} %get-tuple-element.82.refs_6_.own_ref), channel_id=1, source_target_pairs={{8,16},{16,8},{9,17},{17,9},{10,18},{18,10},{11,19},{19,11},{12,20... | collective-permute-start | bytes 2555912 | tf_op jit(solution)/shard_map/mate3/ppermute | solution.py:447
  283.5 19.9 %collective-permute-start.16 = (bf16[832,512]{1,0:T(8,128)(2,1)}, bf16[832,512]{1,0:T(8,128)(2,1)S(1)}, u32[]{:S(2)}, u32[]{:S(2)}) collective-permute-start(bf16[832,512]{1,0:T(8,128)(2,1)} %get-tuple-element.82.refs_6_.own_ref), channel_id=1, source_target_pairs={{0,8},{24,16},{1,9},{25,17},{2,10},{26,18},{3,11},{27,19},{4,12},{... | collective-permute-start | bytes 2555912 | tf_op jit(solution)/shard_map/outer3/ppermute | solution.py:445
  299.3 50.3 %collective-permute-start.22 = (bf16[1280,640]{1,0:T(8,128)(2,1)}, bf16[1280,640]{1,0:T(8,128)(2,1)S(1)}, u32[]{:S(2)}, u32[]{:S(2)}) collective-permute-start(bf16[1280,640]{1,0:T(8,128)(2,1)} %get-tuple-element.76), channel_id=1, source_target_pairs={{8,0},{16,24},{9,1},{17,25},{10,2},{18,26},{11,3},{19,27},{12,4},{... | collective-permute-start | bytes 4915208 | tf_op jit(solution)/shard_map/sums1/ppermute | solution.py:465
  303.4 56.0 %copy-start.16 = (bf16[832,512]{1,0:T(8,128)(2,1)}, bf16[832,512]{1,0:T(8,128)(2,1)S(1)}, u32[]{:S(2)}) copy-start(bf16[832,512]{1,0:T(8,128)(2,1)S(1)} %collective-permute-done.16.refs_7_) | copy-start | bytes 2555908
  303.4 56.0 %collective-permute-start.21 = (bf16[832,512]{1,0:T(8,128)(2,1)S(1)}, bf16[832,512]{1,0:T(8,128)(2,1)S(1)}, u32[]{:S(2)}, u32[]{:S(2)}) collective-permute-start(bf16[832,512]{1,0:T(8,128)(2,1)S(1)} %collective-permute-done.16.refs_7_), channel_id=1, source_target_pairs={{8,16},{16,8},{9,17},{17,9},{10,18},{18,10},{11,19},{19,11},{12,20... | collective-permute-start | bytes 2555912 | tf_op jit(solution)/shard_map/far3/ppermute | solution.py:452
  304.1 72.1 %collective-permute-start.23 = (bf16[1280,512]{1,0:T(8,128)(2,1)}, bf16[1280,512]{1,0:T(8,128)(2,1)S(1)}, u32[]{:S(2)}, u32[]{:S(2)}) collective-permute-start(bf16[1280,512]{1,0:T(8,128)(2,1)} %get-tuple-element.80), channel_id=1, source_target_pairs={{8,0},{16,24},{9,1},{17,25},{10,2},{18,26},{11,3},{19,27},{12,4},{... | collective-permute-start | bytes 3932168 | tf_op jit(solution)/shard_map/sums2/ppermute | solution.py:465
  305.4 55.9 %collective-permute-start.24 = (bf16[832,384]{1,0:T(8,128)(2,1)S(1)}, bf16[832,384]{1,0:T(8,128)(2,1)S(1)}, u32[]{:S(2)}, u32[]{:S(2)}) collective-permute-start(bf16[832,384]{1,0:T(8,128)(2,1)S(1)} %copy-done.1), channel_id=1, source_target_pairs={{0,8},{24,16},{1,9},{25,17},{2,10},{26,18},{3,11},{27,19},{4,12},{... | collective-permute-start | bytes 1916936 | tf_op jit(solution)/shard_map/outer4/ppermute | solution.py:445
  341.8 34.4 %collective-permute-start.25 = (bf16[832,384]{1,0:T(8,128)(2,1)S(1)}, bf16[832,384]{1,0:T(8,128)(2,1)S(1)}, u32[]{:S(2)}, u32[]{:S(2)}) collective-permute-start(bf16[832,384]{1,0:T(8,128)(2,1)S(1)} %copy-done.1), channel_id=1, source_target_pairs={{8,16},{16,8},{9,17},{17,9},{10,18},{18,10},{11,19},{19,11},{12,20... | collective-permute-start | bytes 1916936 | tf_op jit(solution)/shard_map/mate4/ppermute | solution.py:447
  361.4 14.8 %collective-permute-start.26 = (bf16[832,384]{1,0:T(8,128)(2,1)S(1)}, bf16[832,384]{1,0:T(8,128)(2,1)S(1)}, u32[]{:S(2)}, u32[]{:S(2)}) collective-permute-start(bf16[832,384]{1,0:T(8,128)(2,1)S(1)} %collective-permute-done.24.refs_7_), channel_id=1, source_target_pairs={{8,16},{16,8},{9,17},{17,9},{10,18},{18,10},{11,19},{19,11},{12,20... | collective-permute-start | bytes 1916936 | tf_op jit(solution)/shard_map/far4/ppermute | solution.py:452
  362.1 47.6 %collective-permute-start.28 = (bf16[1280,512]{1,0:T(8,128)(2,1)}, bf16[1280,512]{1,0:T(8,128)(2,1)S(1)}, u32[]{:S(2)}, u32[]{:S(2)}) collective-permute-start(bf16[1280,512]{1,0:T(8,128)(2,1)} %get-tuple-element.87), channel_id=1, source_target_pairs={{8,0},{16,24},{9,1},{17,25},{10,2},{18,26},{11,3},{19,27},{12,4},{... | collective-permute-start | bytes 3932168 | tf_op jit(solution)/shard_map/sums3/ppermute | solution.py:465
  378.7 43.6 %collective-permute-start.27 = (bf16[1280,384]{1,0:T(8,128)(2,1)}, bf16[1280,384]{1,0:T(8,128)(2,1)S(1)}, u32[]{:S(2)}, u32[]{:S(2)}) collective-permute-start(bf16[1280,384]{1,0:T(8,128)(2,1)} %products.10), channel_id=1, source_target_pairs={{8,0},{16,24},{9,1},{17,25},{10,2},{18,26},{11,3},{19,27},{12,4},{... | collective-permute-start | bytes 2949128 | tf_op jit(solution)/shard_map/sums4/ppermute | solution.py:465
  (19 other events, 107.0 us)
Sparse Core Ops, SparseCore 0:
  11.5 94.4 all-gather.4
  107.9 84.5 all-gather.6
where the time goes:
time: 445 us; the launch traced here: 437 us
  Pallas kernels  120 us (27%)
  waiting for transfers between devices  115 us (26%)
  starting transfers between devices  110 us (25%)
  blocking collectives  48.3 us (11%)
  local copies, waits for them, and re-layouts  19.4 us (4%)
  between operations  14.9 us (3%)
  other arithmetic  5.65 us (1%)
    pallas_call x4, Pallas kernels, panel_of(): pl.pallas_call(functools.partial(panel_kernel, steps, splits), out_shape=...  75 us
    ppermute x5, starting transfers between devices, send(): outer[k] = lax.ppermute(sent, 'dp', TO_INNER)  74.1 us
    ppermute x5, waiting for transfers between devices, multiply(): received[k] = lax.ppermute(out[k], 'dp', TO_OUTER)  65 us
    pallas_call x5, Pallas kernels, finish(): pl.pallas_call(functools.partial(finish_kernel, m, start, width), out_sha...  38.8 us
    ppermute x4, waiting for transfers between devices, fetch_half(): fetched.append(lax.ppermute(after(part, *fetched[-1:]), 'dp', TO_INNER))  28.4 us
    all_to_all x1, blocking collectives, token_rows(): parts = lax.all_to_all(part, 'dp', 0, 0, tiled=True)  23.1 us
    ppermute x5, waiting for transfers between devices, send(): outer[k] = lax.ppermute(sent, 'dp', TO_INNER)  19.4 us
    ppermute x4, starting transfers between devices, fetch_half(): fetched.append(lax.ppermute(after(part, *fetched[-1:]), 'dp', TO_INNER))  15.5 us
  transfers between devices with their start and end apart: 31, of which 11 were waited for; matrix products, arithmetic and copies ran while one was open for 4% of the time, Pallas kernels for 26%

commit v1 on v0

--- a/solution.py
+++ b/solution.py
@@ -428,8 +428,7 @@
     token_share = joined(token_share, swap(token_share, 2), 2)
     token_rest = swap(token_share, 4)
 
-    work = [(0, start, width) for start, width in pieces(columns, 768)]
-    work += [(1, start, width) for start, width in pieces(columns, WIDTH)]
+    work = [(m, start, width) for m in range(2) for start, width in pieces(columns, WIDTH)]
     own, outer, mate, far, out, received = ({} for _ in range(6))
     grown = gate = hidden = theirs = None
 
@@ -486,31 +485,34 @@
     mine = (width_growth, token_growth)
     rows_half = jnp.concatenate(fetched[:2] + [after(fetched[2], own[0])], axis=0)
     send(0)
-    panel([1], own[0], token_growth, rows_half)
+    panel([1, 2], own[0], token_growth, rows_half)
     forward(0, mate[0], own[1])
     token_half = after(token_half, own[1])
     theirs = (rows_half, swap(rows_half, 1), token_half, swap(token_half, 1))
     send(1, outer[0])
-    multiply(0, far[0])
-    forward(1, out[0])
-    panel([2], outer[1], out[0], mate[1])
-    send(2)
-    panel([3, 4], own[2], received[0])
-    forward(2, own[3], mate[1])
-    send(3, outer[2])
+    forward(1, far[0])
+    send(2, outer[1])
+    multiply(0, outer[1])
+    forward(2, out[0])
+    panel([3, 4, 5], outer[2], mate[1])
+    send(3)
+    multiply(1, own[3], received[0], far[2])
+    forward(3, out[1], mate[3])
+    send(4, outer[3])
+    multiply(2, outer[3])
     conclude(0)
-    multiply(1, outer[2])
-    multiply(2, out[1], mate[3])
-    forward(3, out[2])
-    send(4, outer[3])
+    forward(4, out[2], far[3])
+    send(5, outer[4])
     conclude(1)
-    multiply(3, outer[3])
-    forward(4, out[3])
+    multiply(3, outer[4])
+    forward(5, out[3], far[4])
     conclude(2)
-    multiply(4, out[3], received[2], keeping=False)
-    multiply(4, out[4], sending=False)
+    multiply(4, outer[5])
     conclude(3)
+    multiply(5, out[4], keeping=False)
+    multiply(5, out[5], sending=False)
     conclude(4)
+    conclude(5)
     return jnp.swapaxes(grown, 1, 2), hidden.T
 
 

time: 445 us -> 417 us (0.937)
  starting transfers between devices: 110 us -> 81 us
    ppermute x5 -> x6, starting transfers between devices: 74.1 us -> 41.4 us  [send(): outer[k] = lax.ppermute(sent, 'dp', TO_INNER)]
    ppermute x5 -> x6, waiting for transfers between devices: 19.4 us -> 40.5 us  [send(): outer[k] = lax.ppermute(sent, 'dp', TO_INNER)]
    ppermute x4, waiting for transfers between devices: 28.4 us -> 16.9 us  [fetch_half(): fetched.append(lax.ppermute(after(part, *fetched[-1:]), 'dp', TO_INNER))]
    ppermute x5 -> x6, waiting for transfers between devices: 65 us -> 55.9 us  [multiply(): received[k] = lax.ppermute(out[k], 'dp', TO_OUTER)]
    pallas_call x4 -> x3, Pallas kernels: 75 us -> 69.9 us  [panel_of(): pl.pallas_call(functools.partial(panel_kernel, steps, splits), out_shape=...]
    pallas_call x5 -> x6, Pallas kernels: 38.8 us -> 42.9 us  [finish(): pl.pallas_call(functools.partial(finish_kernel, m, start, width), out_sha...]
  transfers between devices with their start and end apart: 31 -> 35, of which waited for: 11 -> 11; matrix products, arithmetic and copies ran while one was open for 4% -> 4% of each run, Pallas kernels for 26% -> 28%
where the time goes in v1:
time: 417 us; the launch traced here: 409 us
  Pallas kernels  120 us (29%)
  waiting for transfers between devices  118 us (28%)
  starting transfers between devices  81 us (19%)
  blocking collectives  48.3 us (12%)
  local copies, waits for them, and re-layouts  16.8 us (4%)
  between operations  14.9 us (4%)
  other arithmetic  5.57 us (1%)
  matrix products  4.33 us (1%)
    pallas_call x3, Pallas kernels, panel_of(): pl.pallas_call(functools.partial(panel_kernel, steps, splits), out_shape=...  69.9 us
    ppermute x6, waiting for transfers between devices, multiply(): received[k] = lax.ppermute(out[k], 'dp', TO_OUTER)  55.9 us
    pallas_call x6, Pallas kernels, finish(): pl.pallas_call(functools.partial(finish_kernel, m, start, width), out_sha...  42.9 us
    ppermute x6, starting transfers between devices, send(): outer[k] = lax.ppermute(sent, 'dp', TO_INNER)  41.4 us
    ppermute x6, waiting for transfers between devices, send(): outer[k] = lax.ppermute(sent, 'dp', TO_INNER)  40.5 us
    all_to_all x1, blocking collectives, token_rows(): parts = lax.all_to_all(part, 'dp', 0, 0, tiled=True)  23.1 us
    ppermute x4, waiting for transfers between devices, fetch_half(): fetched.append(lax.ppermute(after(part, *fetched[-1:]), 'dp', TO_INNER))  16.9 us
    ppermute x4, starting transfers between devices, fetch_half(): fetched.append(lax.ppermute(after(part, *fetched[-1:]), 'dp', TO_INNER))  14 us
  transfers between devices with their start and end apart: 35, of which 11 were waited for; matrix products, arithmetic and copies ran while one was open for 4% of the time, Pallas kernels for 28%

profile of v1, /device:TPU:0, one launch (start us, length us, event | category | flops | bytes accessed | tf_op | source)
XLA Modules:
  0.0 409.0 jit_solution(6986633412777574640)
XLA Ops:
  7.2 4.2 %fusion.2 = (bf16[1,104,8960]{2,1,0:T(8,128)(2,1)}, bf16[1,104,8960]{2,1,0:T(8,128)(2,1)}) fusion(bf16[2,104,8960]{2,1,0:T(8,128)(2,1)} %param.6), kind=kLoop, calls=%fused_computation.19 | loop fusion | bytes 7454720 | tf_op jit(solution)/shard_map/slice | solution.py:424
  13.7 5.0 %collective-permute-start = (bf16[176,2560]{1,0:T(8,128)(2,1)S(1)}, bf16[176,2560]{1,0:T(8,128)(2,1)S(1)}, u32[]{:S(2)}, u32[]{:S(2)}) collective-permute-start(bf16[176,2560]{1,0:T(8,128)(2,1)S(1)} %get-tuple-element.123), channel_id=1, source_target_pairs={{0,8},{24,16},{1,9},{25,17},{2,10},{26,18},{3,11},{27,19},{4,12},{... | collective-permute-start | bytes 2703368 | tf_op jit(solution)/shard_map/ppermute | solution.py:412
  18.7 13.3 %all_to_all.44 = bf16[8,32,512]{2,1,0:T(8,128)(2,1)S(1)} all-to-all(bf16[8,32,512]{2,1,0:T(8,128)(2,1)S(1)} %bitcast.22), channel_id=1, replica_groups=mesh['dp'=4,'tensor'=8] {'tensor'}, dimensions={0} | all-to-all | bytes 524288 | tf_op jit(solution)/shard_map/all_to_all | solution.py:27
  32.4 11.9 %all_to_all.45 = bf16[32,4,1024]{2,0,1:T(8,128)(2,1)S(1)} all-to-all(bf16[32,4,1024]{2,0,1:T(8,128)(2,1)S(1)} %copy.31), channel_id=1, replica_groups=mesh['dp'=4,'tensor'=8] {'dp'}, dimensions={1} | all-to-all | bytes 524288 | tf_op jit(solution)/shard_map/all_to_all | solution.py:28
  44.4 4.3 %convolution_convert_fusion = bf16[128,3328]{1,0:T(8,128)(2,1)S(1)} fusion(bf16[128,1024]{1,0:T(8,128)(2,1)S(1)} %bitcast.20, bf16[1024,3328]{1,0:T(8,128)(2,1)} %rows_ref.11), kind=kOutput, calls=%fused_computation | convolution fusion | flops 872841216 | bytes 7929856 | tf_op jit(solution)/shard_map/dot_general | solution.py:30
  48.7 23.1 %all_to_all.46 = bf16[4,32,3328]{2,1,0:T(8,128)(2,1)S(1)} all-to-all(bf16[4,32,3328]{2,1,0:T(8,128)(2,1)S(1)} %bitcast.19), channel_id=1, replica_groups=mesh['dp'=4,'tensor'=8] {'dp'}, dimensions={0} | all-to-all | bytes 1703936 | tf_op jit(solution)/shard_map/all_to_all | solution.py:31
  74.2 2.4 collective-permute-start.4
  79.5 16.9 %collective-permute-done.4 = bf16[176,2560]{1,0:T(8,128)(2,1)S(1)} collective-permute-done((bf16[176,2560]{1,0:T(8,128)(2,1)S(1)}, bf16[176,2560]{1,0:T(8,128)(2,1)S(1)}, u32[]{:S(2)}, u32[]{:S(2)}) %collective-permute-start.4) | collective-permute-done | bytes 901152 | tf_op jit(solution)/shard_map/ppermute | solution.py:412
  96.4 5.3 %collective-permute-start.5 = (bf16[160,2560]{1,0:T(8,128)(2,1)}, bf16[160,2560]{1,0:T(8,128)(2,1)}, u32[]{:S(2)}, u32[]{:S(2)}) collective-permute-start(bf16[160,2560]{1,0:T(8,128)(2,1)} %dynamic_slice.18), channel_id=1, source_target_pairs={{0,8},{24,16},{1,9},{25,17},{2,10},{26,18},{3,11},{27,19},{4,12},{... | collective-permute-start | bytes 2457608 | tf_op jit(solution)/shard_map/ppermute | solution.py:412
  106.0 15.2 %panel.3.refs_6_.own_ref = bf16[832,512]{1,0:T(8,128)(2,1)} custom-call(bf16[832,8960]{1,0:T(8,128)(2,1)} %bitcast.24, bf16[1376,8960]{1,0:T(8,128)(2,1)} %growth_ref.5), custom_call_target="tpu_custom_call" | custom-call | flops 11450449920 | tf_op jit(solution)/shard_map/panel/pallas_call | solution.py:107
  121.2 4.2 %collective-permute-start.6 = (bf16[832,512]{1,0:T(8,128)(2,1)}, bf16[832,512]{1,0:T(8,128)(2,1)}, u32[]{:S(2)}, u32[]{:S(2)}) collective-permute-start(bf16[832,512]{1,0:T(8,128)(2,1)} %panel.3.refs_6_.own_ref), channel_id=1, source_target_pairs={{0,8},{24,16},{1,9},{25,17},{2,10},{26,18},{3,11},{27,19},{4,12},{... | collective-permute-start | bytes 2555912 | tf_op jit(solution)/shard_map/outer0/ppermute | solution.py:444
  126.1 2.5 collective-permute-done.3
  135.0 23.1 %panel.4 = (bf16[832,512]{1,0:T(8,128)(2,1)}, bf16[832,384]{1,0:T(8,128)(2,1)}) custom-call(bf16[832,8960]{1,0:T(8,128)(2,1)} %bitcast.25, bf16[1376,8960]{1,0:T(8,128)(2,1)} %growth_ref.5), custom_call_target="tpu_custom_call" | custom-call | flops 20038287360 | tf_op jit(solution)/shard_map/panel/pallas_call | solution.py:107
  164.8 13.4 %collective-permute-done.8.refs_7_ = bf16[832,512]{1,0:T(8,128)(2,1)} collective-permute-done((bf16[832,512]{1,0:T(8,128)(2,1)}, bf16[832,512]{1,0:T(8,128)(2,1)}, u32[]{:S(2)}, u32[]{:S(2)}) %collective-permute-start.8) | collective-permute-done | bytes 852000 | tf_op jit(solution)/shard_map/outer1/ppermute | solution.py:444
  179.7 6.9 %collective-permute-start.10 = (bf16[832,384]{1,0:T(8,128)(2,1)}, bf16[832,384]{1,0:T(8,128)(2,1)}, u32[]{:S(2)}, u32[]{:S(2)}) collective-permute-start(bf16[832,384]{1,0:T(8,128)(2,1)} %get-tuple-element.89.refs_6_.own_ref), channel_id=1, source_target_pairs={{0,8},{24,16},{1,9},{25,17},{2,10},{26,18},{3,11},{27,19},{4,12},{... | collective-permute-start | bytes 1916936 | tf_op jit(solution)/shard_map/outer2/ppermute | solution.py:444
  190.8 7.9 %collective-permute-done.10.refs_7_ = bf16[832,384]{1,0:T(8,128)(2,1)} collective-permute-done((bf16[832,384]{1,0:T(8,128)(2,1)}, bf16[832,384]{1,0:T(8,128)(2,1)}, u32[]{:S(2)}, u32[]{:S(2)}) %collective-permute-start.10) | collective-permute-done | bytes 639008 | tf_op jit(solution)/shard_map/outer2/ppermute | solution.py:444
  200.3 31.6 %panel.5 = (bf16[832,512]{1,0:T(8,128)(2,1)}, bf16[832,512]{1,0:T(8,128)(2,1)}, bf16[832,384]{1,0:T(8,128)(2,1)}) custom-call(bf16[832,8960]{1,0:T(8,128)(2,1)} %bitcast.23, bf16[1376,8960]{1,0:T(8,128)(2,1)} %growth_ref.5), custom_call_target="tpu_custom_call" | custom-call | flops 31488737280 | tf_op jit(solution)/shard_map/panel/pallas_call | solution.py:107
  231.9 9.6 %collective-permute-start.15 = (bf16[832,512]{1,0:T(8,128)(2,1)}, bf16[832,512]{1,0:T(8,128)(2,1)S(1)}, u32[]{:S(2)}, u32[]{:S(2)}) collective-permute-start(bf16[832,512]{1,0:T(8,128)(2,1)} %get-tuple-element.95.refs_6_.own_ref), channel_id=1, source_target_pairs={{0,8},{24,16},{1,9},{25,17},{2,10},{26,18},{3,11},{27,19},{4,12},{... | collective-permute-start | bytes 2555912 | tf_op jit(solution)/shard_map/outer3/ppermute | solution.py:444
  244.7 13.7 %collective-permute-done.15.refs_7_ = bf16[832,512]{1,0:T(8,128)(2,1)S(1)} collective-permute-done((bf16[832,512]{1,0:T(8,128)(2,1)}, bf16[832,512]{1,0:T(8,128)(2,1)S(1)}, u32[]{:S(2)}, u32[]{:S(2)}) %collective-permute-start.15) | collective-permute-done | bytes 852000 | tf_op jit(solution)/shard_map/outer3/ppermute | solution.py:444
  259.1 12.7 %collective-permute-start.20 = (bf16[832,512]{1,0:T(8,128)(2,1)S(1)}, bf16[832,512]{1,0:T(8,128)(2,1)S(1)}, u32[]{:S(2)}, u32[]{:S(2)}) collective-permute-start(bf16[832,512]{1,0:T(8,128)(2,1)S(1)} %copy-done.13), channel_id=1, source_target_pairs={{0,8},{24,16},{1,9},{25,17},{2,10},{26,18},{3,11},{27,19},{4,12},{... | collective-permute-start | bytes 2555912 | tf_op jit(solution)/shard_map/outer4/ppermute | solution.py:444
  275.6 7.5 %finish.6 = (bf16[2,1376,1024]{2,1,0:T(8,128)(2,1)}, f32[256,1408]{1,0:T(8,128)}) custom-call(s32[7]{0:T(128)} %pad_add_fusion.slots_ref, bf16[1024,3328]{1,0:T(8,128)(2,1)} %rows_ref.11, bf16[256,3328]{1,0:T(8,128)(2,1)} %pad_maximum_fusion.refs_5_.tokens_ref, bf16[832,512]{1,0:T(8,128)(2,1)} %panel.3.refs_6_.own_ref, ...), custom_call_target="tpu_custom_call", output_to_operand_aliasing={{0}: (6, {}), {1}: (5, {})} | custom-call | tf_op jit(solution)/shard_map/finish/pallas_call | solution.py:372
  283.2 5.5 %collective-permute-done.20.refs_7_ = bf16[832,512]{1,0:T(8,128)(2,1)S(1)} collective-permute-done((bf16[832,512]{1,0:T(8,128)(2,1)S(1)}, bf16[832,512]{1,0:T(8,128)(2,1)S(1)}, u32[]{:S(2)}, u32[]{:S(2)}) %collective-permute-start.20) | collective-permute-done | bytes 852000 | tf_op jit(solution)/shard_map/outer4/ppermute | solution.py:444
  290.3 5.8 %collective-permute-start.23 = (bf16[832,384]{1,0:T(8,128)(2,1)S(1)}, bf16[832,384]{1,0:T(8,128)(2,1)S(1)}, u32[]{:S(2)}, u32[]{:S(2)}) collective-permute-start(bf16[832,384]{1,0:T(8,128)(2,1)S(1)} %copy-done.1), channel_id=1, source_target_pairs={{0,8},{24,16},{1,9},{25,17},{2,10},{26,18},{3,11},{27,19},{4,12},{... | collective-permute-start | bytes 1916936 | tf_op jit(solution)/shard_map/outer5/ppermute | solution.py:444
  297.2 7.2 %finish.7 = (bf16[2,1376,1024]{2,1,0:T(8,128)(2,1)}, f32[256,1408]{1,0:T(8,128)}) custom-call(s32[7]{0:T(128)} %pad_add_fusion.slots_ref, bf16[1024,3328]{1,0:T(8,128)(2,1)} %rows_ref.11, bf16[256,3328]{1,0:T(8,128)(2,1)} %pad_maximum_fusion.refs_5_.tokens_ref, ...), custom_call_target="tpu_custom_call", output_to_operand_aliasing={{0}: (6, {}), {1}: (5, {})} | custom-call | tf_op jit(solution)/shard_map/finish/pallas_call | solution.py:372
  305.2 8.3 %collective-permute-done.27.got_ref = bf16[1280,384]{1,0:T(8,128)(2,1)S(1)} collective-permute-done((bf16[1280,384]{1,0:T(8,128)(2,1)}, bf16[1280,384]{1,0:T(8,128)(2,1)S(1)}, u32[]{:S(2)}, u32[]{:S(2)}) %collective-permute-start.27) | collective-permute-done | bytes 983072 | tf_op jit(solution)/shard_map/sums2/ppermute | solution.py:464
  314.7 6.8 %finish.8 = (bf16[2,1376,1024]{2,1,0:T(8,128)(2,1)}, f32[256,1408]{1,0:T(8,128)}) custom-call(s32[7]{0:T(128)} %pad_add_fusion.slots_ref, bf16[1024,3328]{1,0:T(8,128)(2,1)} %rows_ref.11, bf16[256,3328]{1,0:T(8,128)(2,1)} %pad_maximum_fusion.refs_5_.tokens_ref, ...), custom_call_target="tpu_custom_call", output_to_operand_aliasing={{0}: (6, {}), {1}: (5, {})} | custom-call | tf_op jit(solution)/shard_map/finish/pallas_call | solution.py:372
  328.7 17.7 %collective-permute-done.32.got_ref = bf16[1280,512]{1,0:T(8,128)(2,1)S(1)} collective-permute-done((bf16[1280,512]{1,0:T(8,128)(2,1)}, bf16[1280,512]{1,0:T(8,128)(2,1)S(1)}, u32[]{:S(2)}, u32[]{:S(2)}) %collective-permute-start.32) | collective-permute-done | bytes 1310752 | tf_op jit(solution)/shard_map/sums3/ppermute | solution.py:464
  347.5 7.3 %finish.9 = (bf16[2,1376,1024]{2,1,0:T(8,128)(2,1)}, bf16[1376,256]{1,0:T(8,128)(2,1)}) custom-call(s32[7]{0:T(128)} %pad_add_fusion.slots_ref, bf16[1024,3328]{1,0:T(8,128)(2,1)} %rows_ref.11, bf16[256,3328]{1,0:T(8,128)(2,1)} %pad_maximum_fusion.refs_5_.tokens_ref, ...), custom_call_target="tpu_custom_call", output_to_operand_aliasing={{0}: (6, {}), {1}: (7, {})} | custom-call | tf_op jit(solution)/shard_map/finish/pallas_call | solution.py:372
  355.8 21.2 %collective-permute-done.31.got_ref = bf16[1280,512]{1,0:T(8,128)(2,1)S(1)} collective-permute-done((bf16[1280,512]{1,0:T(8,128)(2,1)}, bf16[1280,512]{1,0:T(8,128)(2,1)S(1)}, u32[]{:S(2)}, u32[]{:S(2)}) %collective-permute-start.31) | collective-permute-done | bytes 1310752 | tf_op jit(solution)/shard_map/sums4/ppermute | solution.py:464
  378.1 7.3 %finish.10 = (bf16[2,1376,1024]{2,1,0:T(8,128)(2,1)}, bf16[1376,256]{1,0:T(8,128)(2,1)}) custom-call(s32[7]{0:T(128)} %pad_add_fusion.slots_ref, bf16[1024,3328]{1,0:T(8,128)(2,1)} %rows_ref.11, bf16[256,3328]{1,0:T(8,128)(2,1)} %pad_maximum_fusion.refs_5_.tokens_ref, ...), custom_call_target="tpu_custom_call", output_to_operand_aliasing={{0}: (6, {}), {1}: (7, {})} | custom-call | tf_op jit(solution)/shard_map/finish/pallas_call | solution.py:372
  385.4 8.7 %collective-permute-done.30.got_ref = bf16[1280,384]{1,0:T(8,128)(2,1)S(1)} collective-permute-done((bf16[1280,384]{1,0:T(8,128)(2,1)}, bf16[1280,384]{1,0:T(8,128)(2,1)S(1)}, u32[]{:S(2)}, u32[]{:S(2)}) %collective-permute-start.30) | collective-permute-done | bytes 983072 | tf_op jit(solution)/shard_map/sums5/ppermute | solution.py:464
  395.1 6.9 %finish.11 = (bf16[2,1376,1024]{2,1,0:T(8,128)(2,1)}, bf16[1376,256]{1,0:T(8,128)(2,1)}) custom-call(s32[7]{0:T(128)} %pad_add_fusion.slots_ref, bf16[1024,3328]{1,0:T(8,128)(2,1)} %rows_ref.11, bf16[256,3328]{1,0:T(8,128)(2,1)} %pad_maximum_fusion.refs_5_.tokens_ref, ...), custom_call_target="tpu_custom_call", output_to_operand_aliasing={{0}: (6, {}), {1}: (7, {})} | custom-call | tf_op jit(solution)/shard_map/finish/pallas_call | solution.py:372
  (119 shorter events, 56.9 us)
Async XLA Ops:
  7.2 98.8 %all-gather.5.cloned.1.call-start = ((), (), s32[]{:S(2)}) async-start(), calls=%async_computation.3 | async-start | bytes 16773120 | tf_op jit(solution)/shard_map/all_gather | solution.py:424
  11.4 188.9 %all-gather.7.cloned.1.call-start = ((), (), s32[]{:S(2)}) async-start(), calls=%async_computation.4 | async-start | bytes 16773120 | tf_op jit(solution)/shard_map/all_gather | solution.py:424
  13.7 30.6 %collective-permute-start = (bf16[176,2560]{1,0:T(8,128)(2,1)S(1)}, bf16[176,2560]{1,0:T(8,128)(2,1)S(1)}, u32[]{:S(2)}, u32[]{:S(2)}) collective-permute-start(bf16[176,2560]{1,0:T(8,128)(2,1)S(1)} %get-tuple-element.123), channel_id=1, source_target_pairs={{0,8},{24,16},{1,9},{25,17},{2,10},{26,18},{3,11},{27,19},{4,12},{... | collective-permute-start | bytes 2703368 | tf_op jit(solution)/shard_map/ppermute | solution.py:412
  74.2 22.1 %collective-permute-start.4 = (bf16[176,2560]{1,0:T(8,128)(2,1)S(1)}, bf16[176,2560]{1,0:T(8,128)(2,1)S(1)}, u32[]{:S(2)}, u32[]{:S(2)}) collective-permute-start(bf16[176,2560]{1,0:T(8,128)(2,1)S(1)} %get-tuple-element.63), channel_id=1, source_target_pairs={{0,8},{24,16},{1,9},{25,17},{2,10},{26,18},{3,11},{27,19},{4,12},{... | collective-permute-start | bytes 2703368 | tf_op jit(solution)/shard_map/ppermute | solution.py:412
  76.7 25.0 %collective-permute-start.2 = (bf16[64,3328]{1,0:T(8,128)(2,1)S(1)}, bf16[64,3328]{1,0:T(8,128)(2,1)S(1)}, u32[]{:S(2)}, u32[]{:S(2)}) collective-permute-start(bf16[64,3328]{1,0:T(8,128)(2,1)S(1)} %pad_maximum_fusion.2), channel_id=1, source_target_pairs={{0,2},{1,3},{2,0},{3,1},{4,6},{5,7},{6,4},{7,5},{8,10},{9,11},{10,... | collective-permute-start | bytes 1277960 | tf_op jit(solution)/shard_map/ppermute | solution.py:36
  96.4 29.8 %collective-permute-start.5 = (bf16[160,2560]{1,0:T(8,128)(2,1)}, bf16[160,2560]{1,0:T(8,128)(2,1)}, u32[]{:S(2)}, u32[]{:S(2)}) collective-permute-start(bf16[160,2560]{1,0:T(8,128)(2,1)} %dynamic_slice.18), channel_id=1, source_target_pairs={{0,8},{24,16},{1,9},{25,17},{2,10},{26,18},{3,11},{27,19},{4,12},{... | collective-permute-start | bytes 2457608 | tf_op jit(solution)/shard_map/ppermute | solution.py:412
  102.8 25.8 %collective-permute-start.3 = (bf16[128,3328]{1,0:T(8,128)(2,1)}, bf16[128,3328]{1,0:T(8,128)(2,1)}, u32[]{:S(2)}, u32[]{:S(2)}) collective-permute-start(bf16[128,3328]{1,0:T(8,128)(2,1)} %pad_maximum_fusion.1), channel_id=1, source_target_pairs={{0,4},{1,5},{2,6},{3,7},{4,0},{5,1},{6,2},{7,3},{8,12},{9,13},{10,... | collective-permute-start | bytes 2555912 | tf_op jit(solution)/shard_map/ppermute | solution.py:36
  121.2 36.9 %collective-permute-start.6 = (bf16[832,512]{1,0:T(8,128)(2,1)}, bf16[832,512]{1,0:T(8,128)(2,1)}, u32[]{:S(2)}, u32[]{:S(2)}) collective-permute-start(bf16[832,512]{1,0:T(8,128)(2,1)} %panel.3.refs_6_.own_ref), channel_id=1, source_target_pairs={{0,8},{24,16},{1,9},{25,17},{2,10},{26,18},{3,11},{27,19},{4,12},{... | collective-permute-start | bytes 2555912 | tf_op jit(solution)/shard_map/outer0/ppermute | solution.py:444
  125.4 32.6 %collective-permute-start.7 = (bf16[832,512]{1,0:T(8,128)(2,1)}, bf16[832,512]{1,0:T(8,128)(2,1)S(1)}, u32[]{:S(2)}, u32[]{:S(2)}) collective-permute-start(bf16[832,512]{1,0:T(8,128)(2,1)} %panel.3.refs_6_.own_ref), channel_id=1, source_target_pairs={{8,16},{16,8},{9,17},{17,9},{10,18},{18,10},{11,19},{19,11},{12,20... | collective-permute-start | bytes 2555912 | tf_op jit(solution)/shard_map/mate0/ppermute | solution.py:446
  129.9 58.3 %collective-permute-start.11 = (bf16[512,2560]{1,0:T(8,128)(2,1)S(1)}, bf16[512,2560]{1,0:T(8,128)(2,1)}, u32[]{:S(2)}, u32[]{:S(2)}) collective-permute-start(bf16[512,2560]{1,0:T(8,128)(2,1)S(1)} %constant_dynamic-update-slice_fusion.refs_0_), channel_id=1, source_target_pairs={{0,1},{1,0},{2,3},{3,2},{4,5},{5,4},{6,7},{7,6},{8,9},{9,8},{10,11... | collective-permute-start | bytes 7864328 | tf_op jit(solution)/shard_map/ppermute | solution.py:36
  133.6 28.2 %collective-permute-start.12 = (bf16[128,2560]{1,0:T(8,128)(2,1)S(1)}, bf16[128,2560]{1,0:T(8,128)(2,1)S(1)}, u32[]{:S(2)}, u32[]{:S(2)}) collective-permute-start(bf16[128,2560]{1,0:T(8,128)(2,1)S(1)} %fusion), channel_id=1, source_target_pairs={{0,8},{24,16},{1,9},{25,17},{2,10},{26,18},{3,11},{27,19},{4,12},{... | collective-permute-start | bytes 1966088 | tf_op jit(solution)/shard_map/ppermute | solution.py:412
  158.1 20.1 %collective-permute-start.8 = (bf16[832,512]{1,0:T(8,128)(2,1)}, bf16[832,512]{1,0:T(8,128)(2,1)}, u32[]{:S(2)}, u32[]{:S(2)}) collective-permute-start(bf16[832,512]{1,0:T(8,128)(2,1)} %get-tuple-element.83.refs_6_.own_ref), channel_id=1, source_target_pairs={{0,8},{24,16},{1,9},{25,17},{2,10},{26,18},{3,11},{27,19},{4,12},{... | collective-permute-start | bytes 2555912 | tf_op jit(solution)/shard_map/outer1/ppermute | solution.py:444
  160.3 17.9 %collective-permute-start.9 = (bf16[832,512]{1,0:T(8,128)(2,1)}, bf16[832,512]{1,0:T(8,128)(2,1)}, u32[]{:S(2)}, u32[]{:S(2)}) collective-permute-start(bf16[832,512]{1,0:T(8,128)(2,1)} %collective-permute-done.6.refs_7_), channel_id=1, source_target_pairs={{8,16},{16,8},{9,17},{17,9},{10,18},{18,10},{11,19},{19,11},{12,20... | collective-permute-start | bytes 2555912 | tf_op jit(solution)/shard_map/far0/ppermute | solution.py:451
  161.8 24.8 %collective-permute-start.13 = (bf16[128,2560]{1,0:T(8,128)(2,1)S(1)}, bf16[128,2560]{1,0:T(8,128)(2,1)}, u32[]{:S(2)}, u32[]{:S(2)}) collective-permute-start(bf16[128,2560]{1,0:T(8,128)(2,1)S(1)} %collective-permute-done.12.refs_2_), channel_id=1, source_target_pairs={{0,1},{1,0},{2,3},{3,2},{4,5},{5,4},{6,7},{7,6},{8,9},{9,8},{10,11... | collective-permute-start | bytes 1966088 | tf_op jit(solution)/shard_map/ppermute | solution.py:36
  163.2 37.1 %collective-permute-start.14 = (bf16[832,512]{1,0:T(8,128)(2,1)}, bf16[832,512]{1,0:T(8,128)(2,1)}, u32[]{:S(2)}, u32[]{:S(2)}) collective-permute-start(bf16[832,512]{1,0:T(8,128)(2,1)} %get-tuple-element.83.refs_6_.own_ref), channel_id=1, source_target_pairs={{8,16},{16,8},{9,17},{17,9},{10,18},{18,10},{11,19},{19,11},{12,20... | collective-permute-start | bytes 2555912 | tf_op jit(solution)/shard_map/mate1/ppermute | solution.py:446
  178.2 64.1 %collective-permute-start.18 = (bf16[832,512]{1,0:T(8,128)(2,1)}, bf16[832,512]{1,0:T(8,128)(2,1)}, u32[]{:S(2)}, u32[]{:S(2)}) collective-permute-start(bf16[832,512]{1,0:T(8,128)(2,1)} %collective-permute-done.8.refs_7_), channel_id=1, source_target_pairs={{8,16},{16,8},{9,17},{17,9},{10,18},{18,10},{11,19},{19,11},{12,20... | collective-permute-start | bytes 2555912 | tf_op jit(solution)/shard_map/far1/ppermute | solution.py:451
  179.7 19.0 %collective-permute-start.10 = (bf16[832,384]{1,0:T(8,128)(2,1)}, bf16[832,384]{1,0:T(8,128)(2,1)}, u32[]{:S(2)}, u32[]{:S(2)}) collective-permute-start(bf16[832,384]{1,0:T(8,128)(2,1)} %get-tuple-element.89.refs_6_.own_ref), channel_id=1, source_target_pairs={{0,8},{24,16},{1,9},{25,17},{2,10},{26,18},{3,11},{27,19},{4,12},{... | collective-permute-start | bytes 1916936 | tf_op jit(solution)/shard_map/outer2/ppermute | solution.py:444
  186.6 86.8 %collective-permute-start.21 = (bf16[832,384]{1,0:T(8,128)(2,1)}, bf16[832,384]{1,0:T(8,128)(2,1)}, u32[]{:S(2)}, u32[]{:S(2)}) collective-permute-start(bf16[832,384]{1,0:T(8,128)(2,1)} %get-tuple-element.89.refs_6_.own_ref), channel_id=1, source_target_pairs={{8,16},{16,8},{9,17},{17,9},{10,18},{18,10},{11,19},{19,11},{12,20... | collective-permute-start | bytes 1916936 | tf_op jit(solution)/shard_map/mate2/ppermute | solution.py:446
  189.5 52.7 %collective-permute-start.16 = (bf16[1280,512]{1,0:T(8,128)(2,1)}, bf16[1280,512]{1,0:T(8,128)(2,1)S(1)}, u32[]{:S(2)}, u32[]{:S(2)}) collective-permute-start(bf16[1280,512]{1,0:T(8,128)(2,1)} %get-tuple-element.77), channel_id=1, source_target_pairs={{8,0},{16,24},{9,1},{17,25},{10,2},{18,26},{11,3},{19,27},{12,4},{... | collective-permute-start | bytes 3932168 | tf_op jit(solution)/shard_map/sums0/ppermute | solution.py:464
  198.8 42.7 %collective-permute-start.17 = (bf16[832,384]{1,0:T(8,128)(2,1)}, bf16[832,384]{1,0:T(8,128)(2,1)}, u32[]{:S(2)}, u32[]{:S(2)}) collective-permute-start(bf16[832,384]{1,0:T(8,128)(2,1)} %collective-permute-done.10.refs_7_), channel_id=1, source_target_pairs={{8,16},{16,8},{9,17},{17,9},{10,18},{18,10},{11,19},{19,11},{12,20... | collective-permute-start | bytes 1916936 | tf_op jit(solution)/shard_map/far2/ppermute | solution.py:451
  231.9 26.5 %collective-permute-start.15 = (bf16[832,512]{1,0:T(8,128)(2,1)}, bf16[832,512]{1,0:T(8,128)(2,1)S(1)}, u32[]{:S(2)}, u32[]{:S(2)}) collective-permute-start(bf16[832,512]{1,0:T(8,128)(2,1)} %get-tuple-element.95.refs_6_.own_ref), channel_id=1, source_target_pairs={{0,8},{24,16},{1,9},{25,17},{2,10},{26,18},{3,11},{27,19},{4,12},{... | collective-permute-start | bytes 2555912 | tf_op jit(solution)/shard_map/outer3/ppermute | solution.py:444
  243.4 52.6 %collective-permute-start.24 = (bf16[1280,512]{1,0:T(8,128)(2,1)}, bf16[1280,512]{1,0:T(8,128)(2,1)S(1)}, u32[]{:S(2)}, u32[]{:S(2)}) collective-permute-start(bf16[1280,512]{1,0:T(8,128)(2,1)} %get-tuple-element.86), channel_id=1, source_target_pairs={{8,0},{16,24},{9,1},{17,25},{10,2},{18,26},{11,3},{19,27},{12,4},{... | collective-permute-start | bytes 3932168 | tf_op jit(solution)/shard_map/sums1/ppermute | solution.py:464
  258.4 30.2 %collective-permute-start.22 = (bf16[832,512]{1,0:T(8,128)(2,1)S(1)}, bf16[832,512]{1,0:T(8,128)(2,1)S(1)}, u32[]{:S(2)}, u32[]{:S(2)}) collective-permute-start(bf16[832,512]{1,0:T(8,128)(2,1)S(1)} %collective-permute-done.15.refs_7_), channel_id=1, source_target_pairs={{8,16},{16,8},{9,17},{17,9},{10,18},{18,10},{11,19},{19,11},{12,20... | collective-permute-start | bytes 2555912 | tf_op jit(solution)/shard_map/far3/ppermute | solution.py:451
  259.1 29.5 %collective-permute-start.20 = (bf16[832,512]{1,0:T(8,128)(2,1)S(1)}, bf16[832,512]{1,0:T(8,128)(2,1)S(1)}, u32[]{:S(2)}, u32[]{:S(2)}) collective-permute-start(bf16[832,512]{1,0:T(8,128)(2,1)S(1)} %copy-done.13), channel_id=1, source_target_pairs={{0,8},{24,16},{1,9},{25,17},{2,10},{26,18},{3,11},{27,19},{4,12},{... | collective-permute-start | bytes 2555912 | tf_op jit(solution)/shard_map/outer4/ppermute | solution.py:444
  271.9 50.4 %collective-permute-start.26 = (bf16[832,512]{1,0:T(8,128)(2,1)S(1)}, bf16[832,512]{1,0:T(8,128)(2,1)}, u32[]{:S(2)}, u32[]{:S(2)}) collective-permute-start(bf16[832,512]{1,0:T(8,128)(2,1)S(1)} %copy-done.13), channel_id=1, source_target_pairs={{8,16},{16,8},{9,17},{17,9},{10,18},{18,10},{11,19},{19,11},{12,20... | collective-permute-start | bytes 2555912 | tf_op jit(solution)/shard_map/mate4/ppermute | solution.py:446
  274.3 39.1 %collective-permute-start.27 = (bf16[1280,384]{1,0:T(8,128)(2,1)}, bf16[1280,384]{1,0:T(8,128)(2,1)S(1)}, u32[]{:S(2)}, u32[]{:S(2)}) collective-permute-start(bf16[1280,384]{1,0:T(8,128)(2,1)} %get-tuple-element.92), channel_id=1, source_target_pairs={{8,0},{16,24},{9,1},{17,25},{10,2},{18,26},{11,3},{19,27},{12,4},{... | collective-permute-start | bytes 2949128 | tf_op jit(solution)/shard_map/sums2/ppermute | solution.py:464
  288.6 32.9 %collective-permute-start.25 = (bf16[832,512]{1,0:T(8,128)(2,1)S(1)}, bf16[832,512]{1,0:T(8,128)(2,1)}, u32[]{:S(2)}, u32[]{:S(2)}) collective-permute-start(bf16[832,512]{1,0:T(8,128)(2,1)S(1)} %collective-permute-done.20.refs_7_), channel_id=1, source_target_pairs={{8,16},{16,8},{9,17},{17,9},{10,18},{18,10},{11,19},{19,11},{12,20... | collective-permute-start | bytes 2555912 | tf_op jit(solution)/shard_map/far4/ppermute | solution.py:451
  290.3 31.3 %collective-permute-start.23 = (bf16[832,384]{1,0:T(8,128)(2,1)S(1)}, bf16[832,384]{1,0:T(8,128)(2,1)S(1)}, u32[]{:S(2)}, u32[]{:S(2)}) collective-permute-start(bf16[832,384]{1,0:T(8,128)(2,1)S(1)} %copy-done.1), channel_id=1, source_target_pairs={{0,8},{24,16},{1,9},{25,17},{2,10},{26,18},{3,11},{27,19},{4,12},{... | collective-permute-start | bytes 1916936 | tf_op jit(solution)/shard_map/outer5/ppermute | solution.py:444
  296.1 28.8 %collective-permute-start.28 = (bf16[832,384]{1,0:T(8,128)(2,1)S(1)}, bf16[832,384]{1,0:T(8,128)(2,1)S(1)}, u32[]{:S(2)}, u32[]{:S(2)}) collective-permute-start(bf16[832,384]{1,0:T(8,128)(2,1)S(1)} %copy-done.1), channel_id=1, source_target_pairs={{8,16},{16,8},{9,17},{17,9},{10,18},{18,10},{11,19},{19,11},{12,20... | collective-permute-start | bytes 1916936 | tf_op jit(solution)/shard_map/mate5/ppermute | solution.py:446
  313.4 33.0 %collective-permute-start.32 = (bf16[1280,512]{1,0:T(8,128)(2,1)}, bf16[1280,512]{1,0:T(8,128)(2,1)S(1)}, u32[]{:S(2)}, u32[]{:S(2)}) collective-permute-start(bf16[1280,512]{1,0:T(8,128)(2,1)} %get-tuple-element.102), channel_id=1, source_target_pairs={{8,0},{16,24},{9,1},{17,25},{10,2},{18,26},{11,3},{19,27},{12,4},{... | collective-permute-start | bytes 3932168 | tf_op jit(solution)/shard_map/sums3/ppermute | solution.py:464
  323.6 53.5 %collective-permute-start.31 = (bf16[1280,512]{1,0:T(8,128)(2,1)}, bf16[1280,512]{1,0:T(8,128)(2,1)S(1)}, u32[]{:S(2)}, u32[]{:S(2)}) collective-permute-start(bf16[1280,512]{1,0:T(8,128)(2,1)} %get-tuple-element.109), channel_id=1, source_target_pairs={{8,0},{16,24},{9,1},{17,25},{10,2},{18,26},{11,3},{19,27},{12,4},{... | collective-permute-start | bytes 3932168 | tf_op jit(solution)/shard_map/sums4/ppermute | solution.py:464
  327.4 66.7 %collective-permute-start.30 = (bf16[1280,384]{1,0:T(8,128)(2,1)}, bf16[1280,384]{1,0:T(8,128)(2,1)S(1)}, u32[]{:S(2)}, u32[]{:S(2)}) collective-permute-start(bf16[1280,384]{1,0:T(8,128)(2,1)} %products.12), channel_id=1, source_target_pairs={{8,0},{16,24},{9,1},{17,25},{10,2},{18,26},{11,3},{19,27},{12,4},{... | collective-permute-start | bytes 2949128 | tf_op jit(solution)/shard_map/sums5/ppermute | solution.py:464
  (23 other events, 161.2 us)
Sparse Core Ops, SparseCore 0:
  11.5 94.3 all-gather.4
  107.9 84.5 all-gather.6

commit v2 on v1

--- a/solution.py
+++ b/solution.py
@@ -206,13 +206,10 @@
 
     @pl.when(slots_ref[4] == 1)
     def _():
-        first = [placed(s) for s in ((0, 2, 3) if sending else (0, 1, 2, 3))]
+        first = [placed(s) for s in range(4)]
         for copy in first:
             copy.start()
         coming = [fetch(0), fetch(1)]
-        if sending:
-            outer_row = pl.multiple_of(slots_ref[1] * block, 16)
-            panels_ref[pl.ds(outer_row, block), :] = jnp.zeros((block, panels_ref.shape[1]), BF16)
         if m and keeping:
             gate_copy = pltpu.make_async_copy(
                 gate_ref.at[:, pl.ds(start, tiled(width))], gate_buf, end_sems.at[4])
@@ -243,10 +240,6 @@
                 if sending:
                     stage_ref[count:, :] = product_out(i % 3, extra).astype(BF16)
                     finished(stage_ref, out_ref)
-                if sending and keeping:
-                    outer = placed(1)
-                    outer.start()
-                    outer.wait()
                 if keeping:
                     pre = product(i % 3, extra, extra)
                     if m:
@@ -409,6 +402,8 @@
     fetched = []
     for start in range(0, half, size):
         part = lax.dynamic_slice(rows, (core * half + start, first), (min(size, half - start), used_depth(depth)))
+        column = first + lax.broadcasted_iota(jnp.int32, part.shape, 1)
+        part = jnp.where(column // (depth // 4) == lax.axis_index("dp"), jnp.zeros_like(part), part)
         fetched.append(lax.ppermute(after(part, *fetched[-1:]), "dp", TO_INNER))
     return fetched
 
@@ -490,22 +485,23 @@
     token_half = after(token_half, own[1])
     theirs = (rows_half, swap(rows_half, 1), token_half, swap(token_half, 1))
     send(1, outer[0])
-    forward(1, far[0])
+    multiply(0, far[0])
+    forward(1, out[0])
     send(2, outer[1])
-    multiply(0, outer[1])
-    forward(2, out[0])
-    panel([3, 4, 5], outer[2], mate[1])
+    panel([3], outer[1], out[0], mate[1])
     send(3)
-    multiply(1, own[3], received[0], far[2])
-    forward(3, out[1], mate[3])
-    send(4, outer[3])
-    multiply(2, outer[3])
+    forward(2, own[3])
+    multiply(1, outer[2])
+    forward(3, out[1], mate[2])
+    panel([4, 5], outer[3], received[0])
+    send(4)
     conclude(0)
+    multiply(2, own[4], mate[3])
     forward(4, out[2], far[3])
     send(5, outer[4])
     conclude(1)
     multiply(3, outer[4])
-    forward(5, out[3], far[4])
+    forward(5, out[3], mate[4])
     conclude(2)
     multiply(4, outer[5])
     conclude(3)

time: 417 us -> 410 us (0.983)
  blocking collectives: 48.3 us -> 25.2 us
  waiting for transfers between devices: 118 us -> 129 us
  Pallas kernels: 120 us -> 125 us
  starting transfers between devices: 81 us -> 76.7 us
  other arithmetic: 5.57 us -> 9.8 us
    all_to_all x1 -> x0, blocking collectives: 23.1 us -> none  [token_rows(): parts = lax.all_to_all(part, 'dp', 0, 0, tiled=True)]
    all_to_all x0 -> x1, waiting for transfers between devices: none -> 20.2 us  [token_rows(): parts = lax.all_to_all(part, 'dp', 0, 0, tiled=True)]
    ppermute x6, waiting for transfers between devices: 40.5 us -> 34.2 us  [send(): outer[k] = lax.ppermute(sent, 'dp', TO_INNER)]
    pallas_call x3 -> x4, Pallas kernels: 69.9 us -> 75.4 us  [panel_of(): pl.pallas_call(functools.partial(panel_kernel, steps, splits), out_shape=...]
    select_n x0 -> x3, other arithmetic: none -> 4.45 us  [fetch_half(): jnp.where(column // (depth // 4) == lax.axis_index('dp'), jnp.zeros_like(...]
    ppermute x6, waiting for transfers between devices: 55.9 us -> 51.5 us  [multiply(): received[k] = lax.ppermute(out[k], 'dp', TO_OUTER)]
    ppermute x6, starting transfers between devices: 41.4 us -> 37 us  [send(): outer[k] = lax.ppermute(sent, 'dp', TO_INNER)]
    unnamed x42 -> x46, local copies, waits for them, and re-layouts: 6.54 us -> 9.22 us
  transfers between devices with their start and end apart: 35 -> 36, of which waited for: 11 -> 11; matrix products, arithmetic and copies ran while one was open for 4% -> 5% of each run, Pallas kernels for 28% -> 29%
where the time goes in v2:
time: 410 us; the launch traced here: 402 us
  waiting for transfers between devices  129 us (31%)
  Pallas kernels  125 us (30%)
  starting transfers between devices  76.7 us (19%)
  blocking collectives  25.2 us (6%)
  local copies, waits for them, and re-layouts  15.7 us (4%)
  between operations  15.2 us (4%)
  other arithmetic  9.8 us (2%)
  matrix products  5.26 us (1%)
    pallas_call x4, Pallas kernels, panel_of(): pl.pallas_call(functools.partial(panel_kernel, steps, splits), out_shape=...  75.4 us
    ppermute x6, waiting for transfers between devices, multiply(): received[k] = lax.ppermute(out[k], 'dp', TO_OUTER)  51.5 us
    pallas_call x6, Pallas kernels, finish(): pl.pallas_call(functools.partial(finish_kernel, m, start, width), out_sha...  42.5 us
    ppermute x6, starting transfers between devices, send(): outer[k] = lax.ppermute(sent, 'dp', TO_INNER)  37 us
    ppermute x6, waiting for transfers between devices, send(): outer[k] = lax.ppermute(sent, 'dp', TO_INNER)  34.2 us
    all_to_all x1, waiting for transfers between devices, token_rows(): parts = lax.all_to_all(part, 'dp', 0, 0, tiled=True)  20.2 us
    ppermute x4, waiting for transfers between devices, fetch_half(): fetched.append(lax.ppermute(after(part, *fetched[-1:]), 'dp', TO_INNER))  17.2 us
    all_to_all x1, blocking collectives, token_rows(): by_rows = lax.all_to_all(tokens, 'tensor', 0, 1, tiled=True)  13.2 us
  transfers between devices with their start and end apart: 36, of which 11 were waited for; matrix products, arithmetic and copies ran while one was open for 5% of the time, Pallas kernels for 29%

profile of v2, /device:TPU:0, one launch (start us, length us, event | category | flops | bytes accessed | tf_op | source)
XLA Modules:
  0.0 401.9 jit_solution(15978123126694561118)
XLA Ops:
  7.2 4.2 %fusion.7 = (bf16[1,104,8960]{2,1,0:T(8,128)(2,1)}, bf16[1,104,8960]{2,1,0:T(8,128)(2,1)}) fusion(bf16[2,104,8960]{2,1,0:T(8,128)(2,1)} %param.6), kind=kLoop, calls=%fused_computation.31 | loop fusion | bytes 7454720 | tf_op jit(solution)/shard_map/slice | solution.py:419
  14.0 5.0 %collective-permute-start = (bf16[176,2560]{1,0:T(8,128)(2,1)S(1)}, bf16[176,2560]{1,0:T(8,128)(2,1)S(1)}, u32[]{:S(2)}, u32[]{:S(2)}) collective-permute-start(bf16[176,2560]{1,0:T(8,128)(2,1)S(1)} %get-tuple-element.121), channel_id=1, source_target_pairs={{0,8},{24,16},{1,9},{25,17},{2,10},{26,18},{3,11},{27,19},{4,12},{... | collective-permute-start | bytes 2703368 | tf_op jit(solution)/shard_map/ppermute | solution.py:407
  19.0 13.2 %all_to_all.44 = bf16[8,32,512]{2,1,0:T(8,128)(2,1)S(1)} all-to-all(bf16[8,32,512]{2,1,0:T(8,128)(2,1)S(1)} %bitcast.21), channel_id=1, replica_groups=mesh['dp'=4,'tensor'=8] {'tensor'}, dimensions={0} | all-to-all | bytes 524288 | tf_op jit(solution)/shard_map/all_to_all | solution.py:27
  32.7 12.0 %all_to_all.45 = bf16[32,4,1024]{2,0,1:T(8,128)(2,1)S(1)} all-to-all(bf16[32,4,1024]{2,0,1:T(8,128)(2,1)S(1)} %copy.31), channel_id=1, replica_groups=mesh['dp'=4,'tensor'=8] {'dp'}, dimensions={1} | all-to-all | bytes 524288 | tf_op jit(solution)/shard_map/all_to_all | solution.py:28
  44.7 5.3 %convolution_convert_fusion = bf16[128,3328]{1,0:T(8,128)(2,1)} fusion(bf16[128,1024]{1,0:T(8,128)(2,1)S(1)} %bitcast.19, bf16[1024,3328]{1,0:T(8,128)(2,1)} %rows_ref.11), kind=kOutput, calls=%fused_computation | convolution fusion | flops 872841216 | bytes 7929856 | tf_op jit(solution)/shard_map/dot_general | solution.py:30
  49.9 3.5 all-to-all-start.2
  53.4 20.2 %all-to-all-done.2 = bf16[4,32,3328]{2,1,0:T(8,128)(2,1)S(1)} async-done(((bf16[4,32,3328]{2,1,0:T(8,128)(2,1)}), bf16[4,32,3328]{2,1,0:T(8,128)(2,1)S(1)}, u32[]{:S(2)}, u32[]{:S(2)}) %all-to-all-start.2) | async-done | bytes 852000 | tf_op jit(solution)/shard_map/all_to_all | solution.py:31
  80.3 17.2 %collective-permute-done.4 = bf16[176,2560]{1,0:T(8,128)(2,1)S(1)} collective-permute-done((bf16[176,2560]{1,0:T(8,128)(2,1)S(1)}, bf16[176,2560]{1,0:T(8,128)(2,1)S(1)}, u32[]{:S(2)}, u32[]{:S(2)}) %collective-permute-start.4) | collective-permute-done | bytes 901152 | tf_op jit(solution)/shard_map/ppermute | solution.py:407
  97.6 5.3 %collective-permute-start.5 = (bf16[160,2560]{1,0:T(8,128)(2,1)}, bf16[160,2560]{1,0:T(8,128)(2,1)}, u32[]{:S(2)}, u32[]{:S(2)}) collective-permute-start(bf16[160,2560]{1,0:T(8,128)(2,1)} %fusion.2), channel_id=1, source_target_pairs={{0,8},{24,16},{1,9},{25,17},{2,10},{26,18},{3,11},{27,19},{4,12},{... | collective-permute-start | bytes 2457608 | tf_op jit(solution)/shard_map/ppermute | solution.py:407
  106.3 15.2 %panel.4.refs_6_.own_ref = bf16[832,512]{1,0:T(8,128)(2,1)} custom-call(bf16[832,8960]{1,0:T(8,128)(2,1)} %bitcast.24, bf16[1376,8960]{1,0:T(8,128)(2,1)} %growth_ref.7), custom_call_target="tpu_custom_call" | custom-call | flops 11450449920 | tf_op jit(solution)/shard_map/panel/pallas_call | solution.py:107
  121.5 4.2 %collective-permute-start.6 = (bf16[832,512]{1,0:T(8,128)(2,1)}, bf16[832,512]{1,0:T(8,128)(2,1)}, u32[]{:S(2)}, u32[]{:S(2)}) collective-permute-start(bf16[832,512]{1,0:T(8,128)(2,1)} %panel.4.refs_6_.own_ref), channel_id=1, source_target_pairs={{0,8},{24,16},{1,9},{25,17},{2,10},{26,18},{3,11},{27,19},{4,12},{... | collective-permute-start | bytes 2555912 | tf_op jit(solution)/shard_map/outer0/ppermute | solution.py:439
  126.4 4.6 %collective-permute-done.3 = bf16[128,3328]{1,0:T(8,128)(2,1)} collective-permute-done((bf16[128,3328]{1,0:T(8,128)(2,1)}, bf16[128,3328]{1,0:T(8,128)(2,1)}, u32[]{:S(2)}, u32[]{:S(2)}) %collective-permute-start.3) | collective-permute-done | bytes 852000 | tf_op jit(solution)/shard_map/ppermute | solution.py:36
  137.4 22.8 %panel.5 = (bf16[832,512]{1,0:T(8,128)(2,1)}, bf16[832,384]{1,0:T(8,128)(2,1)}) custom-call(bf16[832,8960]{1,0:T(8,128)(2,1)} %bitcast.25, bf16[1376,8960]{1,0:T(8,128)(2,1)} %growth_ref.7), custom_call_target="tpu_custom_call" | custom-call | flops 20038287360 | tf_op jit(solution)/shard_map/panel/pallas_call | solution.py:107
  169.7 14.2 %collective-permute-done.8.refs_7_ = bf16[832,512]{1,0:T(8,128)(2,1)} collective-permute-done((bf16[832,512]{1,0:T(8,128)(2,1)}, bf16[832,512]{1,0:T(8,128)(2,1)}, u32[]{:S(2)}, u32[]{:S(2)}) %collective-permute-start.8) | collective-permute-done | bytes 852000 | tf_op jit(solution)/shard_map/outer1/ppermute | solution.py:439
  185.5 15.0 %collective-permute-start.15 = (bf16[832,384]{1,0:T(8,128)(2,1)}, bf16[832,384]{1,0:T(8,128)(2,1)}, u32[]{:S(2)}, u32[]{:S(2)}) collective-permute-start(bf16[832,384]{1,0:T(8,128)(2,1)} %get-tuple-element.87.refs_6_.own_ref), channel_id=1, source_target_pairs={{0,8},{24,16},{1,9},{25,17},{2,10},{26,18},{3,11},{27,19},{4,12},{... | collective-permute-start | bytes 1916936 | tf_op jit(solution)/shard_map/outer2/ppermute | solution.py:439
  202.1 14.6 %panel.6.refs_6_.own_ref = bf16[832,512]{1,0:T(8,128)(2,1)} custom-call(bf16[832,8960]{1,0:T(8,128)(2,1)} %bitcast.22, bf16[1376,8960]{1,0:T(8,128)(2,1)} %growth_ref.7), custom_call_target="tpu_custom_call" | custom-call | flops 11450449920 | tf_op jit(solution)/shard_map/panel/pallas_call | solution.py:107
  216.7 2.4 collective-permute-start.14
  222.7 13.8 %collective-permute-done.14.refs_7_ = bf16[832,512]{1,0:T(8,128)(2,1)S(1)} collective-permute-done((bf16[832,512]{1,0:T(8,128)(2,1)}, bf16[832,512]{1,0:T(8,128)(2,1)S(1)}, u32[]{:S(2)}, u32[]{:S(2)}) %collective-permute-start.14) | collective-permute-done | bytes 852000 | tf_op jit(solution)/shard_map/outer3/ppermute | solution.py:439
  237.4 22.8 %panel.7 = (bf16[832,512]{1,0:T(8,128)(2,1)}, bf16[832,384]{1,0:T(8,128)(2,1)}) custom-call(bf16[832,8960]{1,0:T(8,128)(2,1)} %bitcast.23, bf16[1376,8960]{1,0:T(8,128)(2,1)} %growth_ref.7), custom_call_target="tpu_custom_call" | custom-call | flops 20038287360 | tf_op jit(solution)/shard_map/panel/pallas_call | solution.py:107
  260.1 6.2 %collective-permute-start.19 = (bf16[832,512]{1,0:T(8,128)(2,1)}, bf16[832,512]{1,0:T(8,128)(2,1)S(1)}, u32[]{:S(2)}, u32[]{:S(2)}) collective-permute-start(bf16[832,512]{1,0:T(8,128)(2,1)} %get-tuple-element.102.refs_6_.own_ref), channel_id=1, source_target_pairs={{0,8},{24,16},{1,9},{25,17},{2,10},{26,18},{3,11},{27,19},{4,12},{... | collective-permute-start | bytes 2555912 | tf_op jit(solution)/shard_map/outer4/ppermute | solution.py:439
  267.1 7.2 %finish.6 = (bf16[2,1376,1024]{2,1,0:T(8,128)(2,1)}, f32[256,1408]{1,0:T(8,128)}) custom-call(s32[7]{0:T(128)} %pad_add_fusion.slots_ref, bf16[1024,3328]{1,0:T(8,128)(2,1)} %rows_ref.11, bf16[256,3328]{1,0:T(8,128)(2,1)} %pad_maximum_fusion.refs_5_.tokens_ref, bf16[832,512]{1,0:T(8,128)(2,1)} %panel.4.refs_6_.own_ref, ...), custom_call_target="tpu_custom_call", output_to_operand_aliasing={{0}: (6, {}), {1}: (5, {})} | custom-call | tf_op jit(solution)/shard_map/finish/pallas_call | solution.py:365
  277.4 6.2 %collective-permute-done.19.refs_7_ = bf16[832,512]{1,0:T(8,128)(2,1)S(1)} collective-permute-done((bf16[832,512]{1,0:T(8,128)(2,1)}, bf16[832,512]{1,0:T(8,128)(2,1)S(1)}, u32[]{:S(2)}, u32[]{:S(2)}) %collective-permute-start.19) | collective-permute-done | bytes 852000 | tf_op jit(solution)/shard_map/outer4/ppermute | solution.py:439
  284.4 7.0 %collective-permute-start.23 = (bf16[832,384]{1,0:T(8,128)(2,1)S(1)}, bf16[832,384]{1,0:T(8,128)(2,1)S(1)}, u32[]{:S(2)}, u32[]{:S(2)}) collective-permute-start(bf16[832,384]{1,0:T(8,128)(2,1)S(1)} %copy-done.1), channel_id=1, source_target_pairs={{0,8},{24,16},{1,9},{25,17},{2,10},{26,18},{3,11},{27,19},{4,12},{... | collective-permute-start | bytes 1916936 | tf_op jit(solution)/shard_map/outer5/ppermute | solution.py:439
  292.5 7.2 %finish.7 = (bf16[2,1376,1024]{2,1,0:T(8,128)(2,1)}, f32[256,1408]{1,0:T(8,128)}) custom-call(s32[7]{0:T(128)} %pad_add_fusion.slots_ref, bf16[1024,3328]{1,0:T(8,128)(2,1)} %rows_ref.11, bf16[256,3328]{1,0:T(8,128)(2,1)} %pad_maximum_fusion.refs_5_.tokens_ref, ...), custom_call_target="tpu_custom_call", output_to_operand_aliasing={{0}: (6, {}), {1}: (5, {})} | custom-call | tf_op jit(solution)/shard_map/finish/pallas_call | solution.py:365
  300.7 5.6 %collective-permute-done.27.got_ref = bf16[1280,384]{1,0:T(8,128)(2,1)S(1)} collective-permute-done((bf16[1280,384]{1,0:T(8,128)(2,1)}, bf16[1280,384]{1,0:T(8,128)(2,1)S(1)}, u32[]{:S(2)}, u32[]{:S(2)}) %collective-permute-start.27) | collective-permute-done | bytes 983072 | tf_op jit(solution)/shard_map/sums2/ppermute | solution.py:459
  307.6 6.8 %finish.8 = (bf16[2,1376,1024]{2,1,0:T(8,128)(2,1)}, f32[256,1408]{1,0:T(8,128)}) custom-call(s32[7]{0:T(128)} %pad_add_fusion.slots_ref, bf16[1024,3328]{1,0:T(8,128)(2,1)} %rows_ref.11, bf16[256,3328]{1,0:T(8,128)(2,1)} %pad_maximum_fusion.refs_5_.tokens_ref, ...), custom_call_target="tpu_custom_call", output_to_operand_aliasing={{0}: (6, {}), {1}: (5, {})} | custom-call | tf_op jit(solution)/shard_map/finish/pallas_call | solution.py:365
  323.2 16.9 %collective-permute-done.32.got_ref = bf16[1280,512]{1,0:T(8,128)(2,1)S(1)} collective-permute-done((bf16[1280,512]{1,0:T(8,128)(2,1)}, bf16[1280,512]{1,0:T(8,128)(2,1)S(1)}, u32[]{:S(2)}, u32[]{:S(2)}) %collective-permute-start.32) | collective-permute-done | bytes 1310752 | tf_op jit(solution)/shard_map/sums3/ppermute | solution.py:459
  341.2 7.3 %finish.9 = (bf16[2,1376,1024]{2,1,0:T(8,128)(2,1)}, bf16[1376,256]{1,0:T(8,128)(2,1)}) custom-call(s32[7]{0:T(128)} %pad_add_fusion.slots_ref, bf16[1024,3328]{1,0:T(8,128)(2,1)} %rows_ref.11, bf16[256,3328]{1,0:T(8,128)(2,1)} %pad_maximum_fusion.refs_5_.tokens_ref, ...), custom_call_target="tpu_custom_call", output_to_operand_aliasing={{0}: (6, {}), {1}: (7, {})} | custom-call | tf_op jit(solution)/shard_map/finish/pallas_call | solution.py:365
  349.3 18.9 %collective-permute-done.31.got_ref = bf16[1280,512]{1,0:T(8,128)(2,1)S(1)} collective-permute-done((bf16[1280,512]{1,0:T(8,128)(2,1)}, bf16[1280,512]{1,0:T(8,128)(2,1)S(1)}, u32[]{:S(2)}, u32[]{:S(2)}) %collective-permute-start.31) | collective-permute-done | bytes 1310752 | tf_op jit(solution)/shard_map/sums4/ppermute | solution.py:459
  369.3 7.3 %finish.10 = (bf16[2,1376,1024]{2,1,0:T(8,128)(2,1)}, bf16[1376,256]{1,0:T(8,128)(2,1)}) custom-call(s32[7]{0:T(128)} %pad_add_fusion.slots_ref, bf16[1024,3328]{1,0:T(8,128)(2,1)} %rows_ref.11, bf16[256,3328]{1,0:T(8,128)(2,1)} %pad_maximum_fusion.refs_5_.tokens_ref, ...), custom_call_target="tpu_custom_call", output_to_operand_aliasing={{0}: (6, {}), {1}: (7, {})} | custom-call | tf_op jit(solution)/shard_map/finish/pallas_call | solution.py:365
  376.6 10.2 %collective-permute-done.30.got_ref = bf16[1280,384]{1,0:T(8,128)(2,1)S(1)} collective-permute-done((bf16[1280,384]{1,0:T(8,128)(2,1)}, bf16[1280,384]{1,0:T(8,128)(2,1)S(1)}, u32[]{:S(2)}, u32[]{:S(2)}) %collective-permute-start.30) | collective-permute-done | bytes 983072 | tf_op jit(solution)/shard_map/sums5/ppermute | solution.py:459
  387.7 6.9 %finish.11 = (bf16[2,1376,1024]{2,1,0:T(8,128)(2,1)}, bf16[1376,256]{1,0:T(8,128)(2,1)}) custom-call(s32[7]{0:T(128)} %pad_add_fusion.slots_ref, bf16[1024,3328]{1,0:T(8,128)(2,1)} %rows_ref.11, bf16[256,3328]{1,0:T(8,128)(2,1)} %pad_maximum_fusion.refs_5_.tokens_ref, ...), custom_call_target="tpu_custom_call", output_to_operand_aliasing={{0}: (6, {}), {1}: (7, {})} | custom-call | tf_op jit(solution)/shard_map/finish/pallas_call | solution.py:365
  (127 shorter events, 57.9 us)
Async XLA Ops:
  7.2 99.1 %all-gather.5.cloned.1.call-start = ((), (), s32[]{:S(2)}) async-start(), calls=%async_computation.3 | async-start | bytes 16773120 | tf_op jit(solution)/shard_map/all_gather | solution.py:419
  11.4 190.7 %all-gather.7.cloned.1.call-start = ((), (), s32[]{:S(2)}) async-start(), calls=%async_computation.4 | async-start | bytes 16773120 | tf_op jit(solution)/shard_map/all_gather | solution.py:419
  14.0 30.6 %collective-permute-start = (bf16[176,2560]{1,0:T(8,128)(2,1)S(1)}, bf16[176,2560]{1,0:T(8,128)(2,1)S(1)}, u32[]{:S(2)}, u32[]{:S(2)}) collective-permute-start(bf16[176,2560]{1,0:T(8,128)(2,1)S(1)} %get-tuple-element.121), channel_id=1, source_target_pairs={{0,8},{24,16},{1,9},{25,17},{2,10},{26,18},{3,11},{27,19},{4,12},{... | collective-permute-start | bytes 2703368 | tf_op jit(solution)/shard_map/ppermute | solution.py:407
  49.9 23.7 %all-to-all-start.2 = ((bf16[4,32,3328]{2,1,0:T(8,128)(2,1)}), bf16[4,32,3328]{2,1,0:T(8,128)(2,1)S(1)}, u32[]{:S(2)}, u32[]{:S(2)}) async-start(bf16[4,32,3328]{2,1,0:T(8,128)(2,1)} %bitcast.8), calls=%async_computation.2 | async-start | bytes 1703936 | tf_op jit(solution)/shard_map/all_to_all | solution.py:31
  76.1 21.5 %collective-permute-start.4 = (bf16[176,2560]{1,0:T(8,128)(2,1)S(1)}, bf16[176,2560]{1,0:T(8,128)(2,1)S(1)}, u32[]{:S(2)}, u32[]{:S(2)}) collective-permute-start(bf16[176,2560]{1,0:T(8,128)(2,1)S(1)} %get-tuple-element.62), channel_id=1, source_target_pairs={{0,8},{24,16},{1,9},{25,17},{2,10},{26,18},{3,11},{27,19},{4,12},{... | collective-permute-start | bytes 2703368 | tf_op jit(solution)/shard_map/ppermute | solution.py:407
  77.5 25.4 %collective-permute-start.2 = (bf16[64,3328]{1,0:T(8,128)(2,1)S(1)}, bf16[64,3328]{1,0:T(8,128)(2,1)S(1)}, u32[]{:S(2)}, u32[]{:S(2)}) collective-permute-start(bf16[64,3328]{1,0:T(8,128)(2,1)S(1)} %pad_maximum_fusion.2), channel_id=1, source_target_pairs={{0,2},{1,3},{2,0},{3,1},{4,6},{5,7},{6,4},{7,5},{8,10},{9,11},{10,... | collective-permute-start | bytes 1277960 | tf_op jit(solution)/shard_map/ppermute | solution.py:36
  97.6 28.9 %collective-permute-start.5 = (bf16[160,2560]{1,0:T(8,128)(2,1)}, bf16[160,2560]{1,0:T(8,128)(2,1)}, u32[]{:S(2)}, u32[]{:S(2)}) collective-permute-start(bf16[160,2560]{1,0:T(8,128)(2,1)} %fusion.2), channel_id=1, source_target_pairs={{0,8},{24,16},{1,9},{25,17},{2,10},{26,18},{3,11},{27,19},{4,12},{... | collective-permute-start | bytes 2457608 | tf_op jit(solution)/shard_map/ppermute | solution.py:407
  104.0 26.9 %collective-permute-start.3 = (bf16[128,3328]{1,0:T(8,128)(2,1)}, bf16[128,3328]{1,0:T(8,128)(2,1)}, u32[]{:S(2)}, u32[]{:S(2)}) collective-permute-start(bf16[128,3328]{1,0:T(8,128)(2,1)} %pad_maximum_fusion.1), channel_id=1, source_target_pairs={{0,4},{1,5},{2,6},{3,7},{4,0},{5,1},{6,2},{7,3},{8,12},{9,13},{10,... | collective-permute-start | bytes 2555912 | tf_op jit(solution)/shard_map/ppermute | solution.py:36
  121.5 38.7 %collective-permute-start.6 = (bf16[832,512]{1,0:T(8,128)(2,1)}, bf16[832,512]{1,0:T(8,128)(2,1)}, u32[]{:S(2)}, u32[]{:S(2)}) collective-permute-start(bf16[832,512]{1,0:T(8,128)(2,1)} %panel.4.refs_6_.own_ref), channel_id=1, source_target_pairs={{0,8},{24,16},{1,9},{25,17},{2,10},{26,18},{3,11},{27,19},{4,12},{... | collective-permute-start | bytes 2555912 | tf_op jit(solution)/shard_map/outer0/ppermute | solution.py:439
  125.7 34.5 %collective-permute-start.7 = (bf16[832,512]{1,0:T(8,128)(2,1)}, bf16[832,512]{1,0:T(8,128)(2,1)S(1)}, u32[]{:S(2)}, u32[]{:S(2)}) collective-permute-start(bf16[832,512]{1,0:T(8,128)(2,1)} %panel.4.refs_6_.own_ref), channel_id=1, source_target_pairs={{8,16},{16,8},{9,17},{17,9},{10,18},{18,10},{11,19},{19,11},{12,20... | collective-permute-start | bytes 2555912 | tf_op jit(solution)/shard_map/mate0/ppermute | solution.py:441
  132.2 34.9 %collective-permute-start.9 = (bf16[512,2560]{1,0:T(8,128)(2,1)S(1)}, bf16[512,2560]{1,0:T(8,128)(2,1)}, u32[]{:S(2)}, u32[]{:S(2)}) collective-permute-start(bf16[512,2560]{1,0:T(8,128)(2,1)S(1)} %constant_dynamic-update-slice_fusion.refs_0_), channel_id=1, source_target_pairs={{0,1},{1,0},{2,3},{3,2},{4,5},{5,4},{6,7},{7,6},{8,9},{9,8},{10,11... | collective-permute-start | bytes 7864328 | tf_op jit(solution)/shard_map/ppermute | solution.py:36
  136.0 25.8 %collective-permute-start.10 = (bf16[128,2560]{1,0:T(8,128)(2,1)S(1)}, bf16[128,2560]{1,0:T(8,128)(2,1)S(1)}, u32[]{:S(2)}, u32[]{:S(2)}) collective-permute-start(bf16[128,2560]{1,0:T(8,128)(2,1)S(1)} %fusion.3), channel_id=1, source_target_pairs={{0,8},{24,16},{1,9},{25,17},{2,10},{26,18},{3,11},{27,19},{4,12},{... | collective-permute-start | bytes 1966088 | tf_op jit(solution)/shard_map/ppermute | solution.py:407
  163.3 20.6 %collective-permute-start.8 = (bf16[832,512]{1,0:T(8,128)(2,1)}, bf16[832,512]{1,0:T(8,128)(2,1)}, u32[]{:S(2)}, u32[]{:S(2)}) collective-permute-start(bf16[832,512]{1,0:T(8,128)(2,1)} %get-tuple-element.79.refs_6_.own_ref), channel_id=1, source_target_pairs={{0,8},{24,16},{1,9},{25,17},{2,10},{26,18},{3,11},{27,19},{4,12},{... | collective-permute-start | bytes 2555912 | tf_op jit(solution)/shard_map/outer1/ppermute | solution.py:439
  165.5 36.6 %collective-permute-start.13 = (bf16[832,512]{1,0:T(8,128)(2,1)}, bf16[832,512]{1,0:T(8,128)(2,1)}, u32[]{:S(2)}, u32[]{:S(2)}) collective-permute-start(bf16[832,512]{1,0:T(8,128)(2,1)} %get-tuple-element.79.refs_6_.own_ref), channel_id=1, source_target_pairs={{8,16},{16,8},{9,17},{17,9},{10,18},{18,10},{11,19},{19,11},{12,20... | collective-permute-start | bytes 2555912 | tf_op jit(solution)/shard_map/mate1/ppermute | solution.py:441
  168.4 68.9 %collective-permute-start.18 = (bf16[1280,512]{1,0:T(8,128)(2,1)}, bf16[1280,512]{1,0:T(8,128)(2,1)S(1)}, u32[]{:S(2)}, u32[]{:S(2)}) collective-permute-start(bf16[1280,512]{1,0:T(8,128)(2,1)} %get-tuple-element.73), channel_id=1, source_target_pairs={{8,0},{16,24},{9,1},{17,25},{10,2},{18,26},{11,3},{19,27},{12,4},{... | collective-permute-start | bytes 3932168 | tf_op jit(solution)/shard_map/sums0/ppermute | solution.py:459
  183.9 35.9 %collective-permute-start.16 = (bf16[832,512]{1,0:T(8,128)(2,1)}, bf16[832,512]{1,0:T(8,128)(2,1)}, u32[]{:S(2)}, u32[]{:S(2)}) collective-permute-start(bf16[832,512]{1,0:T(8,128)(2,1)} %collective-permute-done.8.refs_7_), channel_id=1, source_target_pairs={{8,16},{16,8},{9,17},{17,9},{10,18},{18,10},{11,19},{19,11},{12,20... | collective-permute-start | bytes 2555912 | tf_op jit(solution)/shard_map/far1/ppermute | solution.py:446
  185.5 33.6 %collective-permute-start.15 = (bf16[832,384]{1,0:T(8,128)(2,1)}, bf16[832,384]{1,0:T(8,128)(2,1)}, u32[]{:S(2)}, u32[]{:S(2)}) collective-permute-start(bf16[832,384]{1,0:T(8,128)(2,1)} %get-tuple-element.87.refs_6_.own_ref), channel_id=1, source_target_pairs={{0,8},{24,16},{1,9},{25,17},{2,10},{26,18},{3,11},{27,19},{4,12},{... | collective-permute-start | bytes 1916936 | tf_op jit(solution)/shard_map/outer2/ppermute | solution.py:439
  200.5 20.9 %collective-permute-start.17 = (bf16[832,384]{1,0:T(8,128)(2,1)}, bf16[832,384]{1,0:T(8,128)(2,1)}, u32[]{:S(2)}, u32[]{:S(2)}) collective-permute-start(bf16[832,384]{1,0:T(8,128)(2,1)} %get-tuple-element.87.refs_6_.own_ref), channel_id=1, source_target_pairs={{8,16},{16,8},{9,17},{17,9},{10,18},{18,10},{11,19},{19,11},{12,20... | collective-permute-start | bytes 1916936 | tf_op jit(solution)/shard_map/mate2/ppermute | solution.py:441
  216.7 19.8 %collective-permute-start.14 = (bf16[832,512]{1,0:T(8,128)(2,1)}, bf16[832,512]{1,0:T(8,128)(2,1)S(1)}, u32[]{:S(2)}, u32[]{:S(2)}) collective-permute-start(bf16[832,512]{1,0:T(8,128)(2,1)} %panel.6.refs_6_.own_ref), channel_id=1, source_target_pairs={{0,8},{24,16},{1,9},{25,17},{2,10},{26,18},{3,11},{27,19},{4,12},{... | collective-permute-start | bytes 2555912 | tf_op jit(solution)/shard_map/outer3/ppermute | solution.py:439
  219.1 47.3 %collective-permute-start.20 = (bf16[832,512]{1,0:T(8,128)(2,1)}, bf16[832,512]{1,0:T(8,128)(2,1)S(1)}, u32[]{:S(2)}, u32[]{:S(2)}) collective-permute-start(bf16[832,512]{1,0:T(8,128)(2,1)} %panel.6.refs_6_.own_ref), channel_id=1, source_target_pairs={{8,16},{16,8},{9,17},{17,9},{10,18},{18,10},{11,19},{19,11},{12,20... | collective-permute-start | bytes 2555912 | tf_op jit(solution)/shard_map/mate3/ppermute | solution.py:441
  219.8 54.5 %collective-permute-start.21 = (bf16[832,384]{1,0:T(8,128)(2,1)}, bf16[832,384]{1,0:T(8,128)(2,1)S(1)}, u32[]{:S(2)}, u32[]{:S(2)}) collective-permute-start(bf16[832,384]{1,0:T(8,128)(2,1)} %collective-permute-done.15.refs_7_), channel_id=1, source_target_pairs={{8,16},{16,8},{9,17},{17,9},{10,18},{18,10},{11,19},{19,11},{12,20... | collective-permute-start | bytes 1916936 | tf_op jit(solution)/shard_map/far2/ppermute | solution.py:446
  221.4 70.0 %collective-permute-start.24 = (bf16[1280,512]{1,0:T(8,128)(2,1)}, bf16[1280,512]{1,0:T(8,128)(2,1)S(1)}, u32[]{:S(2)}, u32[]{:S(2)}) collective-permute-start(bf16[1280,512]{1,0:T(8,128)(2,1)} %get-tuple-element.82), channel_id=1, source_target_pairs={{8,0},{16,24},{9,1},{17,25},{10,2},{18,26},{11,3},{19,27},{12,4},{... | collective-permute-start | bytes 3932168 | tf_op jit(solution)/shard_map/sums1/ppermute | solution.py:459
  236.5 41.0 %collective-permute-start.22 = (bf16[832,512]{1,0:T(8,128)(2,1)S(1)}, bf16[832,512]{1,0:T(8,128)(2,1)S(1)}, u32[]{:S(2)}, u32[]{:S(2)}) collective-permute-start(bf16[832,512]{1,0:T(8,128)(2,1)S(1)} %collective-permute-done.14.refs_7_), channel_id=1, source_target_pairs={{8,16},{16,8},{9,17},{17,9},{10,18},{18,10},{11,19},{19,11},{12,20... | collective-permute-start | bytes 2555912 | tf_op jit(solution)/shard_map/far3/ppermute | solution.py:446
  260.1 23.5 %collective-permute-start.19 = (bf16[832,512]{1,0:T(8,128)(2,1)}, bf16[832,512]{1,0:T(8,128)(2,1)S(1)}, u32[]{:S(2)}, u32[]{:S(2)}) collective-permute-start(bf16[832,512]{1,0:T(8,128)(2,1)} %get-tuple-element.102.refs_6_.own_ref), channel_id=1, source_target_pairs={{0,8},{24,16},{1,9},{25,17},{2,10},{26,18},{3,11},{27,19},{4,12},{... | collective-permute-start | bytes 2555912 | tf_op jit(solution)/shard_map/outer4/ppermute | solution.py:439
  266.4 48.0 %collective-permute-start.25 = (bf16[832,512]{1,0:T(8,128)(2,1)}, bf16[832,512]{1,0:T(8,128)(2,1)S(1)}, u32[]{:S(2)}, u32[]{:S(2)}) collective-permute-start(bf16[832,512]{1,0:T(8,128)(2,1)} %get-tuple-element.102.refs_6_.own_ref), channel_id=1, source_target_pairs={{8,16},{16,8},{9,17},{17,9},{10,18},{18,10},{11,19},{19,11},{12,20... | collective-permute-start | bytes 2555912 | tf_op jit(solution)/shard_map/mate4/ppermute | solution.py:441
  276.1 30.2 %collective-permute-start.27 = (bf16[1280,384]{1,0:T(8,128)(2,1)}, bf16[1280,384]{1,0:T(8,128)(2,1)S(1)}, u32[]{:S(2)}, u32[]{:S(2)}) collective-permute-start(bf16[1280,384]{1,0:T(8,128)(2,1)} %get-tuple-element.92), channel_id=1, source_target_pairs={{8,0},{16,24},{9,1},{17,25},{10,2},{18,26},{11,3},{19,27},{12,4},{... | collective-permute-start | bytes 2949128 | tf_op jit(solution)/shard_map/sums2/ppermute | solution.py:459
  283.7 32.4 %collective-permute-start.26 = (bf16[832,512]{1,0:T(8,128)(2,1)S(1)}, bf16[832,512]{1,0:T(8,128)(2,1)S(1)}, u32[]{:S(2)}, u32[]{:S(2)}) collective-permute-start(bf16[832,512]{1,0:T(8,128)(2,1)S(1)} %collective-permute-done.19.refs_7_), channel_id=1, source_target_pairs={{8,16},{16,8},{9,17},{17,9},{10,18},{18,10},{11,19},{19,11},{12,20... | collective-permute-start | bytes 2555912 | tf_op jit(solution)/shard_map/far4/ppermute | solution.py:446
  284.4 30.9 %collective-permute-start.23 = (bf16[832,384]{1,0:T(8,128)(2,1)S(1)}, bf16[832,384]{1,0:T(8,128)(2,1)S(1)}, u32[]{:S(2)}, u32[]{:S(2)}) collective-permute-start(bf16[832,384]{1,0:T(8,128)(2,1)S(1)} %copy-done.1), channel_id=1, source_target_pairs={{0,8},{24,16},{1,9},{25,17},{2,10},{26,18},{3,11},{27,19},{4,12},{... | collective-permute-start | bytes 1916936 | tf_op jit(solution)/shard_map/outer5/ppermute | solution.py:439
  291.4 27.7 %collective-permute-start.28 = (bf16[832,384]{1,0:T(8,128)(2,1)S(1)}, bf16[832,384]{1,0:T(8,128)(2,1)S(1)}, u32[]{:S(2)}, u32[]{:S(2)}) collective-permute-start(bf16[832,384]{1,0:T(8,128)(2,1)S(1)} %copy-done.1), channel_id=1, source_target_pairs={{8,16},{16,8},{9,17},{17,9},{10,18},{18,10},{11,19},{19,11},{12,20... | collective-permute-start | bytes 1916936 | tf_op jit(solution)/shard_map/mate5/ppermute | solution.py:441
  306.3 33.8 %collective-permute-start.32 = (bf16[1280,512]{1,0:T(8,128)(2,1)}, bf16[1280,512]{1,0:T(8,128)(2,1)S(1)}, u32[]{:S(2)}, u32[]{:S(2)}) collective-permute-start(bf16[1280,512]{1,0:T(8,128)(2,1)} %get-tuple-element.100), channel_id=1, source_target_pairs={{8,0},{16,24},{9,1},{17,25},{10,2},{18,26},{11,3},{19,27},{12,4},{... | collective-permute-start | bytes 3932168 | tf_op jit(solution)/shard_map/sums3/ppermute | solution.py:459
  317.8 50.4 %collective-permute-start.31 = (bf16[1280,512]{1,0:T(8,128)(2,1)}, bf16[1280,512]{1,0:T(8,128)(2,1)S(1)}, u32[]{:S(2)}, u32[]{:S(2)}) collective-permute-start(bf16[1280,512]{1,0:T(8,128)(2,1)} %get-tuple-element.107), channel_id=1, source_target_pairs={{8,0},{16,24},{9,1},{17,25},{10,2},{18,26},{11,3},{19,27},{12,4},{... | collective-permute-start | bytes 3932168 | tf_op jit(solution)/shard_map/sums4/ppermute | solution.py:459
  321.9 64.8 %collective-permute-start.30 = (bf16[1280,384]{1,0:T(8,128)(2,1)}, bf16[1280,384]{1,0:T(8,128)(2,1)S(1)}, u32[]{:S(2)}, u32[]{:S(2)}) collective-permute-start(bf16[1280,384]{1,0:T(8,128)(2,1)} %products.12), channel_id=1, source_target_pairs={{8,0},{16,24},{9,1},{17,25},{10,2},{18,26},{11,3},{19,27},{12,4},{... | collective-permute-start | bytes 2949128 | tf_op jit(solution)/shard_map/sums5/ppermute | solution.py:459
  (26 other events, 141.0 us)
Sparse Core Ops, SparseCore 0:
  11.5 94.6 all-gather.4
  108.1 85.9 all-gather.6

commit v3 on v2

--- a/solution.py
+++ b/solution.py
@@ -305,40 +305,98 @@
     )(slots, *args)
 
 
-def finish_kernel(m, start, width, slots_ref, rows_ref, tokens_ref, own_ref, got_ref, gate_ref, *refs):
-    grown_ref, last_ref = refs[2 if m else 1:][:2]
-    factors_ref, panels_ref, got_buf, gate_buf, slab_ref, extra_ref, sems = refs[2 if m else 1:][2:]
+def own_kernel(slots_ref, rows_ref, tokens_ref, own_ref, sums_ref, factors_ref, panels_ref, sums_buf, sems):
     block = own_ref.shape[0]
-    count = rows_ref.shape[0]
-    wide = panels_ref.shape[1]
-    half = count // 2
-    depth = factors_ref.shape[1]
 
     @pl.when(slots_ref[4] == 0)
     def _():
-        side = pl.multiple_of(slots_ref[5] * depth, 128)
-        place = pl.multiple_of(slots_ref[5] * block, 16)
+        copies = own_copies(slots_ref, rows_ref, tokens_ref, own_ref, factors_ref, panels_ref, sems)
+        for copy in copies:
+            copy.start()
         other = pl.multiple_of((1 - slots_ref[5]) * block, 16)
-        copies = [
-            pltpu.make_async_copy(own_ref, panels_ref.at[pl.ds(place, block), :], sems.at[0]),
-            pltpu.make_async_copy(
-                tokens_ref.at[:, pl.ds(side, depth)], factors_ref.at[pl.ds(count, tokens_ref.shape[0]), :], sems.at[1]),
-            pltpu.make_async_copy(rows_ref.at[:, pl.ds(side, depth)], factors_ref.at[pl.ds(0, count), :], sems.at[2]),
-            pltpu.make_async_copy(got_ref, got_buf, sems.at[3]),
-        ]
+        panels_ref[pl.ds(other, block), :] = jnp.zeros((block, panels_ref.shape[1]), BF16)
+        for copy in copies:
+            copy.wait()
+        sums_buf[...] = jnp.dot(factors_ref[...], panels_ref[...], preferred_element_type=F32)
+        end = pltpu.make_async_copy(sums_buf, sums_ref, sems.at[0])
+        end.start()
+        end.wait()
+
+
+def own_copies(slots_ref, rows_ref, tokens_ref, own_ref, factors_ref, panels_ref, sems):
+    block, count, depth = own_ref.shape[0], rows_ref.shape[0], factors_ref.shape[1]
+    side = pl.multiple_of(slots_ref[5] * depth, 128)
+    place = pl.multiple_of(slots_ref[5] * block, 16)
+    return [
+        pltpu.make_async_copy(own_ref, panels_ref.at[pl.ds(place, block), :], sems.at[0]),
+        pltpu.make_async_copy(
+            tokens_ref.at[:, pl.ds(side, depth)], factors_ref.at[pl.ds(count, tokens_ref.shape[0]), :], sems.at[1]),
+        pltpu.make_async_copy(rows_ref.at[:, pl.ds(side, depth)], factors_ref.at[pl.ds(0, count), :], sems.at[2]),
+    ]
+
+
+def own_product(slots, mine, own):
+    rows, token_growth = mine
+    total, (block, wide) = rows.shape[0] + token_growth.shape[0], own.shape
+    return pl.pallas_call(
+        own_kernel,
+        out_shape=jax.ShapeDtypeStruct((total, wide), F32),
+        grid_spec=pltpu.PrefetchScalarGridSpec(
+            num_scalar_prefetch=1,
+            grid=(1,),
+            in_specs=[ANY] * 3,
+            out_specs=ANY,
+            scratch_shapes=[
+                pltpu.VMEM((total, 2 * block), BF16),
+                pltpu.VMEM((2 * block, wide), BF16),
+                pltpu.VMEM((total, wide), F32),
+                pltpu.SemaphoreType.DMA((3,)),
+            ],
+        ),
+        compiler_params=pltpu.CompilerParams(vmem_limit_bytes=VMEM_LIMIT),
+        cost_estimate=pl.CostEstimate(flops=0, bytes_accessed=0, transcendentals=0),
+        name="own_product",
+    )(slots, rows, token_growth, own)
+
+
+def finish_kernel(m, start, width, made, slots_ref, *refs):
+    refs = list(refs)
+    sources = [refs.pop(0) for _ in range(1 if made else 3)]
+    got_ref, gate_ref = refs.pop(0), refs.pop(0)
+    del refs[:2 if m else 1]
+    grown_ref, last_ref = refs.pop(0), refs.pop(0)
+    bufs = [refs.pop(0) for _ in range(1 if made else 2)]
+    got_buf, gate_buf, slab_ref, extra_ref, sems = refs
+    wide = got_ref.shape[1]
+    count, extra = slab_ref.shape[1], gate_buf.shape[0]
+    half = count // 2
+
+    @pl.when(slots_ref[4] == 0)
+    def _():
+        if made:
+            copies = [pltpu.make_async_copy(sources[0], bufs[0], sems.at[0])]
+        else:
+            copies = own_copies(slots_ref, *sources, *bufs, sems)
+        copies.append(pltpu.make_async_copy(got_ref, got_buf, sems.at[3]))
         if m:
             copies.append(pltpu.make_async_copy(gate_ref.at[:, pl.ds(start, tiled(width))], gate_buf, sems.at[4]))
         for copy in copies:
             copy.start()
-        panels_ref[pl.ds(other, block), :] = jnp.zeros((block, wide), BF16)
+        if not made:
+            block = sources[2].shape[0]
+            other = pl.multiple_of((1 - slots_ref[5]) * block, 16)
+            bufs[1][pl.ds(other, block), :] = jnp.zeros((block, wide), BF16)
         for copy in copies:
             copy.wait()
 
         def product(first, size):
-            sums = jnp.dot(factors_ref[first:first + size, :], panels_ref[...], preferred_element_type=F32)
+            if made:
+                sums = bufs[0][first:first + size, :]
+            else:
+                sums = jnp.dot(bufs[0][first:first + size, :], bufs[1][...], preferred_element_type=F32)
             return sums + got_buf[first:first + size, :].astype(F32)
 
-        pre = product(count, tokens_ref.shape[0])
+        pre = product(count, extra)
         if m:
             extra_ref[...] = gated(gate_buf[...], pre).T
             end = pltpu.make_async_copy(
@@ -356,14 +414,20 @@
         slab.wait()
 
 
-def finish(m, start, width, slots, mine, own, got, gate, grown, hidden, columns):
+def finish(m, start, width, slots, mine, own, got, gate, grown, hidden, columns, made=None):
     rows, token_growth = mine
     count, depth = rows.shape
     extra = token_growth.shape[0]
     block, wide = own.shape
-    args = [rows, token_growth, own, got, gate, grown] + ([hidden] if m else [])
+    args = [rows, token_growth, own] if made is None else [made]
+    args += [got, gate, grown] + ([hidden] if m else [])
+    last = len(args)
+    if made is None:
+        scratch = [pltpu.VMEM((count + extra, 2 * block), BF16), pltpu.VMEM((2 * block, wide), BF16)]
+    else:
+        scratch = [pltpu.VMEM((count + extra, wide), F32)]
     return pl.pallas_call(
-        functools.partial(finish_kernel, m, start, width),
+        functools.partial(finish_kernel, m, start, width, made is not None),
         out_shape=(
             jax.ShapeDtypeStruct((2, columns, count), BF16),
             jax.ShapeDtypeStruct((columns, extra), BF16) if m else jax.ShapeDtypeStruct((extra, tiled(columns)), F32),
@@ -373,9 +437,7 @@
             grid=(1,),
             in_specs=[ANY] * len(args),
             out_specs=(ANY, ANY),
-            scratch_shapes=[
-                pltpu.VMEM((count + extra, 2 * block), BF16),
-                pltpu.VMEM((2 * block, wide), BF16),
+            scratch_shapes=scratch + [
                 pltpu.VMEM((count + extra, wide), BF16),
                 pltpu.VMEM((extra, wide), F32),
                 pltpu.VMEM((wide, count), BF16),
@@ -383,7 +445,7 @@
                 pltpu.SemaphoreType.DMA((5,)),
             ],
         ),
-        input_output_aliases={6: 0, 7: 1} if m else {6: 0, 5: 1},
+        input_output_aliases={last - 1: 0, last: 1} if m else {last: 0, last - 1: 1},
         compiler_params=pltpu.CompilerParams(vmem_limit_bytes=VMEM_LIMIT),
         cost_estimate=pl.CostEstimate(flops=0, bytes_accessed=0, transcendentals=0),
         name="finish",
@@ -464,11 +526,10 @@
             else:
                 gate = made[-1]
 
-    def conclude(k, *made):
+    def conclude(k, made=None):
         nonlocal grown, gate, hidden
         m, start, width = work[k]
-        got = after(received[k], *made) if made else received[k]
-        grown, last = finish(m, start, width, slots, mine, own[k], got, gate, grown, hidden, columns)
+        grown, last = finish(m, start, width, slots, mine, own[k], received[k], gate, grown, hidden, columns, made)
         if m:
             hidden = last
         else:
@@ -480,12 +541,13 @@
     mine = (width_growth, token_growth)
     rows_half = jnp.concatenate(fetched[:2] + [after(fetched[2], own[0])], axis=0)
     send(0)
-    panel([1, 2], own[0], token_growth, rows_half)
+    panel([1], own[0], token_growth, rows_half)
     forward(0, mate[0], own[1])
     token_half = after(token_half, own[1])
     theirs = (rows_half, swap(rows_half, 1), token_half, swap(token_half, 1))
     send(1, outer[0])
-    multiply(0, far[0])
+    panel([2], outer[0])
+    multiply(0, far[0], own[2])
     forward(1, out[0])
     send(2, outer[1])
     panel([3], outer[1], out[0], mate[1])
@@ -507,8 +569,9 @@
     conclude(3)
     multiply(5, out[4], keeping=False)
     multiply(5, out[5], sending=False)
+    last_product = own_product(slots, mine, after(own[5], out[5]))
     conclude(4)
-    conclude(5)
+    conclude(5, last_product)
     return jnp.swapaxes(grown, 1, 2), hidden.T
 
 

time: 410 us -> 411 us (level)
  waiting for transfers between devices: 129 us -> 113 us
  Pallas kernels: 125 us -> 135 us
  starting transfers between devices: 76.7 us -> 81.8 us
    ppermute x6, waiting for transfers between devices: 34.2 us -> 22.5 us  [send(): outer[k] = lax.ppermute(sent, 'dp', TO_INNER)]
    pallas_call x4 -> x5, Pallas kernels: 75.4 us -> 81.6 us  [panel_of(): pl.pallas_call(functools.partial(panel_kernel, steps, splits), out_shape=...]
    ppermute x6, waiting for transfers between devices: 51.5 us -> 45.4 us  [multiply(): received[k] = lax.ppermute(out[k], 'dp', TO_OUTER)]
    ppermute x6, starting transfers between devices: 37 us -> 41.3 us  [send(): outer[k] = lax.ppermute(sent, 'dp', TO_INNER)]
    pallas_call x6 -> x7, Pallas kernels: 42.5 us -> 46.3 us  [the longest x6 39.5 us: finish(): pl.pallas_call(functools.partial(finish_kernel, m, start, width, made is...]
    unnamed x46 -> x48, local copies, waits for them, and re-layouts: 9.22 us -> 11.5 us
  transfers between devices with their start and end apart: 36 -> 36, of which waited for: 11 -> 10; matrix products, arithmetic and copies ran while one was open for 5% -> 5% of each run, Pallas kernels for 29% -> 33%
where the time goes in v3:
time: 411 us; the launch traced here: 403 us
  Pallas kernels  135 us (33%)
  waiting for transfers between devices  113 us (27%)
  starting transfers between devices  81.8 us (20%)
  blocking collectives  25.2 us (6%)
  local copies, waits for them, and re-layouts  17.9 us (4%)
  between operations  15.2 us (4%)
  other arithmetic  9.8 us (2%)
  matrix products  5.26 us (1%)
    pallas_call x5, Pallas kernels, panel_of(): pl.pallas_call(functools.partial(panel_kernel, steps, splits), out_shape=...  81.6 us
    ppermute x6, waiting for transfers between devices, multiply(): received[k] = lax.ppermute(out[k], 'dp', TO_OUTER)  45.4 us
    ppermute x6, starting transfers between devices, send(): outer[k] = lax.ppermute(sent, 'dp', TO_INNER)  41.3 us
    pallas_call x6, Pallas kernels, finish(): pl.pallas_call(functools.partial(finish_kernel, m, start, width, made is...  39.5 us
    ppermute x6, waiting for transfers between devices, send(): outer[k] = lax.ppermute(sent, 'dp', TO_INNER)  22.5 us
    all_to_all x1, waiting for transfers between devices, token_rows(): parts = lax.all_to_all(part, 'dp', 0, 0, tiled=True)  20.2 us
    ppermute x4, waiting for transfers between devices, fetch_half(): fetched.append(lax.ppermute(after(part, *fetched[-1:]), 'dp', TO_INNER))  18.8 us
    all_to_all x1, blocking collectives, token_rows(): by_rows = lax.all_to_all(tokens, 'tensor', 0, 1, tiled=True)  13.2 us
  transfers between devices with their start and end apart: 36, of which 10 were waited for; matrix products, arithmetic and copies ran while one was open for 5% of the time, Pallas kernels for 33%

profile of v3, /device:TPU:0, one launch (start us, length us, event | category | flops | bytes accessed | tf_op | source)
XLA Modules:
  0.0 402.7 jit_solution(1889224774956182523)
XLA Ops:
  7.2 4.2 %fusion.7 = (bf16[1,104,8960]{2,1,0:T(8,128)(2,1)}, bf16[1,104,8960]{2,1,0:T(8,128)(2,1)}) fusion(bf16[2,104,8960]{2,1,0:T(8,128)(2,1)} %param.6), kind=kLoop, calls=%fused_computation.31 | loop fusion | bytes 7454720 | tf_op jit(solution)/shard_map/slice | solution.py:481
  14.0 5.0 %collective-permute-start = (bf16[176,2560]{1,0:T(8,128)(2,1)S(1)}, bf16[176,2560]{1,0:T(8,128)(2,1)S(1)}, u32[]{:S(2)}, u32[]{:S(2)}) collective-permute-start(bf16[176,2560]{1,0:T(8,128)(2,1)S(1)} %get-tuple-element.119), channel_id=1, source_target_pairs={{0,8},{24,16},{1,9},{25,17},{2,10},{26,18},{3,11},{27,19},{4,12},{... | collective-permute-start | bytes 2703368 | tf_op jit(solution)/shard_map/ppermute | solution.py:469
  19.0 13.2 %all_to_all.44 = bf16[8,32,512]{2,1,0:T(8,128)(2,1)S(1)} all-to-all(bf16[8,32,512]{2,1,0:T(8,128)(2,1)S(1)} %bitcast.24), channel_id=1, replica_groups=mesh['dp'=4,'tensor'=8] {'tensor'}, dimensions={0} | all-to-all | bytes 524288 | tf_op jit(solution)/shard_map/all_to_all | solution.py:27
  32.7 12.0 %all_to_all.45 = bf16[32,4,1024]{2,0,1:T(8,128)(2,1)S(1)} all-to-all(bf16[32,4,1024]{2,0,1:T(8,128)(2,1)S(1)} %copy.31), channel_id=1, replica_groups=mesh['dp'=4,'tensor'=8] {'dp'}, dimensions={1} | all-to-all | bytes 524288 | tf_op jit(solution)/shard_map/all_to_all | solution.py:28
  44.7 5.3 %convolution_convert_fusion = bf16[128,3328]{1,0:T(8,128)(2,1)} fusion(bf16[128,1024]{1,0:T(8,128)(2,1)S(1)} %bitcast.22, bf16[1024,3328]{1,0:T(8,128)(2,1)} %refs_0_.9), kind=kOutput, calls=%fused_computation | convolution fusion | flops 872841216 | bytes 7929856 | tf_op jit(solution)/shard_map/dot_general | solution.py:30
  53.4 20.2 %all-to-all-done.2 = bf16[4,32,3328]{2,1,0:T(8,128)(2,1)S(1)} async-done(((bf16[4,32,3328]{2,1,0:T(8,128)(2,1)}), bf16[4,32,3328]{2,1,0:T(8,128)(2,1)S(1)}, u32[]{:S(2)}, u32[]{:S(2)}) %all-to-all-start.2) | async-done | bytes 852000 | tf_op jit(solution)/shard_map/all_to_all | solution.py:31
  81.0 17.2 %collective-permute-done.4 = bf16[176,2560]{1,0:T(8,128)(2,1)S(1)} collective-permute-done((bf16[176,2560]{1,0:T(8,128)(2,1)S(1)}, bf16[176,2560]{1,0:T(8,128)(2,1)S(1)}, u32[]{:S(2)}, u32[]{:S(2)}) %collective-permute-start.4) | collective-permute-done | bytes 901152 | tf_op jit(solution)/shard_map/ppermute | solution.py:469
  98.2 5.3 %collective-permute-start.5 = (bf16[160,2560]{1,0:T(8,128)(2,1)}, bf16[160,2560]{1,0:T(8,128)(2,1)}, u32[]{:S(2)}, u32[]{:S(2)}) collective-permute-start(bf16[160,2560]{1,0:T(8,128)(2,1)} %fusion.2), channel_id=1, source_target_pairs={{0,8},{24,16},{1,9},{25,17},{2,10},{26,18},{3,11},{27,19},{4,12},{... | collective-permute-start | bytes 2457608 | tf_op jit(solution)/shard_map/ppermute | solution.py:469
  106.3 15.3 %panel.5.refs_6_.refs_2_ = bf16[832,512]{1,0:T(8,128)(2,1)} custom-call(bf16[832,8960]{1,0:T(8,128)(2,1)} %bitcast.18, bf16[1376,8960]{1,0:T(8,128)(2,1)} %growth_ref.9), custom_call_target="tpu_custom_call" | custom-call | flops 11450449920 | tf_op jit(solution)/shard_map/panel/pallas_call | solution.py:107
  121.5 4.2 %collective-permute-start.6 = (bf16[832,512]{1,0:T(8,128)(2,1)}, bf16[832,512]{1,0:T(8,128)(2,1)}, u32[]{:S(2)}, u32[]{:S(2)}) collective-permute-start(bf16[832,512]{1,0:T(8,128)(2,1)} %panel.5.refs_6_.refs_2_), channel_id=1, source_target_pairs={{0,8},{24,16},{1,9},{25,17},{2,10},{26,18},{3,11},{27,19},{4,12},{... | collective-permute-start | bytes 2555912 | tf_op jit(solution)/shard_map/outer0/ppermute | solution.py:501
  127.3 5.0 %collective-permute-done.3 = bf16[128,3328]{1,0:T(8,128)(2,1)} collective-permute-done((bf16[128,3328]{1,0:T(8,128)(2,1)}, bf16[128,3328]{1,0:T(8,128)(2,1)}, u32[]{:S(2)}, u32[]{:S(2)}) %collective-permute-start.3) | collective-permute-done | bytes 852000 | tf_op jit(solution)/shard_map/ppermute | solution.py:36
  138.7 15.1 %panel.6.refs_6_.refs_2_ = bf16[832,512]{1,0:T(8,128)(2,1)} custom-call(bf16[832,8960]{1,0:T(8,128)(2,1)} %bitcast.19, bf16[1376,8960]{1,0:T(8,128)(2,1)} %growth_ref.9), custom_call_target="tpu_custom_call" | custom-call | flops 11450449920 | tf_op jit(solution)/shard_map/panel/pallas_call | solution.py:107
  157.6 5.3 %collective-permute-start.8 = (bf16[832,512]{1,0:T(8,128)(2,1)}, bf16[832,512]{1,0:T(8,128)(2,1)}, u32[]{:S(2)}, u32[]{:S(2)}) collective-permute-start(bf16[832,512]{1,0:T(8,128)(2,1)} %panel.6.refs_6_.refs_2_), channel_id=1, source_target_pairs={{0,8},{24,16},{1,9},{25,17},{2,10},{26,18},{3,11},{27,19},{4,12},{... | collective-permute-start | bytes 2555912 | tf_op jit(solution)/shard_map/outer1/ppermute | solution.py:501
  164.5 13.9 %panel.7.refs_6_.refs_2_ = bf16[832,384]{1,0:T(8,128)(2,1)} custom-call(bf16[832,8960]{1,0:T(8,128)(2,1)} %bitcast.20, bf16[1376,8960]{1,0:T(8,128)(2,1)} %growth_ref.9), custom_call_target="tpu_custom_call" | custom-call | flops 8587837440 | tf_op jit(solution)/shard_map/panel/pallas_call | solution.py:107
  185.0 16.8 %collective-permute-start.15 = (bf16[832,384]{1,0:T(8,128)(2,1)}, bf16[832,384]{1,0:T(8,128)(2,1)}, u32[]{:S(2)}, u32[]{:S(2)}) collective-permute-start(bf16[832,384]{1,0:T(8,128)(2,1)} %panel.7.refs_6_.refs_2_), channel_id=1, source_target_pairs={{0,8},{24,16},{1,9},{25,17},{2,10},{26,18},{3,11},{27,19},{4,12},{... | collective-permute-start | bytes 1916936 | tf_op jit(solution)/shard_map/outer2/ppermute | solution.py:501
  203.3 14.7 %panel.8.refs_6_.refs_2_ = bf16[832,512]{1,0:T(8,128)(2,1)} custom-call(bf16[832,8960]{1,0:T(8,128)(2,1)} %bitcast.25, bf16[1376,8960]{1,0:T(8,128)(2,1)} %growth_ref.9), custom_call_target="tpu_custom_call" | custom-call | flops 11450449920 | tf_op jit(solution)/shard_map/panel/pallas_call | solution.py:107
  223.9 15.4 %collective-permute-done.14.refs_7_ = bf16[832,512]{1,0:T(8,128)(2,1)S(1)} collective-permute-done((bf16[832,512]{1,0:T(8,128)(2,1)}, bf16[832,512]{1,0:T(8,128)(2,1)S(1)}, u32[]{:S(2)}, u32[]{:S(2)}) %collective-permute-start.14) | collective-permute-done | bytes 852000 | tf_op jit(solution)/shard_map/outer3/ppermute | solution.py:501
  240.2 22.7 %panel.9 = (bf16[832,512]{1,0:T(8,128)(2,1)}, bf16[832,384]{1,0:T(8,128)(2,1)}) custom-call(bf16[832,8960]{1,0:T(8,128)(2,1)} %bitcast.26, bf16[1376,8960]{1,0:T(8,128)(2,1)} %growth_ref.9), custom_call_target="tpu_custom_call" | custom-call | flops 20038287360 | tf_op jit(solution)/shard_map/panel/pallas_call | solution.py:107
  262.8 6.6 %collective-permute-start.19 = (bf16[832,512]{1,0:T(8,128)(2,1)}, bf16[832,512]{1,0:T(8,128)(2,1)S(1)}, u32[]{:S(2)}, u32[]{:S(2)}) collective-permute-start(bf16[832,512]{1,0:T(8,128)(2,1)} %get-tuple-element.100.refs_6_.refs_2_), channel_id=1, source_target_pairs={{0,8},{24,16},{1,9},{25,17},{2,10},{26,18},{3,11},{27,19},{4,12},{... | collective-permute-start | bytes 2555912 | tf_op jit(solution)/shard_map/outer4/ppermute | solution.py:501
  270.1 7.2 %finish.6 = (bf16[2,1376,1024]{2,1,0:T(8,128)(2,1)}, f32[256,1408]{1,0:T(8,128)}) custom-call(s32[7]{0:T(128)} %pad_add_fusion.slots_ref, bf16[1024,3328]{1,0:T(8,128)(2,1)} %refs_0_.9, bf16[256,3328]{1,0:T(8,128)(2,1)} %pad_maximum_fusion.refs_5_.refs_1_.tokens_ref, ...), custom_call_target="tpu_custom_call", output_to_operand_aliasing={{0}: (6, {}), {1}: (5, {})} | custom-call | tf_op jit(solution)/shard_map/finish/pallas_call | solution.py:429
  280.5 7.1 %collective-permute-done.19.refs_7_ = bf16[832,512]{1,0:T(8,128)(2,1)S(1)} collective-permute-done((bf16[832,512]{1,0:T(8,128)(2,1)}, bf16[832,512]{1,0:T(8,128)(2,1)S(1)}, u32[]{:S(2)}, u32[]{:S(2)}) %collective-permute-start.19) | collective-permute-done | bytes 852000 | tf_op jit(solution)/shard_map/outer4/ppermute | solution.py:501
  288.3 6.2 %collective-permute-start.23 = (bf16[832,384]{1,0:T(8,128)(2,1)S(1)}, bf16[832,384]{1,0:T(8,128)(2,1)S(1)}, u32[]{:S(2)}, u32[]{:S(2)}) collective-permute-start(bf16[832,384]{1,0:T(8,128)(2,1)S(1)} %copy-done.2), channel_id=1, source_target_pairs={{0,8},{24,16},{1,9},{25,17},{2,10},{26,18},{3,11},{27,19},{4,12},{... | collective-permute-start | bytes 1916936 | tf_op jit(solution)/shard_map/outer5/ppermute | solution.py:501
  295.6 7.2 %finish.7 = (bf16[2,1376,1024]{2,1,0:T(8,128)(2,1)}, f32[256,1408]{1,0:T(8,128)}) custom-call(s32[7]{0:T(128)} %pad_add_fusion.slots_ref, bf16[1024,3328]{1,0:T(8,128)(2,1)} %refs_0_.9, bf16[256,3328]{1,0:T(8,128)(2,1)} %pad_maximum_fusion.refs_5_.refs_1_.tokens_ref, ...), custom_call_target="tpu_custom_call", output_to_operand_aliasing={{0}: (6, {}), {1}: (5, {})} | custom-call | tf_op jit(solution)/shard_map/finish/pallas_call | solution.py:429
  303.8 5.6 %collective-permute-done.27.refs_3_ = bf16[1280,384]{1,0:T(8,128)(2,1)S(1)} collective-permute-done((bf16[1280,384]{1,0:T(8,128)(2,1)}, bf16[1280,384]{1,0:T(8,128)(2,1)S(1)}, u32[]{:S(2)}, u32[]{:S(2)}) %collective-permute-start.27) | collective-permute-done | bytes 983072 | tf_op jit(solution)/shard_map/sums2/ppermute | solution.py:521
  310.7 6.8 %finish.8 = (bf16[2,1376,1024]{2,1,0:T(8,128)(2,1)}, f32[256,1408]{1,0:T(8,128)}) custom-call(s32[7]{0:T(128)} %pad_add_fusion.slots_ref, bf16[1024,3328]{1,0:T(8,128)(2,1)} %refs_0_.9, bf16[256,3328]{1,0:T(8,128)(2,1)} %pad_maximum_fusion.refs_5_.refs_1_.tokens_ref, ...), custom_call_target="tpu_custom_call", output_to_operand_aliasing={{0}: (6, {}), {1}: (5, {})} | custom-call | tf_op jit(solution)/shard_map/finish/pallas_call | solution.py:429
  326.3 6.9 %own_product.1.refs_0_ = f32[1280,384]{1,0:T(8,128)} custom-call(s32[7]{0:T(128)} %pad_add_fusion.slots_ref, bf16[1024,3328]{1,0:T(8,128)(2,1)} %refs_0_.9, bf16[256,3328]{1,0:T(8,128)(2,1)} %pad_maximum_fusion.refs_5_.refs_1_.tokens_ref, bf16[832,384]{1,0:T(8,128)(2,1)} %get-tuple-element.107.refs_6_.own_ref), custom_call_target="tpu_custom_call" | custom-call | tf_op jit(solution)/shard_map/own_product/pallas_call | solution.py:341
  333.2 10.1 %collective-permute-done.32.refs_3_ = bf16[1280,512]{1,0:T(8,128)(2,1)S(1)} collective-permute-done((bf16[1280,512]{1,0:T(8,128)(2,1)}, bf16[1280,512]{1,0:T(8,128)(2,1)S(1)}, u32[]{:S(2)}, u32[]{:S(2)}) %collective-permute-start.32) | collective-permute-done | bytes 1310752 | tf_op jit(solution)/shard_map/sums3/ppermute | solution.py:521
  344.3 7.3 %finish.9 = (bf16[2,1376,1024]{2,1,0:T(8,128)(2,1)}, bf16[1376,256]{1,0:T(8,128)(2,1)}) custom-call(s32[7]{0:T(128)} %pad_add_fusion.slots_ref, bf16[1024,3328]{1,0:T(8,128)(2,1)} %refs_0_.9, bf16[256,3328]{1,0:T(8,128)(2,1)} %pad_maximum_fusion.refs_5_.refs_1_.tokens_ref, ...), custom_call_target="tpu_custom_call", output_to_operand_aliasing={{0}: (6, {}), {1}: (7, {})} | custom-call | tf_op jit(solution)/shard_map/finish/pallas_call | solution.py:429
  352.5 18.9 %collective-permute-done.31.refs_3_ = bf16[1280,512]{1,0:T(8,128)(2,1)S(1)} collective-permute-done((bf16[1280,512]{1,0:T(8,128)(2,1)}, bf16[1280,512]{1,0:T(8,128)(2,1)S(1)}, u32[]{:S(2)}, u32[]{:S(2)}) %collective-permute-start.31) | collective-permute-done | bytes 1310752 | tf_op jit(solution)/shard_map/sums4/ppermute | solution.py:521
  372.4 7.3 %finish.10 = (bf16[2,1376,1024]{2,1,0:T(8,128)(2,1)}, bf16[1376,256]{1,0:T(8,128)(2,1)}) custom-call(s32[7]{0:T(128)} %pad_add_fusion.slots_ref, bf16[1024,3328]{1,0:T(8,128)(2,1)} %refs_0_.9, bf16[256,3328]{1,0:T(8,128)(2,1)} %pad_maximum_fusion.refs_5_.refs_1_.tokens_ref, ...), custom_call_target="tpu_custom_call", output_to_operand_aliasing={{0}: (6, {}), {1}: (7, {})} | custom-call | tf_op jit(solution)/shard_map/finish/pallas_call | solution.py:429
  379.7 10.8 %collective-permute-done.30.refs_1_ = bf16[1280,384]{1,0:T(8,128)(2,1)S(1)} collective-permute-done((bf16[1280,384]{1,0:T(8,128)(2,1)}, bf16[1280,384]{1,0:T(8,128)(2,1)S(1)}, u32[]{:S(2)}, u32[]{:S(2)}) %collective-permute-start.30) | collective-permute-done | bytes 983072 | tf_op jit(solution)/shard_map/sums5/ppermute | solution.py:521
  391.5 3.8 finish.11
  (131 shorter events, 65.3 us)
Async XLA Ops:
  7.2 99.1 %all-gather.5.cloned.1.call-start = ((), (), s32[]{:S(2)}) async-start(), calls=%async_computation.3 | async-start | bytes 16773120 | tf_op jit(solution)/shard_map/all_gather | solution.py:481
  11.4 191.9 %all-gather.7.cloned.1.call-start = ((), (), s32[]{:S(2)}) async-start(), calls=%async_computation.4 | async-start | bytes 16773120 | tf_op jit(solution)/shard_map/all_gather | solution.py:481
  14.0 30.6 %collective-permute-start = (bf16[176,2560]{1,0:T(8,128)(2,1)S(1)}, bf16[176,2560]{1,0:T(8,128)(2,1)S(1)}, u32[]{:S(2)}, u32[]{:S(2)}) collective-permute-start(bf16[176,2560]{1,0:T(8,128)(2,1)S(1)} %get-tuple-element.119), channel_id=1, source_target_pairs={{0,8},{24,16},{1,9},{25,17},{2,10},{26,18},{3,11},{27,19},{4,12},{... | collective-permute-start | bytes 2703368 | tf_op jit(solution)/shard_map/ppermute | solution.py:469
  49.9 23.7 %all-to-all-start.2 = ((bf16[4,32,3328]{2,1,0:T(8,128)(2,1)}), bf16[4,32,3328]{2,1,0:T(8,128)(2,1)S(1)}, u32[]{:S(2)}, u32[]{:S(2)}) async-start(bf16[4,32,3328]{2,1,0:T(8,128)(2,1)} %bitcast.8), calls=%async_computation.2 | async-start | bytes 1703936 | tf_op jit(solution)/shard_map/all_to_all | solution.py:31
  76.8 21.4 %collective-permute-start.4 = (bf16[176,2560]{1,0:T(8,128)(2,1)S(1)}, bf16[176,2560]{1,0:T(8,128)(2,1)S(1)}, u32[]{:S(2)}, u32[]{:S(2)}) collective-permute-start(bf16[176,2560]{1,0:T(8,128)(2,1)S(1)} %get-tuple-element.61), channel_id=1, source_target_pairs={{0,8},{24,16},{1,9},{25,17},{2,10},{26,18},{3,11},{27,19},{4,12},{... | collective-permute-start | bytes 2703368 | tf_op jit(solution)/shard_map/ppermute | solution.py:469
  78.2 25.4 %collective-permute-start.2 = (bf16[64,3328]{1,0:T(8,128)(2,1)S(1)}, bf16[64,3328]{1,0:T(8,128)(2,1)S(1)}, u32[]{:S(2)}, u32[]{:S(2)}) collective-permute-start(bf16[64,3328]{1,0:T(8,128)(2,1)S(1)} %pad_maximum_fusion.2), channel_id=1, source_target_pairs={{0,2},{1,3},{2,0},{3,1},{4,6},{5,7},{6,4},{7,5},{8,10},{9,11},{10,... | collective-permute-start | bytes 1277960 | tf_op jit(solution)/shard_map/ppermute | solution.py:36
  98.2 29.1 %collective-permute-start.5 = (bf16[160,2560]{1,0:T(8,128)(2,1)}, bf16[160,2560]{1,0:T(8,128)(2,1)}, u32[]{:S(2)}, u32[]{:S(2)}) collective-permute-start(bf16[160,2560]{1,0:T(8,128)(2,1)} %fusion.2), channel_id=1, source_target_pairs={{0,8},{24,16},{1,9},{25,17},{2,10},{26,18},{3,11},{27,19},{4,12},{... | collective-permute-start | bytes 2457608 | tf_op jit(solution)/shard_map/ppermute | solution.py:469
  104.7 27.6 %collective-permute-start.3 = (bf16[128,3328]{1,0:T(8,128)(2,1)}, bf16[128,3328]{1,0:T(8,128)(2,1)}, u32[]{:S(2)}, u32[]{:S(2)}) collective-permute-start(bf16[128,3328]{1,0:T(8,128)(2,1)} %pad_maximum_fusion.1), channel_id=1, source_target_pairs={{0,4},{1,5},{2,6},{3,7},{4,0},{5,1},{6,2},{7,3},{8,12},{9,13},{10,... | collective-permute-start | bytes 2555912 | tf_op jit(solution)/shard_map/ppermute | solution.py:36
  121.5 32.3 %collective-permute-start.6 = (bf16[832,512]{1,0:T(8,128)(2,1)}, bf16[832,512]{1,0:T(8,128)(2,1)}, u32[]{:S(2)}, u32[]{:S(2)}) collective-permute-start(bf16[832,512]{1,0:T(8,128)(2,1)} %panel.5.refs_6_.refs_2_), channel_id=1, source_target_pairs={{0,8},{24,16},{1,9},{25,17},{2,10},{26,18},{3,11},{27,19},{4,12},{... | collective-permute-start | bytes 2555912 | tf_op jit(solution)/shard_map/outer0/ppermute | solution.py:501
  125.7 28.1 %collective-permute-start.7 = (bf16[832,512]{1,0:T(8,128)(2,1)}, bf16[832,512]{1,0:T(8,128)(2,1)}, u32[]{:S(2)}, u32[]{:S(2)}) collective-permute-start(bf16[832,512]{1,0:T(8,128)(2,1)} %panel.5.refs_6_.refs_2_), channel_id=1, source_target_pairs={{8,16},{16,8},{9,17},{17,9},{10,18},{18,10},{11,19},{19,11},{12,20... | collective-permute-start | bytes 2555912 | tf_op jit(solution)/shard_map/mate0/ppermute | solution.py:503
  133.5 45.0 %collective-permute-start.9 = (bf16[512,2560]{1,0:T(8,128)(2,1)S(1)}, bf16[512,2560]{1,0:T(8,128)(2,1)S(1)}, u32[]{:S(2)}, u32[]{:S(2)}) collective-permute-start(bf16[512,2560]{1,0:T(8,128)(2,1)S(1)} %constant_dynamic-update-slice_fusion.refs_0_), channel_id=1, source_target_pairs={{0,1},{1,0},{2,3},{3,2},{4,5},{5,4},{6,7},{7,6},{8,9},{9,8},{10,11... | collective-permute-start | bytes 7864328 | tf_op jit(solution)/shard_map/ppermute | solution.py:36
  153.8 24.6 %collective-permute-start.12 = (bf16[832,512]{1,0:T(8,128)(2,1)}, bf16[832,512]{1,0:T(8,128)(2,1)}, u32[]{:S(2)}, u32[]{:S(2)}) collective-permute-start(bf16[832,512]{1,0:T(8,128)(2,1)} %collective-permute-done.6.refs_7_), channel_id=1, source_target_pairs={{8,16},{16,8},{9,17},{17,9},{10,18},{18,10},{11,19},{19,11},{12,20... | collective-permute-start | bytes 2555912 | tf_op jit(solution)/shard_map/far0/ppermute | solution.py:508
  157.6 20.8 %collective-permute-start.11 = (bf16[128,2560]{1,0:T(8,128)(2,1)S(1)}, bf16[128,2560]{1,0:T(8,128)(2,1)S(1)}, u32[]{:S(2)}, u32[]{:S(2)}) collective-permute-start(bf16[128,2560]{1,0:T(8,128)(2,1)S(1)} %collective-permute-done.10.refs_2_), channel_id=1, source_target_pairs={{0,1},{1,0},{2,3},{3,2},{4,5},{5,4},{6,7},{7,6},{8,9},{9,8},{10,11... | collective-permute-start | bytes 1966088 | tf_op jit(solution)/shard_map/ppermute | solution.py:36
  157.6 24.5 %collective-permute-start.8 = (bf16[832,512]{1,0:T(8,128)(2,1)}, bf16[832,512]{1,0:T(8,128)(2,1)}, u32[]{:S(2)}, u32[]{:S(2)}) collective-permute-start(bf16[832,512]{1,0:T(8,128)(2,1)} %panel.6.refs_6_.refs_2_), channel_id=1, source_target_pairs={{0,8},{24,16},{1,9},{25,17},{2,10},{26,18},{3,11},{27,19},{4,12},{... | collective-permute-start | bytes 2555912 | tf_op jit(solution)/shard_map/outer1/ppermute | solution.py:501
  162.9 40.4 %collective-permute-start.13 = (bf16[832,512]{1,0:T(8,128)(2,1)}, bf16[832,512]{1,0:T(8,128)(2,1)}, u32[]{:S(2)}, u32[]{:S(2)}) collective-permute-start(bf16[832,512]{1,0:T(8,128)(2,1)} %panel.6.refs_6_.refs_2_), channel_id=1, source_target_pairs={{8,16},{16,8},{9,17},{17,9},{10,18},{18,10},{11,19},{19,11},{12,20... | collective-permute-start | bytes 2555912 | tf_op jit(solution)/shard_map/mate1/ppermute | solution.py:503
  182.1 38.9 %collective-permute-start.16 = (bf16[832,512]{1,0:T(8,128)(2,1)}, bf16[832,512]{1,0:T(8,128)(2,1)}, u32[]{:S(2)}, u32[]{:S(2)}) collective-permute-start(bf16[832,512]{1,0:T(8,128)(2,1)} %collective-permute-done.8.refs_7_), channel_id=1, source_target_pairs={{8,16},{16,8},{9,17},{17,9},{10,18},{18,10},{11,19},{19,11},{12,20... | collective-permute-start | bytes 2555912 | tf_op jit(solution)/shard_map/far1/ppermute | solution.py:508
  183.7 56.4 %collective-permute-start.18 = (bf16[1280,512]{1,0:T(8,128)(2,1)}, bf16[1280,512]{1,0:T(8,128)(2,1)S(1)}, u32[]{:S(2)}, u32[]{:S(2)}) collective-permute-start(bf16[1280,512]{1,0:T(8,128)(2,1)} %get-tuple-element.72), channel_id=1, source_target_pairs={{8,0},{16,24},{9,1},{17,25},{10,2},{18,26},{11,3},{19,27},{12,4},{... | collective-permute-start | bytes 3932168 | tf_op jit(solution)/shard_map/sums0/ppermute | solution.py:521
  185.0 35.3 %collective-permute-start.15 = (bf16[832,384]{1,0:T(8,128)(2,1)}, bf16[832,384]{1,0:T(8,128)(2,1)}, u32[]{:S(2)}, u32[]{:S(2)}) collective-permute-start(bf16[832,384]{1,0:T(8,128)(2,1)} %panel.7.refs_6_.refs_2_), channel_id=1, source_target_pairs={{0,8},{24,16},{1,9},{25,17},{2,10},{26,18},{3,11},{27,19},{4,12},{... | collective-permute-start | bytes 1916936 | tf_op jit(solution)/shard_map/outer2/ppermute | solution.py:501
  218.0 21.3 %collective-permute-start.14 = (bf16[832,512]{1,0:T(8,128)(2,1)}, bf16[832,512]{1,0:T(8,128)(2,1)S(1)}, u32[]{:S(2)}, u32[]{:S(2)}) collective-permute-start(bf16[832,512]{1,0:T(8,128)(2,1)} %panel.8.refs_6_.refs_2_), channel_id=1, source_target_pairs={{0,8},{24,16},{1,9},{25,17},{2,10},{26,18},{3,11},{27,19},{4,12},{... | collective-permute-start | bytes 2555912 | tf_op jit(solution)/shard_map/outer3/ppermute | solution.py:501
  220.3 49.1 %collective-permute-start.20 = (bf16[832,512]{1,0:T(8,128)(2,1)}, bf16[832,512]{1,0:T(8,128)(2,1)S(1)}, u32[]{:S(2)}, u32[]{:S(2)}) collective-permute-start(bf16[832,512]{1,0:T(8,128)(2,1)} %panel.8.refs_6_.refs_2_), channel_id=1, source_target_pairs={{8,16},{16,8},{9,17},{17,9},{10,18},{18,10},{11,19},{19,11},{12,20... | collective-permute-start | bytes 2555912 | tf_op jit(solution)/shard_map/mate3/ppermute | solution.py:503
  221.0 56.3 %collective-permute-start.21 = (bf16[832,384]{1,0:T(8,128)(2,1)}, bf16[832,384]{1,0:T(8,128)(2,1)S(1)}, u32[]{:S(2)}, u32[]{:S(2)}) collective-permute-start(bf16[832,384]{1,0:T(8,128)(2,1)} %collective-permute-done.15.refs_7_), channel_id=1, source_target_pairs={{8,16},{16,8},{9,17},{17,9},{10,18},{18,10},{11,19},{19,11},{12,20... | collective-permute-start | bytes 1916936 | tf_op jit(solution)/shard_map/far2/ppermute | solution.py:508
  222.6 72.0 %collective-permute-start.24 = (bf16[1280,512]{1,0:T(8,128)(2,1)}, bf16[1280,512]{1,0:T(8,128)(2,1)S(1)}, u32[]{:S(2)}, u32[]{:S(2)}) collective-permute-start(bf16[1280,512]{1,0:T(8,128)(2,1)} %get-tuple-element.80), channel_id=1, source_target_pairs={{8,0},{16,24},{9,1},{17,25},{10,2},{18,26},{11,3},{19,27},{12,4},{... | collective-permute-start | bytes 3932168 | tf_op jit(solution)/shard_map/sums1/ppermute | solution.py:521
  239.3 41.2 %collective-permute-start.22 = (bf16[832,512]{1,0:T(8,128)(2,1)S(1)}, bf16[832,512]{1,0:T(8,128)(2,1)S(1)}, u32[]{:S(2)}, u32[]{:S(2)}) collective-permute-start(bf16[832,512]{1,0:T(8,128)(2,1)S(1)} %collective-permute-done.14.refs_7_), channel_id=1, source_target_pairs={{8,16},{16,8},{9,17},{17,9},{10,18},{18,10},{11,19},{19,11},{12,20... | collective-permute-start | bytes 2555912 | tf_op jit(solution)/shard_map/far3/ppermute | solution.py:508
  262.8 24.7 %collective-permute-start.19 = (bf16[832,512]{1,0:T(8,128)(2,1)}, bf16[832,512]{1,0:T(8,128)(2,1)S(1)}, u32[]{:S(2)}, u32[]{:S(2)}) collective-permute-start(bf16[832,512]{1,0:T(8,128)(2,1)} %get-tuple-element.100.refs_6_.refs_2_), channel_id=1, source_target_pairs={{0,8},{24,16},{1,9},{25,17},{2,10},{26,18},{3,11},{27,19},{4,12},{... | collective-permute-start | bytes 2555912 | tf_op jit(solution)/shard_map/outer4/ppermute | solution.py:501
  269.4 48.1 %collective-permute-start.25 = (bf16[832,512]{1,0:T(8,128)(2,1)}, bf16[832,512]{1,0:T(8,128)(2,1)S(1)}, u32[]{:S(2)}, u32[]{:S(2)}) collective-permute-start(bf16[832,512]{1,0:T(8,128)(2,1)} %get-tuple-element.100.refs_6_.refs_2_), channel_id=1, source_target_pairs={{8,16},{16,8},{9,17},{17,9},{10,18},{18,10},{11,19},{19,11},{12,20... | collective-permute-start | bytes 2555912 | tf_op jit(solution)/shard_map/mate4/ppermute | solution.py:503
  279.1 30.3 %collective-permute-start.27 = (bf16[1280,384]{1,0:T(8,128)(2,1)}, bf16[1280,384]{1,0:T(8,128)(2,1)S(1)}, u32[]{:S(2)}, u32[]{:S(2)}) collective-permute-start(bf16[1280,384]{1,0:T(8,128)(2,1)} %get-tuple-element.90), channel_id=1, source_target_pairs={{8,0},{16,24},{9,1},{17,25},{10,2},{18,26},{11,3},{19,27},{12,4},{... | collective-permute-start | bytes 2949128 | tf_op jit(solution)/shard_map/sums2/ppermute | solution.py:521
  287.6 31.6 %collective-permute-start.26 = (bf16[832,512]{1,0:T(8,128)(2,1)S(1)}, bf16[832,512]{1,0:T(8,128)(2,1)S(1)}, u32[]{:S(2)}, u32[]{:S(2)}) collective-permute-start(bf16[832,512]{1,0:T(8,128)(2,1)S(1)} %collective-permute-done.19.refs_7_), channel_id=1, source_target_pairs={{8,16},{16,8},{9,17},{17,9},{10,18},{18,10},{11,19},{19,11},{12,20... | collective-permute-start | bytes 2555912 | tf_op jit(solution)/shard_map/far4/ppermute | solution.py:508
  288.3 30.2 %collective-permute-start.23 = (bf16[832,384]{1,0:T(8,128)(2,1)S(1)}, bf16[832,384]{1,0:T(8,128)(2,1)S(1)}, u32[]{:S(2)}, u32[]{:S(2)}) collective-permute-start(bf16[832,384]{1,0:T(8,128)(2,1)S(1)} %copy-done.2), channel_id=1, source_target_pairs={{0,8},{24,16},{1,9},{25,17},{2,10},{26,18},{3,11},{27,19},{4,12},{... | collective-permute-start | bytes 1916936 | tf_op jit(solution)/shard_map/outer5/ppermute | solution.py:501
  294.6 27.7 %collective-permute-start.28 = (bf16[832,384]{1,0:T(8,128)(2,1)S(1)}, bf16[832,384]{1,0:T(8,128)(2,1)S(1)}, u32[]{:S(2)}, u32[]{:S(2)}) collective-permute-start(bf16[832,384]{1,0:T(8,128)(2,1)S(1)} %copy-done.2), channel_id=1, source_target_pairs={{8,16},{16,8},{9,17},{17,9},{10,18},{18,10},{11,19},{19,11},{12,20... | collective-permute-start | bytes 1916936 | tf_op jit(solution)/shard_map/mate5/ppermute | solution.py:503
  309.4 33.8 %collective-permute-start.32 = (bf16[1280,512]{1,0:T(8,128)(2,1)}, bf16[1280,512]{1,0:T(8,128)(2,1)S(1)}, u32[]{:S(2)}, u32[]{:S(2)}) collective-permute-start(bf16[1280,512]{1,0:T(8,128)(2,1)} %get-tuple-element.98), channel_id=1, source_target_pairs={{8,0},{16,24},{9,1},{17,25},{10,2},{18,26},{11,3},{19,27},{12,4},{... | collective-permute-start | bytes 3932168 | tf_op jit(solution)/shard_map/sums3/ppermute | solution.py:521
  320.9 50.4 %collective-permute-start.31 = (bf16[1280,512]{1,0:T(8,128)(2,1)}, bf16[1280,512]{1,0:T(8,128)(2,1)S(1)}, u32[]{:S(2)}, u32[]{:S(2)}) collective-permute-start(bf16[1280,512]{1,0:T(8,128)(2,1)} %get-tuple-element.105), channel_id=1, source_target_pairs={{8,0},{16,24},{9,1},{17,25},{10,2},{18,26},{11,3},{19,27},{12,4},{... | collective-permute-start | bytes 3932168 | tf_op jit(solution)/shard_map/sums4/ppermute | solution.py:521
  325.0 65.5 %collective-permute-start.30 = (bf16[1280,384]{1,0:T(8,128)(2,1)}, bf16[1280,384]{1,0:T(8,128)(2,1)S(1)}, u32[]{:S(2)}, u32[]{:S(2)}) collective-permute-start(bf16[1280,384]{1,0:T(8,128)(2,1)} %products.12), channel_id=1, source_target_pairs={{8,0},{16,24},{9,1},{17,25},{10,2},{18,26},{11,3},{19,27},{12,4},{... | collective-permute-start | bytes 2949128 | tf_op jit(solution)/shard_map/sums5/ppermute | solution.py:521
  (27 other events, 187.5 us)
Sparse Core Ops, SparseCore 0:
  11.5 94.6 all-gather.4
  108.1 86.6 all-gather.6

commit v4 on v3

--- a/solution.py
+++ b/solution.py
@@ -98,7 +98,7 @@
     return -(-width // 128) * 128
 
 
-def panel_of(small, growth, splits):
+def panel_of(small, growth, splits, weight):
     rows, depth = small.shape
     first = splits[0][0]
     wide = tiled(splits[-1][0] + splits[-1][1] - first)
@@ -115,7 +115,7 @@
         out_specs=[pl.BlockSpec((rows, tiled(width)), lambda k: (0, 0)) for _, width in splits],
         scratch_shapes=[pltpu.VMEM((rows, wide), F32)],
         compiler_params=pltpu.CompilerParams(vmem_limit_bytes=VMEM_LIMIT),
-        cost_estimate=pl.CostEstimate(flops=3 * rows * depth * wide, bytes_accessed=0, transcendentals=0),
+        cost_estimate=pl.CostEstimate(flops=weight * rows * depth * wide, bytes_accessed=0, transcendentals=0),
         name="panel",
     )(small, growth)
 
@@ -489,10 +489,10 @@
     own, outer, mate, far, out, received = ({} for _ in range(6))
     grown = gate = hidden = theirs = None
 
-    def panel(chosen, *made):
+    def panel(chosen, *made, weight=3):
         m = work[chosen[0]][0]
         source = after(small[m], *made) if made else small[m]
-        for k, part in zip(chosen, panel_of(source, ffn_growth, [work[k][1:] for k in chosen])):
+        for k, part in zip(chosen, panel_of(source, ffn_growth, [work[k][1:] for k in chosen], weight)):
             own[k] = part
 
     def send(k, *made):
@@ -543,11 +543,11 @@
     send(0)
     panel([1], own[0], token_growth, rows_half)
     forward(0, mate[0], own[1])
-    token_half = after(token_half, own[1])
+    send(1, outer[0])
+    panel([2], outer[0], weight=3)
+    token_half = after(token_half, own[2])
     theirs = (rows_half, swap(rows_half, 1), token_half, swap(token_half, 1))
-    send(1, outer[0])
-    panel([2], outer[0])
-    multiply(0, far[0], own[2])
+    multiply(0, far[0], own[2], outer[1])
     forward(1, out[0])
     send(2, outer[1])
     panel([3], outer[1], out[0], mate[1])

time: 411 us -> 406 us (0.988)
    unnamed x48 -> x46, local copies, waits for them, and re-layouts: 11.5 us -> 9.15 us
  transfers between devices with their start and end apart: 36 -> 36, of which waited for: 10 -> 11; matrix products, arithmetic and copies ran while one was open for 5% -> 5% of each run, Pallas kernels for 33% -> 33%
where the time goes in v4:
time: 406 us; the launch traced here: 398 us
  Pallas kernels  134 us (33%)
  waiting for transfers between devices  112 us (28%)
  starting transfers between devices  80 us (20%)
  blocking collectives  25.2 us (6%)
  local copies, waits for them, and re-layouts  15.6 us (4%)
  between operations  15.2 us (4%)
  other arithmetic  9.83 us (2%)
  matrix products  5.25 us (1%)
    pallas_call x5, Pallas kernels, panel_of(): pl.pallas_call(functools.partial(panel_kernel, steps, splits), out_shape=...  81.2 us
    ppermute x6, waiting for transfers between devices, multiply(): received[k] = lax.ppermute(out[k], 'dp', TO_OUTER)  44.7 us
    ppermute x6, starting transfers between devices, send(): outer[k] = lax.ppermute(sent, 'dp', TO_INNER)  40.4 us
    pallas_call x6, Pallas kernels, finish(): pl.pallas_call(functools.partial(finish_kernel, m, start, width, made is...  39.5 us
    ppermute x6, waiting for transfers between devices, send(): outer[k] = lax.ppermute(sent, 'dp', TO_INNER)  24.3 us
    all_to_all x1, waiting for transfers between devices, token_rows(): parts = lax.all_to_all(part, 'dp', 0, 0, tiled=True)  20.2 us
    ppermute x4, waiting for transfers between devices, fetch_half(): fetched.append(lax.ppermute(after(part, *fetched[-1:]), 'dp', TO_INNER))  17.2 us
    all_to_all x1, blocking collectives, token_rows(): by_rows = lax.all_to_all(tokens, 'tensor', 0, 1, tiled=True)  13.2 us
  transfers between devices with their start and end apart: 36, of which 11 were waited for; matrix products, arithmetic and copies ran while one was open for 5% of the time, Pallas kernels for 33%

profile of v4, /device:TPU:0, one launch (start us, length us, event | category | flops | bytes accessed | tf_op | source)
XLA Modules:
  0.0 398.0 jit_solution(12343132599581588725)
XLA Ops:
  7.2 4.2 %fusion.7 = (bf16[1,104,8960]{2,1,0:T(8,128)(2,1)}, bf16[1,104,8960]{2,1,0:T(8,128)(2,1)}) fusion(bf16[2,104,8960]{2,1,0:T(8,128)(2,1)} %param.6), kind=kLoop, calls=%fused_computation.31 | loop fusion | bytes 7454720 | tf_op jit(solution)/shard_map/slice | solution.py:481
  14.0 5.0 %collective-permute-start = (bf16[176,2560]{1,0:T(8,128)(2,1)S(1)}, bf16[176,2560]{1,0:T(8,128)(2,1)S(1)}, u32[]{:S(2)}, u32[]{:S(2)}) collective-permute-start(bf16[176,2560]{1,0:T(8,128)(2,1)S(1)} %get-tuple-element.119), channel_id=1, source_target_pairs={{0,8},{24,16},{1,9},{25,17},{2,10},{26,18},{3,11},{27,19},{4,12},{... | collective-permute-start | bytes 2703368 | tf_op jit(solution)/shard_map/ppermute | solution.py:469
  19.0 13.2 %all_to_all.44 = bf16[8,32,512]{2,1,0:T(8,128)(2,1)S(1)} all-to-all(bf16[8,32,512]{2,1,0:T(8,128)(2,1)S(1)} %bitcast.24), channel_id=1, replica_groups=mesh['dp'=4,'tensor'=8] {'tensor'}, dimensions={0} | all-to-all | bytes 524288 | tf_op jit(solution)/shard_map/all_to_all | solution.py:27
  32.7 12.0 %all_to_all.45 = bf16[32,4,1024]{2,0,1:T(8,128)(2,1)S(1)} all-to-all(bf16[32,4,1024]{2,0,1:T(8,128)(2,1)S(1)} %copy.31), channel_id=1, replica_groups=mesh['dp'=4,'tensor'=8] {'dp'}, dimensions={1} | all-to-all | bytes 524288 | tf_op jit(solution)/shard_map/all_to_all | solution.py:28
  44.7 5.3 %convolution_convert_fusion = bf16[128,3328]{1,0:T(8,128)(2,1)} fusion(bf16[128,1024]{1,0:T(8,128)(2,1)S(1)} %bitcast.22, bf16[1024,3328]{1,0:T(8,128)(2,1)} %refs_0_.9), kind=kOutput, calls=%fused_computation | convolution fusion | flops 872841216 | bytes 7929856 | tf_op jit(solution)/shard_map/dot_general | solution.py:30
  49.9 3.5 all-to-all-start.2
  53.4 20.2 %all-to-all-done.2 = bf16[4,32,3328]{2,1,0:T(8,128)(2,1)S(1)} async-done(((bf16[4,32,3328]{2,1,0:T(8,128)(2,1)}), bf16[4,32,3328]{2,1,0:T(8,128)(2,1)S(1)}, u32[]{:S(2)}, u32[]{:S(2)}) %all-to-all-start.2) | async-done | bytes 852000 | tf_op jit(solution)/shard_map/all_to_all | solution.py:31
  80.3 17.2 %collective-permute-done.4 = bf16[176,2560]{1,0:T(8,128)(2,1)S(1)} collective-permute-done((bf16[176,2560]{1,0:T(8,128)(2,1)S(1)}, bf16[176,2560]{1,0:T(8,128)(2,1)S(1)}, u32[]{:S(2)}, u32[]{:S(2)}) %collective-permute-start.4) | collective-permute-done | bytes 901152 | tf_op jit(solution)/shard_map/ppermute | solution.py:469
  97.6 5.3 %collective-permute-start.5 = (bf16[160,2560]{1,0:T(8,128)(2,1)}, bf16[160,2560]{1,0:T(8,128)(2,1)}, u32[]{:S(2)}, u32[]{:S(2)}) collective-permute-start(bf16[160,2560]{1,0:T(8,128)(2,1)} %fusion.2), channel_id=1, source_target_pairs={{0,8},{24,16},{1,9},{25,17},{2,10},{26,18},{3,11},{27,19},{4,12},{... | collective-permute-start | bytes 2457608 | tf_op jit(solution)/shard_map/ppermute | solution.py:469
  106.3 15.3 %panel.5.refs_6_.refs_2_ = bf16[832,512]{1,0:T(8,128)(2,1)} custom-call(bf16[832,8960]{1,0:T(8,128)(2,1)} %bitcast.18, bf16[1376,8960]{1,0:T(8,128)(2,1)} %growth_ref.9), custom_call_target="tpu_custom_call" | custom-call | flops 11450449920 | tf_op jit(solution)/shard_map/panel/pallas_call | solution.py:107
  121.5 4.2 %collective-permute-start.6 = (bf16[832,512]{1,0:T(8,128)(2,1)}, bf16[832,512]{1,0:T(8,128)(2,1)}, u32[]{:S(2)}, u32[]{:S(2)}) collective-permute-start(bf16[832,512]{1,0:T(8,128)(2,1)} %panel.5.refs_6_.refs_2_), channel_id=1, source_target_pairs={{0,8},{24,16},{1,9},{25,17},{2,10},{26,18},{3,11},{27,19},{4,12},{... | collective-permute-start | bytes 2555912 | tf_op jit(solution)/shard_map/outer0/ppermute | solution.py:501
  126.4 4.5 %collective-permute-done.3 = bf16[128,3328]{1,0:T(8,128)(2,1)} collective-permute-done((bf16[128,3328]{1,0:T(8,128)(2,1)}, bf16[128,3328]{1,0:T(8,128)(2,1)}, u32[]{:S(2)}, u32[]{:S(2)}) %collective-permute-start.3) | collective-permute-done | bytes 852000 | tf_op jit(solution)/shard_map/ppermute | solution.py:36
  137.4 14.6 %panel.6.refs_6_.refs_2_ = bf16[832,512]{1,0:T(8,128)(2,1)} custom-call(bf16[832,8960]{1,0:T(8,128)(2,1)} %bitcast.19, bf16[1376,8960]{1,0:T(8,128)(2,1)} %growth_ref.9), custom_call_target="tpu_custom_call" | custom-call | flops 11450449920 | tf_op jit(solution)/shard_map/panel/pallas_call | solution.py:107
  155.8 14.0 %panel.7.refs_6_.refs_2_ = bf16[832,384]{1,0:T(8,128)(2,1)} custom-call(bf16[832,8960]{1,0:T(8,128)(2,1)} %bitcast.20, bf16[1376,8960]{1,0:T(8,128)(2,1)} %growth_ref.9), custom_call_target="tpu_custom_call" | custom-call | flops 8587837440 | tf_op jit(solution)/shard_map/panel/pallas_call | solution.py:107
  180.2 19.6 %collective-permute-start.15 = (bf16[832,384]{1,0:T(8,128)(2,1)}, bf16[832,384]{1,0:T(8,128)(2,1)}, u32[]{:S(2)}, u32[]{:S(2)}) collective-permute-start(bf16[832,384]{1,0:T(8,128)(2,1)} %panel.7.refs_6_.refs_2_), channel_id=1, source_target_pairs={{0,8},{24,16},{1,9},{25,17},{2,10},{26,18},{3,11},{27,19},{4,12},{... | collective-permute-start | bytes 1916936 | tf_op jit(solution)/shard_map/outer2/ppermute | solution.py:501
  201.3 14.6 %panel.8.refs_6_.refs_2_ = bf16[832,512]{1,0:T(8,128)(2,1)} custom-call(bf16[832,8960]{1,0:T(8,128)(2,1)} %bitcast.25, bf16[1376,8960]{1,0:T(8,128)(2,1)} %growth_ref.9), custom_call_target="tpu_custom_call" | custom-call | flops 11450449920 | tf_op jit(solution)/shard_map/panel/pallas_call | solution.py:107
  221.0 14.8 %collective-permute-done.14.refs_7_ = bf16[832,512]{1,0:T(8,128)(2,1)S(1)} collective-permute-done((bf16[832,512]{1,0:T(8,128)(2,1)}, bf16[832,512]{1,0:T(8,128)(2,1)S(1)}, u32[]{:S(2)}, u32[]{:S(2)}) %collective-permute-start.14) | collective-permute-done | bytes 852000 | tf_op jit(solution)/shard_map/outer3/ppermute | solution.py:501
  236.7 22.7 %panel.9 = (bf16[832,512]{1,0:T(8,128)(2,1)}, bf16[832,384]{1,0:T(8,128)(2,1)}) custom-call(bf16[832,8960]{1,0:T(8,128)(2,1)} %bitcast.26, bf16[1376,8960]{1,0:T(8,128)(2,1)} %growth_ref.9), custom_call_target="tpu_custom_call" | custom-call | flops 20038287360 | tf_op jit(solution)/shard_map/panel/pallas_call | solution.py:107
  259.4 6.9 %collective-permute-start.19 = (bf16[832,512]{1,0:T(8,128)(2,1)}, bf16[832,512]{1,0:T(8,128)(2,1)S(1)}, u32[]{:S(2)}, u32[]{:S(2)}) collective-permute-start(bf16[832,512]{1,0:T(8,128)(2,1)} %get-tuple-element.100.refs_6_.refs_2_), channel_id=1, source_target_pairs={{0,8},{24,16},{1,9},{25,17},{2,10},{26,18},{3,11},{27,19},{4,12},{... | collective-permute-start | bytes 2555912 | tf_op jit(solution)/shard_map/outer4/ppermute | solution.py:501
  267.0 7.2 %finish.6 = (bf16[2,1376,1024]{2,1,0:T(8,128)(2,1)}, f32[256,1408]{1,0:T(8,128)}) custom-call(s32[7]{0:T(128)} %pad_add_fusion.slots_ref, bf16[1024,3328]{1,0:T(8,128)(2,1)} %refs_0_.9, bf16[256,3328]{1,0:T(8,128)(2,1)} %pad_maximum_fusion.refs_5_.refs_1_.tokens_ref, ...), custom_call_target="tpu_custom_call", output_to_operand_aliasing={{0}: (6, {}), {1}: (5, {})} | custom-call | tf_op jit(solution)/shard_map/finish/pallas_call | solution.py:429
  277.3 6.4 %collective-permute-done.19.refs_7_ = bf16[832,512]{1,0:T(8,128)(2,1)S(1)} collective-permute-done((bf16[832,512]{1,0:T(8,128)(2,1)}, bf16[832,512]{1,0:T(8,128)(2,1)S(1)}, u32[]{:S(2)}, u32[]{:S(2)}) %collective-permute-start.19) | collective-permute-done | bytes 852000 | tf_op jit(solution)/shard_map/outer4/ppermute | solution.py:501
  284.4 6.1 %collective-permute-start.23 = (bf16[832,384]{1,0:T(8,128)(2,1)S(1)}, bf16[832,384]{1,0:T(8,128)(2,1)S(1)}, u32[]{:S(2)}, u32[]{:S(2)}) collective-permute-start(bf16[832,384]{1,0:T(8,128)(2,1)S(1)} %copy-done.1), channel_id=1, source_target_pairs={{0,8},{24,16},{1,9},{25,17},{2,10},{26,18},{3,11},{27,19},{4,12},{... | collective-permute-start | bytes 1916936 | tf_op jit(solution)/shard_map/outer5/ppermute | solution.py:501
  291.6 7.2 %finish.7 = (bf16[2,1376,1024]{2,1,0:T(8,128)(2,1)}, f32[256,1408]{1,0:T(8,128)}) custom-call(s32[7]{0:T(128)} %pad_add_fusion.slots_ref, bf16[1024,3328]{1,0:T(8,128)(2,1)} %refs_0_.9, bf16[256,3328]{1,0:T(8,128)(2,1)} %pad_maximum_fusion.refs_5_.refs_1_.tokens_ref, ...), custom_call_target="tpu_custom_call", output_to_operand_aliasing={{0}: (6, {}), {1}: (5, {})} | custom-call | tf_op jit(solution)/shard_map/finish/pallas_call | solution.py:429
  299.8 5.6 %collective-permute-done.27.refs_3_ = bf16[1280,384]{1,0:T(8,128)(2,1)S(1)} collective-permute-done((bf16[1280,384]{1,0:T(8,128)(2,1)}, bf16[1280,384]{1,0:T(8,128)(2,1)S(1)}, u32[]{:S(2)}, u32[]{:S(2)}) %collective-permute-start.27) | collective-permute-done | bytes 983072 | tf_op jit(solution)/shard_map/sums2/ppermute | solution.py:521
  306.7 6.8 %finish.8 = (bf16[2,1376,1024]{2,1,0:T(8,128)(2,1)}, f32[256,1408]{1,0:T(8,128)}) custom-call(s32[7]{0:T(128)} %pad_add_fusion.slots_ref, bf16[1024,3328]{1,0:T(8,128)(2,1)} %refs_0_.9, bf16[256,3328]{1,0:T(8,128)(2,1)} %pad_maximum_fusion.refs_5_.refs_1_.tokens_ref, ...), custom_call_target="tpu_custom_call", output_to_operand_aliasing={{0}: (6, {}), {1}: (5, {})} | custom-call | tf_op jit(solution)/shard_map/finish/pallas_call | solution.py:429
  322.3 6.9 %own_product.1.refs_0_ = f32[1280,384]{1,0:T(8,128)} custom-call(s32[7]{0:T(128)} %pad_add_fusion.slots_ref, bf16[1024,3328]{1,0:T(8,128)(2,1)} %refs_0_.9, bf16[256,3328]{1,0:T(8,128)(2,1)} %pad_maximum_fusion.refs_5_.refs_1_.tokens_ref, bf16[832,384]{1,0:T(8,128)(2,1)} %get-tuple-element.107.refs_6_.own_ref), custom_call_target="tpu_custom_call" | custom-call | tf_op jit(solution)/shard_map/own_product/pallas_call | solution.py:341
  329.1 10.1 %collective-permute-done.32.refs_3_ = bf16[1280,512]{1,0:T(8,128)(2,1)S(1)} collective-permute-done((bf16[1280,512]{1,0:T(8,128)(2,1)}, bf16[1280,512]{1,0:T(8,128)(2,1)S(1)}, u32[]{:S(2)}, u32[]{:S(2)}) %collective-permute-start.32) | collective-permute-done | bytes 1310752 | tf_op jit(solution)/shard_map/sums3/ppermute | solution.py:521
  340.3 7.3 %finish.9 = (bf16[2,1376,1024]{2,1,0:T(8,128)(2,1)}, bf16[1376,256]{1,0:T(8,128)(2,1)}) custom-call(s32[7]{0:T(128)} %pad_add_fusion.slots_ref, bf16[1024,3328]{1,0:T(8,128)(2,1)} %refs_0_.9, bf16[256,3328]{1,0:T(8,128)(2,1)} %pad_maximum_fusion.refs_5_.refs_1_.tokens_ref, ...), custom_call_target="tpu_custom_call", output_to_operand_aliasing={{0}: (6, {}), {1}: (7, {})} | custom-call | tf_op jit(solution)/shard_map/finish/pallas_call | solution.py:429
  348.5 18.9 %collective-permute-done.31.refs_3_ = bf16[1280,512]{1,0:T(8,128)(2,1)S(1)} collective-permute-done((bf16[1280,512]{1,0:T(8,128)(2,1)}, bf16[1280,512]{1,0:T(8,128)(2,1)S(1)}, u32[]{:S(2)}, u32[]{:S(2)}) %collective-permute-start.31) | collective-permute-done | bytes 1310752 | tf_op jit(solution)/shard_map/sums4/ppermute | solution.py:521
  368.4 7.3 %finish.10 = (bf16[2,1376,1024]{2,1,0:T(8,128)(2,1)}, bf16[1376,256]{1,0:T(8,128)(2,1)}) custom-call(s32[7]{0:T(128)} %pad_add_fusion.slots_ref, bf16[1024,3328]{1,0:T(8,128)(2,1)} %refs_0_.9, bf16[256,3328]{1,0:T(8,128)(2,1)} %pad_maximum_fusion.refs_5_.refs_1_.tokens_ref, ...), custom_call_target="tpu_custom_call", output_to_operand_aliasing={{0}: (6, {}), {1}: (7, {})} | custom-call | tf_op jit(solution)/shard_map/finish/pallas_call | solution.py:429
  375.6 10.2 %collective-permute-done.30.refs_1_ = bf16[1280,384]{1,0:T(8,128)(2,1)S(1)} collective-permute-done((bf16[1280,384]{1,0:T(8,128)(2,1)}, bf16[1280,384]{1,0:T(8,128)(2,1)S(1)}, u32[]{:S(2)}, u32[]{:S(2)}) %collective-permute-start.30) | collective-permute-done | bytes 983072 | tf_op jit(solution)/shard_map/sums5/ppermute | solution.py:521
  386.8 3.8 finish.11
  (129 shorter events, 62.4 us)
Async XLA Ops:
  7.2 99.1 %all-gather.5.cloned.1.call-start = ((), (), s32[]{:S(2)}) async-start(), calls=%async_computation.3 | async-start | bytes 16773120 | tf_op jit(solution)/shard_map/all_gather | solution.py:481
  11.4 189.9 %all-gather.7.cloned.1.call-start = ((), (), s32[]{:S(2)}) async-start(), calls=%async_computation.4 | async-start | bytes 16773120 | tf_op jit(solution)/shard_map/all_gather | solution.py:481
  14.0 30.6 %collective-permute-start = (bf16[176,2560]{1,0:T(8,128)(2,1)S(1)}, bf16[176,2560]{1,0:T(8,128)(2,1)S(1)}, u32[]{:S(2)}, u32[]{:S(2)}) collective-permute-start(bf16[176,2560]{1,0:T(8,128)(2,1)S(1)} %get-tuple-element.119), channel_id=1, source_target_pairs={{0,8},{24,16},{1,9},{25,17},{2,10},{26,18},{3,11},{27,19},{4,12},{... | collective-permute-start | bytes 2703368 | tf_op jit(solution)/shard_map/ppermute | solution.py:469
  49.9 23.7 %all-to-all-start.2 = ((bf16[4,32,3328]{2,1,0:T(8,128)(2,1)}), bf16[4,32,3328]{2,1,0:T(8,128)(2,1)S(1)}, u32[]{:S(2)}, u32[]{:S(2)}) async-start(bf16[4,32,3328]{2,1,0:T(8,128)(2,1)} %bitcast.8), calls=%async_computation.2 | async-start | bytes 1703936 | tf_op jit(solution)/shard_map/all_to_all | solution.py:31
  76.1 21.5 %collective-permute-start.4 = (bf16[176,2560]{1,0:T(8,128)(2,1)S(1)}, bf16[176,2560]{1,0:T(8,128)(2,1)S(1)}, u32[]{:S(2)}, u32[]{:S(2)}) collective-permute-start(bf16[176,2560]{1,0:T(8,128)(2,1)S(1)} %get-tuple-element.61), channel_id=1, source_target_pairs={{0,8},{24,16},{1,9},{25,17},{2,10},{26,18},{3,11},{27,19},{4,12},{... | collective-permute-start | bytes 2703368 | tf_op jit(solution)/shard_map/ppermute | solution.py:469
  77.5 25.4 %collective-permute-start.2 = (bf16[64,3328]{1,0:T(8,128)(2,1)S(1)}, bf16[64,3328]{1,0:T(8,128)(2,1)S(1)}, u32[]{:S(2)}, u32[]{:S(2)}) collective-permute-start(bf16[64,3328]{1,0:T(8,128)(2,1)S(1)} %pad_maximum_fusion.2), channel_id=1, source_target_pairs={{0,2},{1,3},{2,0},{3,1},{4,6},{5,7},{6,4},{7,5},{8,10},{9,11},{10,... | collective-permute-start | bytes 1277960 | tf_op jit(solution)/shard_map/ppermute | solution.py:36
  97.6 28.9 %collective-permute-start.5 = (bf16[160,2560]{1,0:T(8,128)(2,1)}, bf16[160,2560]{1,0:T(8,128)(2,1)}, u32[]{:S(2)}, u32[]{:S(2)}) collective-permute-start(bf16[160,2560]{1,0:T(8,128)(2,1)} %fusion.2), channel_id=1, source_target_pairs={{0,8},{24,16},{1,9},{25,17},{2,10},{26,18},{3,11},{27,19},{4,12},{... | collective-permute-start | bytes 2457608 | tf_op jit(solution)/shard_map/ppermute | solution.py:469
  104.0 26.9 %collective-permute-start.3 = (bf16[128,3328]{1,0:T(8,128)(2,1)}, bf16[128,3328]{1,0:T(8,128)(2,1)}, u32[]{:S(2)}, u32[]{:S(2)}) collective-permute-start(bf16[128,3328]{1,0:T(8,128)(2,1)} %pad_maximum_fusion.1), channel_id=1, source_target_pairs={{0,4},{1,5},{2,6},{3,7},{4,0},{5,1},{6,2},{7,3},{8,12},{9,13},{10,... | collective-permute-start | bytes 2555912 | tf_op jit(solution)/shard_map/ppermute | solution.py:36
  121.5 30.5 %collective-permute-start.6 = (bf16[832,512]{1,0:T(8,128)(2,1)}, bf16[832,512]{1,0:T(8,128)(2,1)}, u32[]{:S(2)}, u32[]{:S(2)}) collective-permute-start(bf16[832,512]{1,0:T(8,128)(2,1)} %panel.5.refs_6_.refs_2_), channel_id=1, source_target_pairs={{0,8},{24,16},{1,9},{25,17},{2,10},{26,18},{3,11},{27,19},{4,12},{... | collective-permute-start | bytes 2555912 | tf_op jit(solution)/shard_map/outer0/ppermute | solution.py:501
  125.7 26.3 %collective-permute-start.7 = (bf16[832,512]{1,0:T(8,128)(2,1)}, bf16[832,512]{1,0:T(8,128)(2,1)S(1)}, u32[]{:S(2)}, u32[]{:S(2)}) collective-permute-start(bf16[832,512]{1,0:T(8,128)(2,1)} %panel.5.refs_6_.refs_2_), channel_id=1, source_target_pairs={{8,16},{16,8},{9,17},{17,9},{10,18},{18,10},{11,19},{19,11},{12,20... | collective-permute-start | bytes 2555912 | tf_op jit(solution)/shard_map/mate0/ppermute | solution.py:503
  132.2 43.8 %collective-permute-start.9 = (bf16[512,2560]{1,0:T(8,128)(2,1)S(1)}, bf16[512,2560]{1,0:T(8,128)(2,1)}, u32[]{:S(2)}, u32[]{:S(2)}) collective-permute-start(bf16[512,2560]{1,0:T(8,128)(2,1)S(1)} %constant_dynamic-update-slice_fusion.refs_0_), channel_id=1, source_target_pairs={{0,1},{1,0},{2,3},{3,2},{4,5},{5,4},{6,7},{7,6},{8,9},{9,8},{10,11... | collective-permute-start | bytes 7864328 | tf_op jit(solution)/shard_map/ppermute | solution.py:36
  136.0 33.8 %collective-permute-start.10 = (bf16[128,2560]{1,0:T(8,128)(2,1)S(1)}, bf16[128,2560]{1,0:T(8,128)(2,1)S(1)}, u32[]{:S(2)}, u32[]{:S(2)}) collective-permute-start(bf16[128,2560]{1,0:T(8,128)(2,1)S(1)} %fusion.3), channel_id=1, source_target_pairs={{0,8},{24,16},{1,9},{25,17},{2,10},{26,18},{3,11},{27,19},{4,12},{... | collective-permute-start | bytes 1966088 | tf_op jit(solution)/shard_map/ppermute | solution.py:469
  152.0 24.0 %collective-permute-start.12 = (bf16[832,512]{1,0:T(8,128)(2,1)}, bf16[832,512]{1,0:T(8,128)(2,1)}, u32[]{:S(2)}, u32[]{:S(2)}) collective-permute-start(bf16[832,512]{1,0:T(8,128)(2,1)} %collective-permute-done.6.refs_7_), channel_id=1, source_target_pairs={{8,16},{16,8},{9,17},{17,9},{10,18},{18,10},{11,19},{19,11},{12,20... | collective-permute-start | bytes 2555912 | tf_op jit(solution)/shard_map/far0/ppermute | solution.py:508
  153.6 22.4 %collective-permute-start.8 = (bf16[832,512]{1,0:T(8,128)(2,1)}, bf16[832,512]{1,0:T(8,128)(2,1)}, u32[]{:S(2)}, u32[]{:S(2)}) collective-permute-start(bf16[832,512]{1,0:T(8,128)(2,1)} %panel.6.refs_6_.refs_2_), channel_id=1, source_target_pairs={{0,8},{24,16},{1,9},{25,17},{2,10},{26,18},{3,11},{27,19},{4,12},{... | collective-permute-start | bytes 2555912 | tf_op jit(solution)/shard_map/outer1/ppermute | solution.py:501
  171.3 30.0 %collective-permute-start.13 = (bf16[832,512]{1,0:T(8,128)(2,1)}, bf16[832,512]{1,0:T(8,128)(2,1)}, u32[]{:S(2)}, u32[]{:S(2)}) collective-permute-start(bf16[832,512]{1,0:T(8,128)(2,1)} %panel.6.refs_6_.refs_2_), channel_id=1, source_target_pairs={{8,16},{16,8},{9,17},{17,9},{10,18},{18,10},{11,19},{19,11},{12,20... | collective-permute-start | bytes 2555912 | tf_op jit(solution)/shard_map/mate1/ppermute | solution.py:503
  177.3 40.8 %collective-permute-start.16 = (bf16[832,512]{1,0:T(8,128)(2,1)}, bf16[832,512]{1,0:T(8,128)(2,1)}, u32[]{:S(2)}, u32[]{:S(2)}) collective-permute-start(bf16[832,512]{1,0:T(8,128)(2,1)} %collective-permute-done.8.refs_7_), channel_id=1, source_target_pairs={{8,16},{16,8},{9,17},{17,9},{10,18},{18,10},{11,19},{19,11},{12,20... | collective-permute-start | bytes 2555912 | tf_op jit(solution)/shard_map/far1/ppermute | solution.py:508
  178.9 57.7 %collective-permute-start.18 = (bf16[1280,512]{1,0:T(8,128)(2,1)}, bf16[1280,512]{1,0:T(8,128)(2,1)S(1)}, u32[]{:S(2)}, u32[]{:S(2)}) collective-permute-start(bf16[1280,512]{1,0:T(8,128)(2,1)} %get-tuple-element.72), channel_id=1, source_target_pairs={{8,0},{16,24},{9,1},{17,25},{10,2},{18,26},{11,3},{19,27},{12,4},{... | collective-permute-start | bytes 3932168 | tf_op jit(solution)/shard_map/sums0/ppermute | solution.py:521
  180.2 37.1 %collective-permute-start.15 = (bf16[832,384]{1,0:T(8,128)(2,1)}, bf16[832,384]{1,0:T(8,128)(2,1)}, u32[]{:S(2)}, u32[]{:S(2)}) collective-permute-start(bf16[832,384]{1,0:T(8,128)(2,1)} %panel.7.refs_6_.refs_2_), channel_id=1, source_target_pairs={{0,8},{24,16},{1,9},{25,17},{2,10},{26,18},{3,11},{27,19},{4,12},{... | collective-permute-start | bytes 1916936 | tf_op jit(solution)/shard_map/outer2/ppermute | solution.py:501
  199.8 19.9 %collective-permute-start.17 = (bf16[832,384]{1,0:T(8,128)(2,1)}, bf16[832,384]{1,0:T(8,128)(2,1)}, u32[]{:S(2)}, u32[]{:S(2)}) collective-permute-start(bf16[832,384]{1,0:T(8,128)(2,1)} %panel.7.refs_6_.refs_2_), channel_id=1, source_target_pairs={{8,16},{16,8},{9,17},{17,9},{10,18},{18,10},{11,19},{19,11},{12,20... | collective-permute-start | bytes 1916936 | tf_op jit(solution)/shard_map/mate2/ppermute | solution.py:503
  217.4 48.9 %collective-permute-start.20 = (bf16[832,512]{1,0:T(8,128)(2,1)}, bf16[832,512]{1,0:T(8,128)(2,1)S(1)}, u32[]{:S(2)}, u32[]{:S(2)}) collective-permute-start(bf16[832,512]{1,0:T(8,128)(2,1)} %panel.8.refs_6_.refs_2_), channel_id=1, source_target_pairs={{8,16},{16,8},{9,17},{17,9},{10,18},{18,10},{11,19},{19,11},{12,20... | collective-permute-start | bytes 2555912 | tf_op jit(solution)/shard_map/mate3/ppermute | solution.py:503
  218.1 56.1 %collective-permute-start.21 = (bf16[832,384]{1,0:T(8,128)(2,1)}, bf16[832,384]{1,0:T(8,128)(2,1)S(1)}, u32[]{:S(2)}, u32[]{:S(2)}) collective-permute-start(bf16[832,384]{1,0:T(8,128)(2,1)} %collective-permute-done.15.refs_7_), channel_id=1, source_target_pairs={{8,16},{16,8},{9,17},{17,9},{10,18},{18,10},{11,19},{19,11},{12,20... | collective-permute-start | bytes 1916936 | tf_op jit(solution)/shard_map/far2/ppermute | solution.py:508
  219.7 70.8 %collective-permute-start.24 = (bf16[1280,512]{1,0:T(8,128)(2,1)}, bf16[1280,512]{1,0:T(8,128)(2,1)S(1)}, u32[]{:S(2)}, u32[]{:S(2)}) collective-permute-start(bf16[1280,512]{1,0:T(8,128)(2,1)} %get-tuple-element.80), channel_id=1, source_target_pairs={{8,0},{16,24},{9,1},{17,25},{10,2},{18,26},{11,3},{19,27},{12,4},{... | collective-permute-start | bytes 3932168 | tf_op jit(solution)/shard_map/sums1/ppermute | solution.py:521
  235.8 41.5 %collective-permute-start.22 = (bf16[832,512]{1,0:T(8,128)(2,1)S(1)}, bf16[832,512]{1,0:T(8,128)(2,1)S(1)}, u32[]{:S(2)}, u32[]{:S(2)}) collective-permute-start(bf16[832,512]{1,0:T(8,128)(2,1)S(1)} %collective-permute-done.14.refs_7_), channel_id=1, source_target_pairs={{8,16},{16,8},{9,17},{17,9},{10,18},{18,10},{11,19},{19,11},{12,20... | collective-permute-start | bytes 2555912 | tf_op jit(solution)/shard_map/far3/ppermute | solution.py:508
  259.4 24.3 %collective-permute-start.19 = (bf16[832,512]{1,0:T(8,128)(2,1)}, bf16[832,512]{1,0:T(8,128)(2,1)S(1)}, u32[]{:S(2)}, u32[]{:S(2)}) collective-permute-start(bf16[832,512]{1,0:T(8,128)(2,1)} %get-tuple-element.100.refs_6_.refs_2_), channel_id=1, source_target_pairs={{0,8},{24,16},{1,9},{25,17},{2,10},{26,18},{3,11},{27,19},{4,12},{... | collective-permute-start | bytes 2555912 | tf_op jit(solution)/shard_map/outer4/ppermute | solution.py:501
  266.3 47.2 %collective-permute-start.25 = (bf16[832,512]{1,0:T(8,128)(2,1)}, bf16[832,512]{1,0:T(8,128)(2,1)S(1)}, u32[]{:S(2)}, u32[]{:S(2)}) collective-permute-start(bf16[832,512]{1,0:T(8,128)(2,1)} %get-tuple-element.100.refs_6_.refs_2_), channel_id=1, source_target_pairs={{8,16},{16,8},{9,17},{17,9},{10,18},{18,10},{11,19},{19,11},{12,20... | collective-permute-start | bytes 2555912 | tf_op jit(solution)/shard_map/mate4/ppermute | solution.py:503
  276.0 29.4 %collective-permute-start.27 = (bf16[1280,384]{1,0:T(8,128)(2,1)}, bf16[1280,384]{1,0:T(8,128)(2,1)S(1)}, u32[]{:S(2)}, u32[]{:S(2)}) collective-permute-start(bf16[1280,384]{1,0:T(8,128)(2,1)} %get-tuple-element.90), channel_id=1, source_target_pairs={{8,0},{16,24},{9,1},{17,25},{10,2},{18,26},{11,3},{19,27},{12,4},{... | collective-permute-start | bytes 2949128 | tf_op jit(solution)/shard_map/sums2/ppermute | solution.py:521
  283.7 31.4 %collective-permute-start.26 = (bf16[832,512]{1,0:T(8,128)(2,1)S(1)}, bf16[832,512]{1,0:T(8,128)(2,1)S(1)}, u32[]{:S(2)}, u32[]{:S(2)}) collective-permute-start(bf16[832,512]{1,0:T(8,128)(2,1)S(1)} %collective-permute-done.19.refs_7_), channel_id=1, source_target_pairs={{8,16},{16,8},{9,17},{17,9},{10,18},{18,10},{11,19},{19,11},{12,20... | collective-permute-start | bytes 2555912 | tf_op jit(solution)/shard_map/far4/ppermute | solution.py:508
  284.4 30.0 %collective-permute-start.23 = (bf16[832,384]{1,0:T(8,128)(2,1)S(1)}, bf16[832,384]{1,0:T(8,128)(2,1)S(1)}, u32[]{:S(2)}, u32[]{:S(2)}) collective-permute-start(bf16[832,384]{1,0:T(8,128)(2,1)S(1)} %copy-done.1), channel_id=1, source_target_pairs={{0,8},{24,16},{1,9},{25,17},{2,10},{26,18},{3,11},{27,19},{4,12},{... | collective-permute-start | bytes 1916936 | tf_op jit(solution)/shard_map/outer5/ppermute | solution.py:501
  290.5 27.7 %collective-permute-start.28 = (bf16[832,384]{1,0:T(8,128)(2,1)S(1)}, bf16[832,384]{1,0:T(8,128)(2,1)S(1)}, u32[]{:S(2)}, u32[]{:S(2)}) collective-permute-start(bf16[832,384]{1,0:T(8,128)(2,1)S(1)} %copy-done.1), channel_id=1, source_target_pairs={{8,16},{16,8},{9,17},{17,9},{10,18},{18,10},{11,19},{19,11},{12,20... | collective-permute-start | bytes 1916936 | tf_op jit(solution)/shard_map/mate5/ppermute | solution.py:503
  305.4 33.8 %collective-permute-start.32 = (bf16[1280,512]{1,0:T(8,128)(2,1)}, bf16[1280,512]{1,0:T(8,128)(2,1)S(1)}, u32[]{:S(2)}, u32[]{:S(2)}) collective-permute-start(bf16[1280,512]{1,0:T(8,128)(2,1)} %get-tuple-element.98), channel_id=1, source_target_pairs={{8,0},{16,24},{9,1},{17,25},{10,2},{18,26},{11,3},{19,27},{12,4},{... | collective-permute-start | bytes 3932168 | tf_op jit(solution)/shard_map/sums3/ppermute | solution.py:521
  316.9 50.4 %collective-permute-start.31 = (bf16[1280,512]{1,0:T(8,128)(2,1)}, bf16[1280,512]{1,0:T(8,128)(2,1)S(1)}, u32[]{:S(2)}, u32[]{:S(2)}) collective-permute-start(bf16[1280,512]{1,0:T(8,128)(2,1)} %get-tuple-element.105), channel_id=1, source_target_pairs={{8,0},{16,24},{9,1},{17,25},{10,2},{18,26},{11,3},{19,27},{12,4},{... | collective-permute-start | bytes 3932168 | tf_op jit(solution)/shard_map/sums4/ppermute | solution.py:521
  321.0 64.9 %collective-permute-start.30 = (bf16[1280,384]{1,0:T(8,128)(2,1)}, bf16[1280,384]{1,0:T(8,128)(2,1)S(1)}, u32[]{:S(2)}, u32[]{:S(2)}) collective-permute-start(bf16[1280,384]{1,0:T(8,128)(2,1)} %products.12), channel_id=1, source_target_pairs={{8,0},{16,24},{9,1},{17,25},{10,2},{18,26},{11,3},{19,27},{12,4},{... | collective-permute-start | bytes 2949128 | tf_op jit(solution)/shard_map/sums5/ppermute | solution.py:521
  (26 other events, 170.3 us)
Sparse Core Ops, SparseCore 0:
  11.5 94.6 all-gather.4
  108.1 85.9 all-gather.6

commit v5 on v4

--- a/solution.py
+++ b/solution.py
@@ -300,7 +300,7 @@
         ),
         input_output_aliases=aliases,
         compiler_params=pltpu.CompilerParams(vmem_limit_bytes=VMEM_LIMIT),
-        cost_estimate=pl.CostEstimate(flops=3 * (sending + keeping) * (count + extra) * depth * wide, bytes_accessed=0, transcendentals=0),
+        cost_estimate=pl.CostEstimate(flops=(6 if sending and keeping else 6) * (count + extra) * depth * wide, bytes_accessed=0, transcendentals=0),
         name="products",
     )(slots, *args)
 
@@ -562,14 +562,16 @@
     forward(4, out[2], far[3])
     send(5, outer[4])
     conclude(1)
-    multiply(3, outer[4])
+    multiply(3, outer[4], keeping=False)
     forward(5, out[3], mate[4])
     conclude(2)
-    multiply(4, outer[5])
+    multiply(4, outer[5], keeping=False)
+    multiply(3, out[4], sending=False)
+    multiply(5, own[3], received[3], keeping=False)
+    last_product = own_product(slots, mine, after(own[5], out[5]))
     conclude(3)
-    multiply(5, out[4], keeping=False)
+    multiply(4, out[5], sending=False)
     multiply(5, out[5], sending=False)
-    last_product = own_product(slots, mine, after(own[5], out[5]))
     conclude(4)
     conclude(5, last_product)
     return jnp.swapaxes(grown, 1, 2), hidden.T

time: 406 us -> 407 us (level)
    pallas_call x7 -> x9, Pallas kernels: 6.9 us -> 8.31 us  [products(): pl.pallas_call(functools.partial(products_kernel, m, start, width, sendin...]
    unnamed x46 -> x48, local copies, waits for them, and re-layouts: 9.15 us -> 8.97 us
  transfers between devices with their start and end apart: 36 -> 36, of which waited for: 11 -> 11; matrix products, arithmetic and copies ran while one was open for 5% -> 4% of each run, Pallas kernels for 33% -> 33%
where the time goes in v5:
time: 407 us; the launch traced here: 399 us
  Pallas kernels  136 us (33%)
  waiting for transfers between devices  114 us (28%)
  starting transfers between devices  80 us (20%)
  blocking collectives  25.2 us (6%)
  local copies, waits for them, and re-layouts  16.4 us (4%)
  between operations  15.3 us (4%)
  other arithmetic  7.75 us (2%)
  matrix products  4.93 us (1%)
    pallas_call x5, Pallas kernels, panel_of(): pl.pallas_call(functools.partial(panel_kernel, steps, splits), out_shape=...  81.2 us
    ppermute x6, waiting for transfers between devices, multiply(): received[k] = lax.ppermute(out[k], 'dp', TO_OUTER)  45.1 us
    ppermute x6, starting transfers between devices, send(): outer[k] = lax.ppermute(sent, 'dp', TO_INNER)  40.1 us
    pallas_call x6, Pallas kernels, finish(): pl.pallas_call(functools.partial(finish_kernel, m, start, width, made is...  39.7 us
    ppermute x6, waiting for transfers between devices, send(): outer[k] = lax.ppermute(sent, 'dp', TO_INNER)  26.3 us
    all_to_all x1, waiting for transfers between devices, token_rows(): parts = lax.all_to_all(part, 'dp', 0, 0, tiled=True)  20.2 us
    ppermute x4, waiting for transfers between devices, fetch_half(): fetched.append(lax.ppermute(after(part, *fetched[-1:]), 'dp', TO_INNER))  16.6 us
    all_to_all x1, blocking collectives, token_rows(): by_rows = lax.all_to_all(tokens, 'tensor', 0, 1, tiled=True)  13.2 us
  transfers between devices with their start and end apart: 36, of which 11 were waited for; matrix products, arithmetic and copies ran while one was open for 4% of the time, Pallas kernels for 33%

profile of v5, /device:TPU:0, one launch (start us, length us, event | category | flops | bytes accessed | tf_op | source)
XLA Modules:
  0.0 399.2 jit_solution(4135977582266284148)
XLA Ops:
  7.2 4.2 %fusion.7 = (bf16[1,104,8960]{2,1,0:T(8,128)(2,1)}, bf16[1,104,8960]{2,1,0:T(8,128)(2,1)}) fusion(bf16[2,104,8960]{2,1,0:T(8,128)(2,1)} %param.6), kind=kLoop, calls=%fused_computation.31 | loop fusion | bytes 7454720 | tf_op jit(solution)/shard_map/slice | solution.py:481
  14.0 5.0 %collective-permute-start = (bf16[176,2560]{1,0:T(8,128)(2,1)S(1)}, bf16[176,2560]{1,0:T(8,128)(2,1)S(1)}, u32[]{:S(2)}, u32[]{:S(2)}) collective-permute-start(bf16[176,2560]{1,0:T(8,128)(2,1)S(1)} %get-tuple-element.119), channel_id=1, source_target_pairs={{0,8},{24,16},{1,9},{25,17},{2,10},{26,18},{3,11},{27,19},{4,12},{... | collective-permute-start | bytes 2703368 | tf_op jit(solution)/shard_map/ppermute | solution.py:469
  19.0 13.2 %all_to_all.44 = bf16[8,32,512]{2,1,0:T(8,128)(2,1)S(1)} all-to-all(bf16[8,32,512]{2,1,0:T(8,128)(2,1)S(1)} %bitcast.24), channel_id=1, replica_groups=mesh['dp'=4,'tensor'=8] {'tensor'}, dimensions={0} | all-to-all | bytes 524288 | tf_op jit(solution)/shard_map/all_to_all | solution.py:27
  32.7 12.0 %all_to_all.45 = bf16[32,4,1024]{2,0,1:T(8,128)(2,1)S(1)} all-to-all(bf16[32,4,1024]{2,0,1:T(8,128)(2,1)S(1)} %copy.31), channel_id=1, replica_groups=mesh['dp'=4,'tensor'=8] {'dp'}, dimensions={1} | all-to-all | bytes 524288 | tf_op jit(solution)/shard_map/all_to_all | solution.py:28
  44.7 4.9 %convolution_convert_fusion = bf16[128,3328]{1,0:T(8,128)(2,1)} fusion(bf16[128,1024]{1,0:T(8,128)(2,1)S(1)} %bitcast.22, bf16[1024,3328]{1,0:T(8,128)(2,1)} %refs_0_.9), kind=kOutput, calls=%fused_computation | convolution fusion | flops 872841216 | bytes 7929856 | tf_op jit(solution)/shard_map/dot_general | solution.py:30
  53.1 20.2 %all-to-all-done.2 = bf16[4,32,3328]{2,1,0:T(8,128)(2,1)S(1)} async-done(((bf16[4,32,3328]{2,1,0:T(8,128)(2,1)}), bf16[4,32,3328]{2,1,0:T(8,128)(2,1)S(1)}, u32[]{:S(2)}, u32[]{:S(2)}) %all-to-all-start.2) | async-done | bytes 852000 | tf_op jit(solution)/shard_map/all_to_all | solution.py:31
  80.4 16.6 %collective-permute-done.4 = bf16[176,2560]{1,0:T(8,128)(2,1)S(1)} collective-permute-done((bf16[176,2560]{1,0:T(8,128)(2,1)S(1)}, bf16[176,2560]{1,0:T(8,128)(2,1)S(1)}, u32[]{:S(2)}, u32[]{:S(2)}) %collective-permute-start.4) | collective-permute-done | bytes 901152 | tf_op jit(solution)/shard_map/ppermute | solution.py:469
  97.0 5.3 %collective-permute-start.5 = (bf16[160,2560]{1,0:T(8,128)(2,1)S(1)}, bf16[160,2560]{1,0:T(8,128)(2,1)}, u32[]{:S(2)}, u32[]{:S(2)}) collective-permute-start(bf16[160,2560]{1,0:T(8,128)(2,1)S(1)} %fusion.2), channel_id=1, source_target_pairs={{0,8},{24,16},{1,9},{25,17},{2,10},{26,18},{3,11},{27,19},{4,12},{... | collective-permute-start | bytes 2457608 | tf_op jit(solution)/shard_map/ppermute | solution.py:469
  106.3 15.2 %panel.5.refs_6_.refs_2_ = bf16[832,512]{1,0:T(8,128)(2,1)} custom-call(bf16[832,8960]{1,0:T(8,128)(2,1)} %bitcast.18, bf16[1376,8960]{1,0:T(8,128)(2,1)} %growth_ref.9), custom_call_target="tpu_custom_call" | custom-call | flops 11450449920 | tf_op jit(solution)/shard_map/panel/pallas_call | solution.py:107
  121.5 4.2 %collective-permute-start.6 = (bf16[832,512]{1,0:T(8,128)(2,1)}, bf16[832,512]{1,0:T(8,128)(2,1)}, u32[]{:S(2)}, u32[]{:S(2)}) collective-permute-start(bf16[832,512]{1,0:T(8,128)(2,1)} %panel.5.refs_6_.refs_2_), channel_id=1, source_target_pairs={{0,8},{24,16},{1,9},{25,17},{2,10},{26,18},{3,11},{27,19},{4,12},{... | collective-permute-start | bytes 2555912 | tf_op jit(solution)/shard_map/outer0/ppermute | solution.py:501
  126.4 3.6 collective-permute-done.3
  135.5 14.7 %panel.6.refs_6_.refs_2_ = bf16[832,512]{1,0:T(8,128)(2,1)} custom-call(bf16[832,8960]{1,0:T(8,128)(2,1)} %bitcast.19, bf16[1376,8960]{1,0:T(8,128)(2,1)} %growth_ref.9), custom_call_target="tpu_custom_call" | custom-call | flops 11450449920 | tf_op jit(solution)/shard_map/panel/pallas_call | solution.py:107
  153.6 13.9 %panel.7.refs_6_.refs_2_ = bf16[832,384]{1,0:T(8,128)(2,1)} custom-call(bf16[832,8960]{1,0:T(8,128)(2,1)} %bitcast.20, bf16[1376,8960]{1,0:T(8,128)(2,1)} %growth_ref.9), custom_call_target="tpu_custom_call" | custom-call | flops 8587837440 | tf_op jit(solution)/shard_map/panel/pallas_call | solution.py:107
  170.7 5.3 %collective-permute-done.8.refs_7_ = bf16[832,512]{1,0:T(8,128)(2,1)} collective-permute-done((bf16[832,512]{1,0:T(8,128)(2,1)}, bf16[832,512]{1,0:T(8,128)(2,1)}, u32[]{:S(2)}, u32[]{:S(2)}) %collective-permute-start.8) | collective-permute-done | bytes 852000 | tf_op jit(solution)/shard_map/outer1/ppermute | solution.py:501
  181.1 18.8 %collective-permute-start.15 = (bf16[832,384]{1,0:T(8,128)(2,1)S(1)}, bf16[832,384]{1,0:T(8,128)(2,1)S(1)}, u32[]{:S(2)}, u32[]{:S(2)}) collective-permute-start(bf16[832,384]{1,0:T(8,128)(2,1)S(1)} %copy-done), channel_id=1, source_target_pairs={{0,8},{24,16},{1,9},{25,17},{2,10},{26,18},{3,11},{27,19},{4,12},{... | collective-permute-start | bytes 1916936 | tf_op jit(solution)/shard_map/outer2/ppermute | solution.py:501
  201.4 14.6 %panel.8.refs_6_.refs_2_ = bf16[832,512]{1,0:T(8,128)(2,1)} custom-call(bf16[832,8960]{1,0:T(8,128)(2,1)} %bitcast.25, bf16[1376,8960]{1,0:T(8,128)(2,1)} %growth_ref.9), custom_call_target="tpu_custom_call" | custom-call | flops 11450449920 | tf_op jit(solution)/shard_map/panel/pallas_call | solution.py:107
  221.9 14.6 %collective-permute-done.14.refs_7_ = bf16[832,512]{1,0:T(8,128)(2,1)S(1)} collective-permute-done((bf16[832,512]{1,0:T(8,128)(2,1)}, bf16[832,512]{1,0:T(8,128)(2,1)S(1)}, u32[]{:S(2)}, u32[]{:S(2)}) %collective-permute-start.14) | collective-permute-done | bytes 852000 | tf_op jit(solution)/shard_map/outer3/ppermute | solution.py:501
  238.3 22.8 %panel.9 = (bf16[832,512]{1,0:T(8,128)(2,1)}, bf16[832,384]{1,0:T(8,128)(2,1)}) custom-call(bf16[832,8960]{1,0:T(8,128)(2,1)} %bitcast.26, bf16[1376,8960]{1,0:T(8,128)(2,1)} %growth_ref.9), custom_call_target="tpu_custom_call" | custom-call | flops 20038287360 | tf_op jit(solution)/shard_map/panel/pallas_call | solution.py:107
  261.1 6.1 %collective-permute-start.19 = (bf16[832,512]{1,0:T(8,128)(2,1)}, bf16[832,512]{1,0:T(8,128)(2,1)S(1)}, u32[]{:S(2)}, u32[]{:S(2)}) collective-permute-start(bf16[832,512]{1,0:T(8,128)(2,1)} %get-tuple-element.103.refs_6_.refs_2_), channel_id=1, source_target_pairs={{0,8},{24,16},{1,9},{25,17},{2,10},{26,18},{3,11},{27,19},{4,12},{... | collective-permute-start | bytes 2555912 | tf_op jit(solution)/shard_map/outer4/ppermute | solution.py:501
  268.0 7.2 %finish.6 = (bf16[2,1376,1024]{2,1,0:T(8,128)(2,1)}, f32[256,1408]{1,0:T(8,128)}) custom-call(s32[7]{0:T(128)} %pad_add_fusion.slots_ref, bf16[1024,3328]{1,0:T(8,128)(2,1)} %refs_0_.9, bf16[256,3328]{1,0:T(8,128)(2,1)} %pad_maximum_fusion.refs_5_.refs_1_.tokens_ref, ...), custom_call_target="tpu_custom_call", output_to_operand_aliasing={{0}: (6, {}), {1}: (5, {})} | custom-call | tf_op jit(solution)/shard_map/finish/pallas_call | solution.py:429
  278.3 6.4 %collective-permute-done.19.refs_7_ = bf16[832,512]{1,0:T(8,128)(2,1)S(1)} collective-permute-done((bf16[832,512]{1,0:T(8,128)(2,1)}, bf16[832,512]{1,0:T(8,128)(2,1)S(1)}, u32[]{:S(2)}, u32[]{:S(2)}) %collective-permute-start.19) | collective-permute-done | bytes 852000 | tf_op jit(solution)/shard_map/outer4/ppermute | solution.py:501
  285.4 6.1 %collective-permute-start.24 = (bf16[832,384]{1,0:T(8,128)(2,1)S(1)}, bf16[832,384]{1,0:T(8,128)(2,1)S(1)}, u32[]{:S(2)}, u32[]{:S(2)}) collective-permute-start(bf16[832,384]{1,0:T(8,128)(2,1)S(1)} %copy-done.8), channel_id=1, source_target_pairs={{0,8},{24,16},{1,9},{25,17},{2,10},{26,18},{3,11},{27,19},{4,12},{... | collective-permute-start | bytes 1916936 | tf_op jit(solution)/shard_map/outer5/ppermute | solution.py:501
  292.6 7.2 %finish.7 = (bf16[2,1376,1024]{2,1,0:T(8,128)(2,1)}, f32[256,1408]{1,0:T(8,128)}) custom-call(s32[7]{0:T(128)} %pad_add_fusion.slots_ref, bf16[1024,3328]{1,0:T(8,128)(2,1)} %refs_0_.9, bf16[256,3328]{1,0:T(8,128)(2,1)} %pad_maximum_fusion.refs_5_.refs_1_.tokens_ref, ...), custom_call_target="tpu_custom_call", output_to_operand_aliasing={{0}: (6, {}), {1}: (5, {})} | custom-call | tf_op jit(solution)/shard_map/finish/pallas_call | solution.py:429
  300.8 5.6 %collective-permute-done.29.refs_3_ = bf16[1280,384]{1,0:T(8,128)(2,1)S(1)} collective-permute-done((bf16[1280,384]{1,0:T(8,128)(2,1)}, bf16[1280,384]{1,0:T(8,128)(2,1)S(1)}, u32[]{:S(2)}, u32[]{:S(2)}) %collective-permute-start.29) | collective-permute-done | bytes 983072 | tf_op jit(solution)/shard_map/sums2/ppermute | solution.py:521
  307.7 6.8 %finish.8 = (bf16[2,1376,1024]{2,1,0:T(8,128)(2,1)}, f32[256,1408]{1,0:T(8,128)}) custom-call(s32[7]{0:T(128)} %pad_add_fusion.slots_ref, bf16[1024,3328]{1,0:T(8,128)(2,1)} %refs_0_.9, bf16[256,3328]{1,0:T(8,128)(2,1)} %pad_maximum_fusion.refs_5_.refs_1_.tokens_ref, ...), custom_call_target="tpu_custom_call", output_to_operand_aliasing={{0}: (6, {}), {1}: (5, {})} | custom-call | tf_op jit(solution)/shard_map/finish/pallas_call | solution.py:429
  319.3 20.9 %collective-permute-done.23.refs_3_ = bf16[1280,512]{1,0:T(8,128)(2,1)S(1)} collective-permute-done((bf16[1280,512]{1,0:T(8,128)(2,1)}, bf16[1280,512]{1,0:T(8,128)(2,1)S(1)}, u32[]{:S(2)}, u32[]{:S(2)}) %collective-permute-start.23) | collective-permute-done | bytes 1310752 | tf_op jit(solution)/shard_map/sums3/ppermute | solution.py:521
  344.1 7.5 %finish.9 = (bf16[2,1376,1024]{2,1,0:T(8,128)(2,1)}, bf16[1376,256]{1,0:T(8,128)(2,1)}) custom-call(s32[7]{0:T(128)} %pad_add_fusion.slots_ref, bf16[1024,3328]{1,0:T(8,128)(2,1)} %refs_0_.9, bf16[256,3328]{1,0:T(8,128)(2,1)} %pad_maximum_fusion.refs_5_.refs_1_.tokens_ref, ...), custom_call_target="tpu_custom_call", output_to_operand_aliasing={{0}: (6, {}), {1}: (7, {})} | custom-call | tf_op jit(solution)/shard_map/finish/pallas_call | solution.py:429
  352.5 6.8 %own_product.1.refs_0_ = f32[1280,384]{1,0:T(8,128)} custom-call(s32[7]{0:T(128)} %pad_add_fusion.slots_ref, bf16[1024,3328]{1,0:T(8,128)(2,1)} %refs_0_.9, bf16[256,3328]{1,0:T(8,128)(2,1)} %pad_maximum_fusion.refs_5_.refs_1_.tokens_ref, bf16[832,384]{1,0:T(8,128)(2,1)} %get-tuple-element.96.refs_6_.own_ref), custom_call_target="tpu_custom_call" | custom-call | tf_op jit(solution)/shard_map/own_product/pallas_call | solution.py:341
  360.2 8.2 %collective-permute-done.32.refs_3_ = bf16[1280,512]{1,0:T(8,128)(2,1)S(1)} collective-permute-done((bf16[1280,512]{1,0:T(8,128)(2,1)}, bf16[1280,512]{1,0:T(8,128)(2,1)S(1)}, u32[]{:S(2)}, u32[]{:S(2)}) %collective-permute-start.32) | collective-permute-done | bytes 1310752 | tf_op jit(solution)/shard_map/sums4/ppermute | solution.py:521
  369.4 7.3 %finish.10 = (bf16[2,1376,1024]{2,1,0:T(8,128)(2,1)}, bf16[1376,256]{1,0:T(8,128)(2,1)}) custom-call(s32[7]{0:T(128)} %pad_add_fusion.slots_ref, bf16[1024,3328]{1,0:T(8,128)(2,1)} %refs_0_.9, bf16[256,3328]{1,0:T(8,128)(2,1)} %pad_maximum_fusion.refs_5_.refs_1_.tokens_ref, ...), custom_call_target="tpu_custom_call", output_to_operand_aliasing={{0}: (6, {}), {1}: (7, {})} | custom-call | tf_op jit(solution)/shard_map/finish/pallas_call | solution.py:429
  376.6 10.4 %collective-permute-done.28.refs_1_ = bf16[1280,384]{1,0:T(8,128)(2,1)S(1)} collective-permute-done((bf16[1280,384]{1,0:T(8,128)(2,1)}, bf16[1280,384]{1,0:T(8,128)(2,1)S(1)}, u32[]{:S(2)}, u32[]{:S(2)}) %collective-permute-start.28) | collective-permute-done | bytes 983072 | tf_op jit(solution)/shard_map/sums5/ppermute | solution.py:521
  388.0 3.8 finish.11
  (133 shorter events, 64.6 us)
Async XLA Ops:
  7.2 99.1 %all-gather.5.cloned.1.call-start = ((), (), s32[]{:S(2)}) async-start(), calls=%async_computation.3 | async-start | bytes 16773120 | tf_op jit(solution)/shard_map/all_gather | solution.py:481
  11.4 190.0 %all-gather.7.cloned.1.call-start = ((), (), s32[]{:S(2)}) async-start(), calls=%async_computation.4 | async-start | bytes 16773120 | tf_op jit(solution)/shard_map/all_gather | solution.py:481
  14.0 30.6 %collective-permute-start = (bf16[176,2560]{1,0:T(8,128)(2,1)S(1)}, bf16[176,2560]{1,0:T(8,128)(2,1)S(1)}, u32[]{:S(2)}, u32[]{:S(2)}) collective-permute-start(bf16[176,2560]{1,0:T(8,128)(2,1)S(1)} %get-tuple-element.119), channel_id=1, source_target_pairs={{0,8},{24,16},{1,9},{25,17},{2,10},{26,18},{3,11},{27,19},{4,12},{... | collective-permute-start | bytes 2703368 | tf_op jit(solution)/shard_map/ppermute | solution.py:469
  49.6 23.7 %all-to-all-start.2 = ((bf16[4,32,3328]{2,1,0:T(8,128)(2,1)}), bf16[4,32,3328]{2,1,0:T(8,128)(2,1)S(1)}, u32[]{:S(2)}, u32[]{:S(2)}) async-start(bf16[4,32,3328]{2,1,0:T(8,128)(2,1)} %bitcast.8), calls=%async_computation.2 | async-start | bytes 1703936 | tf_op jit(solution)/shard_map/all_to_all | solution.py:31
  75.5 21.5 %collective-permute-start.4 = (bf16[176,2560]{1,0:T(8,128)(2,1)S(1)}, bf16[176,2560]{1,0:T(8,128)(2,1)S(1)}, u32[]{:S(2)}, u32[]{:S(2)}) collective-permute-start(bf16[176,2560]{1,0:T(8,128)(2,1)S(1)} %get-tuple-element.61), channel_id=1, source_target_pairs={{0,8},{24,16},{1,9},{25,17},{2,10},{26,18},{3,11},{27,19},{4,12},{... | collective-permute-start | bytes 2703368 | tf_op jit(solution)/shard_map/ppermute | solution.py:469
  77.9 25.5 %collective-permute-start.2 = (bf16[64,3328]{1,0:T(8,128)(2,1)S(1)}, bf16[64,3328]{1,0:T(8,128)(2,1)S(1)}, u32[]{:S(2)}, u32[]{:S(2)}) collective-permute-start(bf16[64,3328]{1,0:T(8,128)(2,1)S(1)} %pad_maximum_fusion.2), channel_id=1, source_target_pairs={{0,2},{1,3},{2,0},{3,1},{4,6},{5,7},{6,4},{7,5},{8,10},{9,11},{10,... | collective-permute-start | bytes 1277960 | tf_op jit(solution)/shard_map/ppermute | solution.py:36
  97.0 29.4 %collective-permute-start.5 = (bf16[160,2560]{1,0:T(8,128)(2,1)S(1)}, bf16[160,2560]{1,0:T(8,128)(2,1)}, u32[]{:S(2)}, u32[]{:S(2)}) collective-permute-start(bf16[160,2560]{1,0:T(8,128)(2,1)S(1)} %fusion.2), channel_id=1, source_target_pairs={{0,8},{24,16},{1,9},{25,17},{2,10},{26,18},{3,11},{27,19},{4,12},{... | collective-permute-start | bytes 2457608 | tf_op jit(solution)/shard_map/ppermute | solution.py:469
  103.5 26.5 %collective-permute-start.3 = (bf16[128,3328]{1,0:T(8,128)(2,1)S(1)}, bf16[128,3328]{1,0:T(8,128)(2,1)S(1)}, u32[]{:S(2)}, u32[]{:S(2)}) collective-permute-start(bf16[128,3328]{1,0:T(8,128)(2,1)S(1)} %pad_maximum_fusion.1), channel_id=1, source_target_pairs={{0,4},{1,5},{2,6},{3,7},{4,0},{5,1},{6,2},{7,3},{8,12},{9,13},{10,... | collective-permute-start | bytes 2555912 | tf_op jit(solution)/shard_map/ppermute | solution.py:36
  121.5 28.6 %collective-permute-start.6 = (bf16[832,512]{1,0:T(8,128)(2,1)}, bf16[832,512]{1,0:T(8,128)(2,1)}, u32[]{:S(2)}, u32[]{:S(2)}) collective-permute-start(bf16[832,512]{1,0:T(8,128)(2,1)} %panel.5.refs_6_.refs_2_), channel_id=1, source_target_pairs={{0,8},{24,16},{1,9},{25,17},{2,10},{26,18},{3,11},{27,19},{4,12},{... | collective-permute-start | bytes 2555912 | tf_op jit(solution)/shard_map/outer0/ppermute | solution.py:501
  125.7 24.5 %collective-permute-start.7 = (bf16[832,512]{1,0:T(8,128)(2,1)}, bf16[832,512]{1,0:T(8,128)(2,1)S(1)}, u32[]{:S(2)}, u32[]{:S(2)}) collective-permute-start(bf16[832,512]{1,0:T(8,128)(2,1)} %panel.5.refs_6_.refs_2_), channel_id=1, source_target_pairs={{8,16},{16,8},{9,17},{17,9},{10,18},{18,10},{11,19},{19,11},{12,20... | collective-permute-start | bytes 2555912 | tf_op jit(solution)/shard_map/mate0/ppermute | solution.py:503
  132.1 43.9 %collective-permute-start.9 = (bf16[512,2560]{1,0:T(8,128)(2,1)}, bf16[512,2560]{1,0:T(8,128)(2,1)}, u32[]{:S(2)}, u32[]{:S(2)}) collective-permute-start(bf16[512,2560]{1,0:T(8,128)(2,1)} %constant_dynamic-update-slice_fusion.refs_0_), channel_id=1, source_target_pairs={{0,1},{1,0},{2,3},{3,2},{4,5},{5,4},{6,7},{7,6},{8,9},{9,8},{10,11... | collective-permute-start | bytes 7864328 | tf_op jit(solution)/shard_map/ppermute | solution.py:36
  134.1 33.4 %collective-permute-start.10 = (bf16[128,2560]{1,0:T(8,128)(2,1)S(1)}, bf16[128,2560]{1,0:T(8,128)(2,1)S(1)}, u32[]{:S(2)}, u32[]{:S(2)}) collective-permute-start(bf16[128,2560]{1,0:T(8,128)(2,1)S(1)} %fusion.3), channel_id=1, source_target_pairs={{0,8},{24,16},{1,9},{25,17},{2,10},{26,18},{3,11},{27,19},{4,12},{... | collective-permute-start | bytes 1966088 | tf_op jit(solution)/shard_map/ppermute | solution.py:469
  150.2 25.8 %collective-permute-start.12 = (bf16[832,512]{1,0:T(8,128)(2,1)}, bf16[832,512]{1,0:T(8,128)(2,1)S(1)}, u32[]{:S(2)}, u32[]{:S(2)}) collective-permute-start(bf16[832,512]{1,0:T(8,128)(2,1)} %collective-permute-done.6.refs_7_), channel_id=1, source_target_pairs={{8,16},{16,8},{9,17},{17,9},{10,18},{18,10},{11,19},{19,11},{12,20... | collective-permute-start | bytes 2555912 | tf_op jit(solution)/shard_map/far0/ppermute | solution.py:508
  151.0 25.0 %collective-permute-start.8 = (bf16[832,512]{1,0:T(8,128)(2,1)}, bf16[832,512]{1,0:T(8,128)(2,1)}, u32[]{:S(2)}, u32[]{:S(2)}) collective-permute-start(bf16[832,512]{1,0:T(8,128)(2,1)} %panel.6.refs_6_.refs_2_), channel_id=1, source_target_pairs={{0,8},{24,16},{1,9},{25,17},{2,10},{26,18},{3,11},{27,19},{4,12},{... | collective-permute-start | bytes 2555912 | tf_op jit(solution)/shard_map/outer1/ppermute | solution.py:501
  169.0 32.4 %collective-permute-start.13 = (bf16[832,512]{1,0:T(8,128)(2,1)S(1)}, bf16[832,512]{1,0:T(8,128)(2,1)}, u32[]{:S(2)}, u32[]{:S(2)}) collective-permute-start(bf16[832,512]{1,0:T(8,128)(2,1)S(1)} %copy-done.7), channel_id=1, source_target_pairs={{8,16},{16,8},{9,17},{17,9},{10,18},{18,10},{11,19},{19,11},{12,20... | collective-permute-start | bytes 2555912 | tf_op jit(solution)/shard_map/mate1/ppermute | solution.py:503
  178.2 40.8 %collective-permute-start.16 = (bf16[832,512]{1,0:T(8,128)(2,1)}, bf16[832,512]{1,0:T(8,128)(2,1)}, u32[]{:S(2)}, u32[]{:S(2)}) collective-permute-start(bf16[832,512]{1,0:T(8,128)(2,1)} %collective-permute-done.8.refs_7_), channel_id=1, source_target_pairs={{8,16},{16,8},{9,17},{17,9},{10,18},{18,10},{11,19},{19,11},{12,20... | collective-permute-start | bytes 2555912 | tf_op jit(solution)/shard_map/far1/ppermute | solution.py:508
  179.8 58.5 %collective-permute-start.18 = (bf16[1280,512]{1,0:T(8,128)(2,1)}, bf16[1280,512]{1,0:T(8,128)(2,1)S(1)}, u32[]{:S(2)}, u32[]{:S(2)}) collective-permute-start(bf16[1280,512]{1,0:T(8,128)(2,1)} %get-tuple-element.72), channel_id=1, source_target_pairs={{8,0},{16,24},{9,1},{17,25},{10,2},{18,26},{11,3},{19,27},{12,4},{... | collective-permute-start | bytes 3932168 | tf_op jit(solution)/shard_map/sums0/ppermute | solution.py:521
  181.1 37.2 %collective-permute-start.15 = (bf16[832,384]{1,0:T(8,128)(2,1)S(1)}, bf16[832,384]{1,0:T(8,128)(2,1)S(1)}, u32[]{:S(2)}, u32[]{:S(2)}) collective-permute-start(bf16[832,384]{1,0:T(8,128)(2,1)S(1)} %copy-done), channel_id=1, source_target_pairs={{0,8},{24,16},{1,9},{25,17},{2,10},{26,18},{3,11},{27,19},{4,12},{... | collective-permute-start | bytes 1916936 | tf_op jit(solution)/shard_map/outer2/ppermute | solution.py:501
  218.3 48.9 %collective-permute-start.20 = (bf16[832,512]{1,0:T(8,128)(2,1)}, bf16[832,512]{1,0:T(8,128)(2,1)S(1)}, u32[]{:S(2)}, u32[]{:S(2)}) collective-permute-start(bf16[832,512]{1,0:T(8,128)(2,1)} %panel.8.refs_6_.refs_2_), channel_id=1, source_target_pairs={{8,16},{16,8},{9,17},{17,9},{10,18},{18,10},{11,19},{19,11},{12,20... | collective-permute-start | bytes 2555912 | tf_op jit(solution)/shard_map/mate3/ppermute | solution.py:503
  219.0 56.1 %collective-permute-start.21 = (bf16[832,384]{1,0:T(8,128)(2,1)S(1)}, bf16[832,384]{1,0:T(8,128)(2,1)S(1)}, u32[]{:S(2)}, u32[]{:S(2)}) collective-permute-start(bf16[832,384]{1,0:T(8,128)(2,1)S(1)} %collective-permute-done.15.refs_7_), channel_id=1, source_target_pairs={{8,16},{16,8},{9,17},{17,9},{10,18},{18,10},{11,19},{19,11},{12,20... | collective-permute-start | bytes 1916936 | tf_op jit(solution)/shard_map/far2/ppermute | solution.py:508
  220.6 70.9 %collective-permute-start.30 = (bf16[1280,512]{1,0:T(8,128)(2,1)}, bf16[1280,512]{1,0:T(8,128)(2,1)S(1)}, u32[]{:S(2)}, u32[]{:S(2)}) collective-permute-start(bf16[1280,512]{1,0:T(8,128)(2,1)} %get-tuple-element.80), channel_id=1, source_target_pairs={{8,0},{16,24},{9,1},{17,25},{10,2},{18,26},{11,3},{19,27},{12,4},{... | collective-permute-start | bytes 3932168 | tf_op jit(solution)/shard_map/sums1/ppermute | solution.py:521
  236.5 41.7 %collective-permute-start.22 = (bf16[832,512]{1,0:T(8,128)(2,1)S(1)}, bf16[832,512]{1,0:T(8,128)(2,1)}, u32[]{:S(2)}, u32[]{:S(2)}) collective-permute-start(bf16[832,512]{1,0:T(8,128)(2,1)S(1)} %collective-permute-done.14.refs_7_), channel_id=1, source_target_pairs={{8,16},{16,8},{9,17},{17,9},{10,18},{18,10},{11,19},{19,11},{12,20... | collective-permute-start | bytes 2555912 | tf_op jit(solution)/shard_map/far3/ppermute | solution.py:508
  261.1 23.6 %collective-permute-start.19 = (bf16[832,512]{1,0:T(8,128)(2,1)}, bf16[832,512]{1,0:T(8,128)(2,1)S(1)}, u32[]{:S(2)}, u32[]{:S(2)}) collective-permute-start(bf16[832,512]{1,0:T(8,128)(2,1)} %get-tuple-element.103.refs_6_.refs_2_), channel_id=1, source_target_pairs={{0,8},{24,16},{1,9},{25,17},{2,10},{26,18},{3,11},{27,19},{4,12},{... | collective-permute-start | bytes 2555912 | tf_op jit(solution)/shard_map/outer4/ppermute | solution.py:501
  267.2 47.3 %collective-permute-start.25 = (bf16[832,512]{1,0:T(8,128)(2,1)}, bf16[832,512]{1,0:T(8,128)(2,1)S(1)}, u32[]{:S(2)}, u32[]{:S(2)}) collective-permute-start(bf16[832,512]{1,0:T(8,128)(2,1)} %get-tuple-element.103.refs_6_.refs_2_), channel_id=1, source_target_pairs={{8,16},{16,8},{9,17},{17,9},{10,18},{18,10},{11,19},{19,11},{12,20... | collective-permute-start | bytes 2555912 | tf_op jit(solution)/shard_map/mate4/ppermute | solution.py:503
  277.0 29.5 %collective-permute-start.29 = (bf16[1280,384]{1,0:T(8,128)(2,1)}, bf16[1280,384]{1,0:T(8,128)(2,1)S(1)}, u32[]{:S(2)}, u32[]{:S(2)}) collective-permute-start(bf16[1280,384]{1,0:T(8,128)(2,1)} %get-tuple-element.90), channel_id=1, source_target_pairs={{8,0},{16,24},{9,1},{17,25},{10,2},{18,26},{11,3},{19,27},{12,4},{... | collective-permute-start | bytes 2949128 | tf_op jit(solution)/shard_map/sums2/ppermute | solution.py:521
  284.7 30.6 %collective-permute-start.31 = (bf16[832,512]{1,0:T(8,128)(2,1)S(1)}, bf16[832,512]{1,0:T(8,128)(2,1)S(1)}, u32[]{:S(2)}, u32[]{:S(2)}) collective-permute-start(bf16[832,512]{1,0:T(8,128)(2,1)S(1)} %collective-permute-done.19.refs_7_), channel_id=1, source_target_pairs={{8,16},{16,8},{9,17},{17,9},{10,18},{18,10},{11,19},{19,11},{12,20... | collective-permute-start | bytes 2555912 | tf_op jit(solution)/shard_map/far4/ppermute | solution.py:508
  285.4 29.1 %collective-permute-start.24 = (bf16[832,384]{1,0:T(8,128)(2,1)S(1)}, bf16[832,384]{1,0:T(8,128)(2,1)S(1)}, u32[]{:S(2)}, u32[]{:S(2)}) collective-permute-start(bf16[832,384]{1,0:T(8,128)(2,1)S(1)} %copy-done.8), channel_id=1, source_target_pairs={{0,8},{24,16},{1,9},{25,17},{2,10},{26,18},{3,11},{27,19},{4,12},{... | collective-permute-start | bytes 1916936 | tf_op jit(solution)/shard_map/outer5/ppermute | solution.py:501
  291.5 48.7 %collective-permute-start.26 = (bf16[832,384]{1,0:T(8,128)(2,1)S(1)}, bf16[832,384]{1,0:T(8,128)(2,1)S(1)}, u32[]{:S(2)}, u32[]{:S(2)}) collective-permute-start(bf16[832,384]{1,0:T(8,128)(2,1)S(1)} %copy-done.8), channel_id=1, source_target_pairs={{8,16},{16,8},{9,17},{17,9},{10,18},{18,10},{11,19},{19,11},{12,20... | collective-permute-start | bytes 1916936 | tf_op jit(solution)/shard_map/mate5/ppermute | solution.py:503
  306.4 33.8 %collective-permute-start.23 = (bf16[1280,512]{1,0:T(8,128)(2,1)}, bf16[1280,512]{1,0:T(8,128)(2,1)S(1)}, u32[]{:S(2)}, u32[]{:S(2)}) collective-permute-start(bf16[1280,512]{1,0:T(8,128)(2,1)} %products.12), channel_id=1, source_target_pairs={{8,0},{16,24},{9,1},{17,25},{10,2},{18,26},{11,3},{19,27},{12,4},{... | collective-permute-start | bytes 3932168 | tf_op jit(solution)/shard_map/sums3/ppermute | solution.py:521
  314.5 25.7 %collective-permute-start.27 = (bf16[832,384]{1,0:T(8,128)(2,1)S(1)}, bf16[832,384]{1,0:T(8,128)(2,1)S(1)}, u32[]{:S(2)}, u32[]{:S(2)}) collective-permute-start(bf16[832,384]{1,0:T(8,128)(2,1)S(1)} %collective-permute-done.24.refs_7_), channel_id=1, source_target_pairs={{8,16},{16,8},{9,17},{17,9},{10,18},{18,10},{11,19},{19,11},{12,20... | collective-permute-start | bytes 1916936 | tf_op jit(solution)/shard_map/far5/ppermute | solution.py:508
  317.2 51.1 %collective-permute-start.32 = (bf16[1280,512]{1,0:T(8,128)(2,1)}, bf16[1280,512]{1,0:T(8,128)(2,1)S(1)}, u32[]{:S(2)}, u32[]{:S(2)}) collective-permute-start(bf16[1280,512]{1,0:T(8,128)(2,1)} %products.14), channel_id=1, source_target_pairs={{8,0},{16,24},{9,1},{17,25},{10,2},{18,26},{11,3},{19,27},{12,4},{... | collective-permute-start | bytes 3932168 | tf_op jit(solution)/shard_map/sums4/ppermute | solution.py:521
  342.8 44.3 %collective-permute-start.28 = (bf16[1280,384]{1,0:T(8,128)(2,1)}, bf16[1280,384]{1,0:T(8,128)(2,1)S(1)}, u32[]{:S(2)}, u32[]{:S(2)}) collective-permute-start(bf16[1280,384]{1,0:T(8,128)(2,1)} %products.13), channel_id=1, source_target_pairs={{8,0},{16,24},{9,1},{17,25},{10,2},{18,26},{11,3},{19,27},{12,4},{... | collective-permute-start | bytes 2949128 | tf_op jit(solution)/shard_map/sums5/ppermute | solution.py:521
  (27 other events, 213.0 us)
Sparse Core Ops, SparseCore 0:
  11.5 94.6 all-gather.4
  108.1 85.3 all-gather.6
